TPU v7x, 32 devices: a whole 2x2x4 slice. The times are simulated.
32 devices in a mesh: sec: 4 (over x, core), tile: 8 (over z, y).
Axes of the slice: x: 2, y: 2, z: 4, core: 2. Of those that a mesh axis runs over, the one named last changes fastest.
Arguments:
- ocean_u: float32 [64, 16384], P(None, ('sec', 'tile')), may hold values from -2 to 2
- ocean_b: float32 [64, 16384], P(None, ('sec', 'tile')), may hold values from -4 to 4
- tracers: bfloat16 [17, 64, 12288], P(None, None, ('sec', 'tile')), may hold values from 0.099609375 to 2
- wet_tiles: int32 [96], replicated, may hold values from 0 to 127, as said below
- kinetic_matrix: float32 [17, 17], replicated, may hold values from -0.42 to 1.5
Outputs:
- tracers_out: bfloat16 [17, 64, 12288], P(None, None, ('sec', 'tile'))
- ocean_u_out: float32 [64, 16384], P(None, ('sec', 'tile'))
- ocean_b_out: float32 [64, 16384], P(None, ('sec', 'tile'))
Inputs may be any that keep to these rules, and one draw needn't show every extreme that they name: `wet_tiles`: increasing tile numbers. For every k, of the tiles k * 4 to k * 4 + 3 either 2 or 4 are listed, and for every even k the tiles of k and k + 1 hold 6 listed tiles together.
All inputs are finite; a program needn't handle non-finite values.
Results may differ from a plain program's by a relative error of at most 0.001.
Values sent between devices are 32-bit elements; how exact they have to be, the bound alone decides.
No kernel may reach another device: no remote copies, remote signals or barrier semaphores. Data moves between devices by JAX's collectives and lax.ppermute only.
A program may use at most 64 MiB of HBM per device.

v0:
```python
import jax
import jax.numpy as jnp
from jax import lax
from jax.sharding import PartitionSpec as P

TILE_COLS = 128
STEPS = 2
WET_DEV = 3
OCEAN_DEV = 4


DT_OCEAN = 0.25
PRESSURE = 1.0
HORIZ_VISC = 0.2
VERT_VISC = 0.2
HEATING = 0.2
KAPPA_BASE = 0.05
KAPPA_SPAN = 0.35
DT_TRACER = 0.3
DT_MIX = 1.0
KINETIC_DELTA = 0.5
SURFACE_LIGHT = 10.0
WATER_ATT = 0.04
PIGMENT_ATT = 0.08
GROWTH = 0.05
THERMAL_GAIN = 0.1


def partner(value, axis, stride):
    mask = 2**stride
    pairs = [(source, source ^ mask) for source in range(lax.axis_size(axis))]
    return lax.ppermute(value, axis, pairs)


def with_halo(x, sides, width):
    for axis, dim in sides:
        size, length = (lax.axis_size(axis), x.shape[dim])
        up = [(i, (i + 1) % size) for i in range(size)]
        down = [(j, i) for i, j in up]
        last = lax.slice_in_dim(x, length - width, length, axis=dim)
        leading = lax.slice_in_dim(x, 0, width, axis=dim)
        before = lax.ppermute(last, axis, up)
        after = lax.ppermute(leading, axis, down)
        x = jnp.concatenate([before, x, after], axis=dim)
    return x


def vertical_term(field):
    upper_cells = jnp.concatenate([field[:1], field[:-1]], axis=0)
    lower_cells = jnp.concatenate([field[1:], field[-1:]], axis=0)
    return upper_cells + lower_cells - 2.0 * field


def ocean_core(vel_ext, buoy_ext):
    velocity = vel_ext[:, 1:-1]
    buoyancy = buoy_ext[:, 1:-1]
    horiz_term = vel_ext[:, :-2] + vel_ext[:, 2:] - 2.0 * velocity
    press_term = buoy_ext[:, 2:] - buoyancy
    updated = velocity + DT_OCEAN * (
        HORIZ_VISC * horiz_term + VERT_VISC * vertical_term(velocity) - PRESSURE * press_term
    )
    return (updated, buoyancy)


def diffusivity_of(velocity, buoyancy):
    shear_sq = (velocity[:-1] - velocity[1:]) ** 2
    stratified = buoyancy[:-1] - buoyancy[1:]
    interior = KAPPA_BASE + KAPPA_SPAN * jax.nn.sigmoid(4.0 * (shear_sq - stratified))
    return jnp.concatenate([interior, jnp.zeros_like(interior[:1])], axis=0)


def absorption_of(tracer_state):
    pigment = tracer_state[0]
    attenuation = WATER_ATT + PIGMENT_ATT * pigment * pigment
    optical_depth = jnp.cumsum(attenuation, axis=0)
    return SURFACE_LIGHT * (jnp.exp(attenuation - optical_depth) - jnp.exp(-optical_depth))


def profile_change(
    transported_solutes, turbulent_spreading, seawater_warmth, captured_radiance, kinetic_matrix
):
    lower_cells = jnp.concatenate([transported_solutes[:, 1:], transported_solutes[:, -1:]], axis=1)
    vert_flux = turbulent_spreading[None] * (lower_cells - transported_solutes)
    upper_flux = jnp.concatenate([jnp.zeros_like(vert_flux[:, :1]), vert_flux[:, :-1]], axis=1)
    depth_blended_fields = transported_solutes + DT_MIX * (vert_flux - upper_flux)
    kinetic_drift = jnp.einsum(
        "ij,jlc->ilc", kinetic_matrix, depth_blended_fields, precision=lax.Precision.HIGHEST
    )
    converted_solutes = (
        depth_blended_fields
        + KINETIC_DELTA * jnp.exp(THERMAL_GAIN * seawater_warmth)[None] * kinetic_drift
    )
    return jnp.concatenate(
        [converted_solutes[:1] + GROWTH * captured_radiance[None], converted_solutes[1:]], axis=0
    )


def on_device(ocean_u, ocean_b, tracers, wet_tiles, kinetic_matrix):
    levels = ocean_u.shape[0]
    device_count = lax.axis_size("sec") * lax.axis_size("tile")
    total_tiles = OCEAN_DEV * device_count
    total_wet = WET_DEV * device_count
    device = lax.axis_index("sec") * lax.axis_size("tile") + lax.axis_index("tile")
    slot_ids = device * WET_DEV + jnp.arange(WET_DEV, dtype=jnp.int32)
    slot_tiles = wet_tiles[slot_ids]
    slot_local = slot_tiles // OCEAN_DEV == device
    slot_block = jnp.where(slot_local, slot_tiles % OCEAN_DEV, OCEAN_DEV)
    own_tiles = device * OCEAN_DEV + jnp.arange(OCEAN_DEV, dtype=jnp.int32)
    own_wet = jnp.any(wet_tiles[None, :] == own_tiles[:, None], axis=1)
    own_pos = jnp.sum((wet_tiles[None, :] < own_tiles[:, None]).astype(jnp.int32), axis=1)
    own_extra = jnp.logical_and(own_wet, own_pos // WET_DEV != device)
    own_kept = jnp.logical_and(own_wet, jnp.logical_not(own_extra))
    own_slot = jnp.clip(own_pos - device * WET_DEV, 0, WET_DEV - 1)
    beside_all = jnp.mod(device * WET_DEV - 1 + jnp.arange(WET_DEV + 2, dtype=jnp.int32), total_wet)
    around_tiles = wet_tiles[beside_all]
    adjacent = (jnp.mod(around_tiles[1:] - around_tiles[:-1], total_tiles) == 1).astype(jnp.float32)
    face_open = jnp.ones((WET_DEV + 1, TILE_COLS), jnp.float32).at[:, 0].set(adjacent)
    face_open = face_open.reshape((WET_DEV + 1) * TILE_COLS)[: WET_DEV * TILE_COLS + 1]
    tracer_state = tracers.astype(jnp.float32)
    velocity = ocean_u
    buoyancy = ocean_b
    for step_index in range(STEPS):
        captured_radiance = absorption_of(tracer_state)
        slot_light = captured_radiance.reshape(levels, WET_DEV, TILE_COLS)
        send_back = jnp.sum(
            jnp.where(jnp.logical_not(slot_local)[None, :, None], slot_light, 0.0), axis=1
        )
        returned = partner(send_back, "tile", 0)
        kept_light = jnp.take(slot_light, own_slot, axis=1)
        heating_term = jnp.where(
            own_kept[None, :, None],
            kept_light,
            jnp.where(own_extra[None, :, None], returned[:, None, :], 0.0),
        )
        buoyancy = buoyancy + HEATING * heating_term.reshape(levels, OCEAN_DEV * TILE_COLS)
        ocean_ext = with_halo(jnp.stack([velocity, buoyancy]), ((("sec", "tile"), 2),), 1)
        velocity, buoyancy = ocean_core(ocean_ext[0], ocean_ext[1])
        turbulent_spreading = diffusivity_of(velocity, buoyancy)
        fields = jnp.stack([velocity, turbulent_spreading, buoyancy]).reshape(
            3, levels, OCEAN_DEV, TILE_COLS
        )
        payload = jnp.sum(jnp.where(own_extra[None, None, :, None], fields, 0.0), axis=2)
        arrived = partner(payload, "tile", 0)
        choose = jnp.concatenate([fields, arrived[:, :, None, :]], axis=2)
        coupled = jnp.take(choose, slot_block, axis=2).reshape(3, levels, WET_DEV * TILE_COLS)
        halo_in = jnp.concatenate([tracer_state, coupled[:1]], axis=0)
        extended = with_halo(halo_in, ((("sec", "tile"), 2),), 1)
        ext_state = extended[:-1]
        face_u = extended[-1][:, :-1]
        face_flux = (
            jnp.maximum(face_u, 0.0) * ext_state[:, :, :-1]
            + jnp.minimum(face_u, 0.0) * ext_state[:, :, 1:]
        ) * face_open
        transported_solutes = tracer_state - DT_TRACER * (
            face_flux[:, :, 1:] - face_flux[:, :, :-1]
        )
        tracer_state = profile_change(
            transported_solutes, coupled[1], coupled[2], captured_radiance, kinetic_matrix
        )
    return (tracer_state.astype(jnp.bfloat16), velocity, buoyancy)


def solution(mesh):
    placed = (
        P(None, ("sec", "tile")),
        P(None, ("sec", "tile")),
        P(None, None, ("sec", "tile")),
        P(),
        P(),
    )
    return jax.shard_map(
        on_device,
        mesh=mesh,
        in_specs=placed,
        out_specs=(
            P(None, None, ("sec", "tile")),
            P(None, ("sec", "tile")),
            P(None, ("sec", "tile")),
        ),
        check_vma=False,
    )
```

profile of v0, /device:TPU:0, one launch (start us, length us, event | category | flops | bytes accessed | tf_op | source)
XLA Modules:
  0.0 81.0 jit_solution(11101557906344269349)
XLA Ops:
  0.7 0.8 %slice.341 = f32[1,64,384]{2,1,0:T(8,128)S(1)} slice(bf16[17,64,384]{2,1,0:T(8,128)(2,1)} %param.13), slice={[0:1], [0:64], [0:384]} | slice | bytes 196608 | tf_op jit(solution)/shard_map/slice | solution.py:73
  1.5 1.3 %convert_element_type.10 = f32[17,64,384]{2,1,0:T(8,128)S(1)} convert(bf16[17,64,384]{2,1,0:T(8,128)(2,1)} %param.13) | non-fusion elementwise | flops 417792 | bytes 2506752 | tf_op jit(solution)/shard_map/convert_element_type | solution.py:119
  2.9 0.6 gather_fusion
  3.9 3.0 %collective-permute-start = (f32[64,128]{1,0:T(8,128)S(1)}, f32[64,128]{1,0:T(8,128)S(1)}, u32[]{:S(2)}, u32[]{:S(2)}) collective-permute-start(f32[64,128]{1,0:T(8,128)S(1)} %get-tuple-element.45), channel_id=1, source_target_pairs={{0,1},{1,0},{2,3},{3,2},{4,5},{5,4},{6,7},{7,6},{8,9},{9,8},{10,11... | collective-permute-start | bytes 98312 | tf_op jit(solution)/shard_map/ppermute | solution.py:32
  7.3 0.6 gather_fusion.1
  8.0 0.6 gather_fusion.2
  8.6 0.6 compare_reduce_fusion
  9.4 1.6 %collective-permute-start.1 = (f32[2,64,1]{2,1,0:T(8,128)S(1)}, f32[2,64,1]{2,1,0:T(8,128)S(1)}, u32[]{:S(2)}, u32[]{:S(2)}) collective-permute-start(f32[2,64,1]{2,1,0:T(8,128)S(1)} %get-tuple-element.63), channel_id=1, source_target_pairs={{0,1},{1,2},{2,3},{3,4},{4,5},{5,6},{6,7},{7,8},{8,9},{9,10},{10,1... | collective-permute-start | bytes 1544 | tf_op jit(solution)/shard_map/ppermute | solution.py:42
  11.0 3.7 %collective-permute-start.2 = (f32[2,64,1]{2,1,0:T(8,128)S(1)}, f32[2,64,1]{2,1,0:T(8,128)S(1)}, u32[]{:S(2)}, u32[]{:S(2)}) collective-permute-start(f32[2,64,1]{2,1,0:T(8,128)S(1)} %get-tuple-element.64), channel_id=1, source_target_pairs={{1,0},{2,1},{3,2},{4,3},{5,4},{6,5},{7,6},{8,7},{9,8},{10,9},{11,1... | collective-permute-start | bytes 1544 | tf_op jit(solution)/shard_map/ppermute | solution.py:43
  14.8 0.7 fusion.89
  15.6 1.4 %collective-permute-done.1 = f32[2,64,1]{2,1,0:T(8,128)S(1)} collective-permute-done((f32[2,64,1]{2,1,0:T(8,128)S(1)}, f32[2,64,1]{2,1,0:T(8,128)S(1)}, u32[]{:S(2)}, u32[]{:S(2)}) %collective-permute-start.1) | collective-permute-done | bytes 544 | tf_op jit(solution)/shard_map/ppermute | solution.py:42
  18.4 0.8 collective-permute-start.3
  19.2 3.9 %collective-permute-done.3 = f32[3,64,128]{2,1,0:T(8,128)S(1)} collective-permute-done((f32[3,64,128]{2,1,0:T(8,128)S(1)}, f32[3,64,128]{2,1,0:T(8,128)S(1)}, u32[]{:S(2)}, u32[]{:S(2)}) %collective-permute-start.3) | collective-permute-done | bytes 98336 | tf_op jit(solution)/shard_map/ppermute | solution.py:32
  23.1 0.6 gather_fusion.3
  24.6 5.2 %collective-permute-start.5 = (f32[18,64,1]{1,2,0:T(1,128)S(1)}, f32[18,64,1]{1,2,0:T(1,128)S(1)}, u32[]{:S(2)}, u32[]{:S(2)}) collective-permute-start(f32[18,64,1]{1,2,0:T(1,128)S(1)} %copy.161), channel_id=1, source_target_pairs={{1,0},{2,1},{3,2},{4,3},{5,4},{6,5},{7,6},{8,7},{9,8},{10,9},{11,1... | collective-permute-start | bytes 13832 | tf_op jit(solution)/shard_map/ppermute | solution.py:43
  29.8 0.6 copy.235
  30.6 5.9 %collective-permute-done.4 = f32[18,64,1]{1,2,0:T(1,128)S(1)} collective-permute-done((f32[18,64,1]{1,2,0:T(1,128)S(1)}, f32[18,64,1]{1,2,0:T(1,128)S(1)}, u32[]{:S(2)}, u32[]{:S(2)}) %collective-permute-start.4) | collective-permute-done | bytes 4640 | tf_op jit(solution)/shard_map/ppermute | solution.py:42
  36.4 0.3 copy.162
  36.7 0.3 copy.163
  37.1 0.7 fusion.10
  37.9 0.4 copy-done.5
  38.3 0.5 fusion.15
  39.0 0.3 fusion.16
  39.3 0.5 subtract_add_fusion.1
  39.8 3.1 %fusion.2 = f32[64,384,17]{1,2,0:T(8,128)S(1)} fusion(f32[17,64,384]{2,1,0:T(8,128)S(1)} %subtract_add_fusion.1, f32[17,17]{1,0:T(8,128)S(1)} %copy-done), kind=kOutput, calls=%fused_computation.8 | convolution fusion | flops 85229568 | bytes 3343492 | tf_op jit(solution)/shard_map/ij,jlc->ilc/dot_general | solution.py:86
  42.9 0.4 bitcast_add_fusion.1
  43.3 0.7 fusion.71
  44.0 1.0 %reduce_window_sum.28 = f32[64,384]{1,0:T(8,128)S(1)} reduce-window(f32[64,384]{1,0:T(8,128)} %get-tuple-element.36, f32[]{:T(128)} %constant.150.clone.1), window={size=64x1 pad=63_0x0_0}, to_apply=%region_6.9 | reduce-window | flops 1548288 | bytes 196612 | tf_op jit(solution)/shard_map/jit(cumsum)/reduce_window_sum | solution.py:75
  45.1 0.8 select_reduce_fusion.2
  45.9 0.7 gather_fusion.4
  46.6 3.2 %collective-permute-done.6 = f32[64,128]{1,0:T(8,128)S(1)} collective-permute-done((f32[64,128]{1,0:T(8,128)S(1)}, f32[64,128]{1,0:T(8,128)S(1)}, u32[]{:S(2)}, u32[]{:S(2)}) %collective-permute-start.6) | collective-permute-done | bytes 32800 | tf_op jit(solution)/shard_map/ppermute | solution.py:32
  49.8 1.0 %fusion.18 = f32[1,64,512]{2,1,0:T(8,128)S(1)} fusion(f32[64,514]{1,0:T(8,128)} %copy-done.4, f32[4,64,128]{2,1,0:T(8,128)S(1)} %gather_fusion.4, f32[64,128]{1,0:T(8,128)S(1)} %collective-permute-done.6, pred[4]{0:T(512)(128)(4,1)} %copy-done.16, pred[4]{0:T(512)(128)(4,1)} %copy-done.11, pred[4]{0:T(512)(128)(4,1)} %copy-done.15), kind=kLoop, calls=%fused_computation.70 | loop fusion | flops 163840 | bytes 425996 | tf_op jit(solution)/shard_map/stack | solution.py:136
  50.9 0.9 %pad_maximum_fusion.28 = (f32[2,64,1]{2,1,0:T(8,128)S(1)}, f32[2,64,1]{2,1,0:T(8,128)S(1)}) fusion(f32[1,64,512]{2,1,0:T(8,128)S(1)} %fusion.18, f32[1,64,512]{2,1,0:T(8,128)} %bitcast.145), kind=kLoop, calls=%fused_computation.188 | loop fusion | flops 256 | bytes 263168 | tf_op jit(solution)/shard_map/slice | solution.py:40
  51.8 5.3 %collective-permute-start.8 = (f32[2,64,1]{2,1,0:T(8,128)S(1)}, f32[2,64,1]{2,1,0:T(8,128)S(1)}, u32[]{:S(2)}, u32[]{:S(2)}) collective-permute-start(f32[2,64,1]{2,1,0:T(8,128)S(1)} %get-tuple-element.62), channel_id=1, source_target_pairs={{1,0},{2,1},{3,2},{4,3},{5,4},{6,5},{7,6},{8,7},{9,8},{10,9},{11,1... | collective-permute-start | bytes 1544 | tf_op jit(solution)/shard_map/ppermute | solution.py:43
  57.1 2.0 %collective-permute-done.7 = f32[2,64,1]{2,1,0:T(8,128)S(1)} collective-permute-done((f32[2,64,1]{2,1,0:T(8,128)S(1)}, f32[2,64,1]{2,1,0:T(8,128)S(1)}, u32[]{:S(2)}, u32[]{:S(2)}) %collective-permute-start.7) | collective-permute-done | bytes 544 | tf_op jit(solution)/shard_map/ppermute | solution.py:42
  60.6 4.6 %collective-permute-done.9 = f32[3,64,128]{2,1,0:T(8,128)S(1)} collective-permute-done((f32[3,64,128]{2,1,0:T(8,128)S(1)}, f32[3,64,128]{2,1,0:T(8,128)S(1)}, u32[]{:S(2)}, u32[]{:S(2)}) %collective-permute-start.9) | collective-permute-done | bytes 98336 | tf_op jit(solution)/shard_map/ppermute | solution.py:32
  65.2 0.7 gather_fusion.5
  66.8 5.5 %collective-permute-start.11 = (f32[18,64,1]{1,2,0:T(1,128)S(1)}, f32[18,64,1]{1,2,0:T(1,128)S(1)}, u32[]{:S(2)}, u32[]{:S(2)}) collective-permute-start(f32[18,64,1]{1,2,0:T(1,128)S(1)} %copy.181), channel_id=1, source_target_pairs={{1,0},{2,1},{3,2},{4,3},{5,4},{6,5},{7,6},{8,7},{9,8},{10,9},{11,1... | collective-permute-start | bytes 13832 | tf_op jit(solution)/shard_map/ppermute | solution.py:43
  72.5 0.7 collective-permute-done.10
  73.3 0.3 copy.182
  73.7 0.3 copy.183
  74.1 0.7 fusion.6
  74.9 0.5 fusion.13
  75.6 0.3 fusion.17
  75.9 0.4 subtract_add_fusion
  76.3 3.1 %fusion = f32[64,384,17]{1,2,0:T(8,128)S(1)} fusion(f32[17,64,384]{2,1,0:T(8,128)S(1)} %subtract_add_fusion, f32[17,17]{1,0:T(8,128)S(1)} %copy-done), kind=kOutput, calls=%fused_computation.6 | convolution fusion | flops 85229568 | bytes 3343492 | tf_op jit(solution)/shard_map/ij,jlc->ilc/dot_general | solution.py:86
  79.4 0.4 bitcast_add_fusion
  80.0 1.0 %pad_maximum_fusion.10 = bf16[17,64,384]{2,1,0:T(8,128)(2,1)} fusion(bf16[16,64,384]{2,1,0:T(8,128)(2,1)S(1)} %slice.527, bf16[1,64,384]{2,1,0:T(8,128)(2,1)S(1)} %fusion.78), kind=kLoop, calls=%fused_computation.45 | loop fusion | flops 417792 | bytes 1671168 | tf_op jit(solution)/shard_map/concatenate | solution.py:93
  (129 shorter events, 6.9 us)
Async XLA Ops:
  0.6 39.1 %copy-start = (f32[17,17]{1,0:T(8,128)S(1)}, f32[17,17]{1,0:T(8,128)}, u32[]{:S(2)}) copy-start(f32[17,17]{1,0:T(8,128)} %param.15) | copy-start | bytes 3472
  0.6 2.2 %copy-start.1 = (s32[96]{0:T(128)S(1)}, s32[96]{0:T(128)}, u32[]{:S(2)}) copy-start(s32[96]{0:T(128)} %param.14) | copy-start | bytes 1156
  2.8 6.4 %copy-start.10 = (f32[64,512]{1,0:T(8,128)S(1)}, f32[64,512]{1,0:T(8,128)}, u32[]{:S(2)}) copy-start(f32[64,512]{1,0:T(8,128)} %param.12) | copy-start | bytes 393220
  2.8 6.5 %copy-start.8 = (f32[64,512]{1,0:T(8,128)S(1)}, f32[64,512]{1,0:T(8,128)}, u32[]{:S(2)}) copy-start(f32[64,512]{1,0:T(8,128)} %param.11) | copy-start | bytes 393220
  3.6 20.1 %copy-start.17 = (pred[3]{0:T(512)(128)(4,1)}, pred[3]{0:T(512)(128)(4,1)S(1)}, u32[]{:S(2)}) copy-start(pred[3]{0:T(512)(128)(4,1)S(1)} %get-tuple-element.38) | copy-start | bytes 13
  3.6 3.7 %copy-start.19 = (pred[3]{0:T(512)(128)(4,1)}, pred[3]{0:T(512)(128)(4,1)S(1)}, u32[]{:S(2)}) copy-start(pred[3]{0:T(512)(128)(4,1)S(1)} %compare_not_fusion) | copy-start | bytes 13
  3.9 5.3 %collective-permute-start = (f32[64,128]{1,0:T(8,128)S(1)}, f32[64,128]{1,0:T(8,128)S(1)}, u32[]{:S(2)}, u32[]{:S(2)}) collective-permute-start(f32[64,128]{1,0:T(8,128)S(1)} %get-tuple-element.45), channel_id=1, source_target_pairs={{0,1},{1,0},{2,3},{3,2},{4,5},{5,4},{6,7},{7,6},{8,9},{9,8},{10,11... | collective-permute-start | bytes 98312 | tf_op jit(solution)/shard_map/ppermute | solution.py:32
  7.3 10.1 %copy-start.15 = (pred[4]{0:T(512)(128)(4,1)}, pred[4]{0:T(512)(128)(4,1)S(1)}, u32[]{:S(2)}) copy-start(pred[4]{0:T(512)(128)(4,1)S(1)} %get-tuple-element.41) | copy-start | bytes 16
  7.3 10.1 %copy-start.16 = (pred[4]{0:T(512)(128)(4,1)}, pred[4]{0:T(512)(128)(4,1)S(1)}, u32[]{:S(2)}) copy-start(pred[4]{0:T(512)(128)(4,1)S(1)} %get-tuple-element.79) | copy-start | bytes 16
  7.3 11.0 %copy-start.11 = (pred[4]{0:T(512)(128)(4,1)}, pred[4]{0:T(512)(128)(4,1)S(1)}, u32[]{:S(2)}) copy-start(pred[4]{0:T(512)(128)(4,1)S(1)} %get-tuple-element.42) | copy-start | bytes 16
  7.3 10.1 %copy-start.13 = (s32[1024]{0:T(1024)}, s32[1024]{0:T(1024)S(1)}, u32[]{:S(2)}) copy-start(s32[1024]{0:T(1024)S(1)} %pad_clamp_fusion.2) | copy-start | bytes 12292
  9.4 7.6 %collective-permute-start.1 = (f32[2,64,1]{2,1,0:T(8,128)S(1)}, f32[2,64,1]{2,1,0:T(8,128)S(1)}, u32[]{:S(2)}, u32[]{:S(2)}) collective-permute-start(f32[2,64,1]{2,1,0:T(8,128)S(1)} %get-tuple-element.63), channel_id=1, source_target_pairs={{0,1},{1,2},{2,3},{3,4},{4,5},{5,6},{6,7},{7,8},{8,9},{9,10},{10,1... | collective-permute-start | bytes 1544 | tf_op jit(solution)/shard_map/ppermute | solution.py:42
  11.0 6.0 %collective-permute-start.2 = (f32[2,64,1]{2,1,0:T(8,128)S(1)}, f32[2,64,1]{2,1,0:T(8,128)S(1)}, u32[]{:S(2)}, u32[]{:S(2)}) collective-permute-start(f32[2,64,1]{2,1,0:T(8,128)S(1)} %get-tuple-element.64), channel_id=1, source_target_pairs={{1,0},{2,1},{3,2},{4,3},{5,4},{6,5},{7,6},{8,7},{9,8},{10,9},{11,1... | collective-permute-start | bytes 1544 | tf_op jit(solution)/shard_map/ppermute | solution.py:43
  17.2 0.7 copy-start.4
  17.7 5.4 %copy-start.2 = (f32[64,512]{1,0:T(8,128)}, f32[64,512]{1,0:T(8,128)S(1)}, u32[]{:S(2)}) copy-start(f32[64,512]{1,0:T(8,128)S(1)} %get-tuple-element.70) | copy-start | bytes 393220
  18.4 4.7 %collective-permute-start.3 = (f32[3,64,128]{2,1,0:T(8,128)S(1)}, f32[3,64,128]{2,1,0:T(8,128)S(1)}, u32[]{:S(2)}, u32[]{:S(2)}) collective-permute-start(f32[3,64,128]{2,1,0:T(8,128)S(1)} %select_reduce_fusion.1), channel_id=1, source_target_pairs={{0,1},{1,0},{2,3},{3,2},{4,5},{5,4},{6,7},{7,6},{8,9},{9,8},{10,11... | collective-permute-start | bytes 294920 | tf_op jit(solution)/shard_map/ppermute | solution.py:32
  19.2 4.9 %copy-start.14 = (s32[1024]{0:T(1024)}, s32[1024]{0:T(1024)S(1)}, u32[]{:S(2)}) copy-start(s32[1024]{0:T(1024)S(1)} %pad_clamp_fusion.1) | copy-start | bytes 12292
  24.6 12.1 %collective-permute-start.5 = (f32[18,64,1]{1,2,0:T(1,128)S(1)}, f32[18,64,1]{1,2,0:T(1,128)S(1)}, u32[]{:S(2)}, u32[]{:S(2)}) collective-permute-start(f32[18,64,1]{1,2,0:T(1,128)S(1)} %copy.161), channel_id=1, source_target_pairs={{1,0},{2,1},{3,2},{4,3},{5,4},{6,5},{7,6},{8,7},{9,8},{10,9},{11,1... | collective-permute-start | bytes 13832 | tf_op jit(solution)/shard_map/ppermute | solution.py:43
  29.8 6.7 %collective-permute-start.4 = (f32[18,64,1]{1,2,0:T(1,128)S(1)}, f32[18,64,1]{1,2,0:T(1,128)S(1)}, u32[]{:S(2)}, u32[]{:S(2)}) collective-permute-start(f32[18,64,1]{1,2,0:T(1,128)S(1)} %copy.160), channel_id=1, source_target_pairs={{0,1},{1,2},{2,3},{3,4},{4,5},{5,6},{6,7},{7,8},{8,9},{9,10},{10,1... | collective-permute-start | bytes 13832 | tf_op jit(solution)/shard_map/ppermute | solution.py:42
  37.1 1.2 %copy-start.5 = (bf16[17,64,384]{2,1,0:T(8,128)(2,1)S(1)}, bf16[17,64,384]{2,1,0:T(8,128)(2,1)}, u32[]{:S(2)}) copy-start(bf16[17,64,384]{2,1,0:T(8,128)(2,1)} %param.13) | copy-start | bytes 2506756
  39.7 3.2 %copy-start.9 = (f32[8,8,3,128]{3,1,2,0:T(8,128)S(1)}, f32[8,8,3,128]{3,1,2,0:T(8,128)}, u32[]{:S(2)}) copy-start(f32[8,8,3,128]{3,1,2,0:T(8,128)} %copy.235) | copy-start | bytes 294916
  44.0 15.1 %copy-start.3 = (f32[64,512]{1,0:T(8,128)S(1)}, f32[64,512]{1,0:T(8,128)}, u32[]{:S(2)}) copy-start(f32[64,512]{1,0:T(8,128)} %copy-done.2) | copy-start | bytes 393220
  45.8 4.0 %collective-permute-start.6 = (f32[64,128]{1,0:T(8,128)S(1)}, f32[64,128]{1,0:T(8,128)S(1)}, u32[]{:S(2)}, u32[]{:S(2)}) collective-permute-start(f32[64,128]{1,0:T(8,128)S(1)} %get-tuple-element.34), channel_id=1, source_target_pairs={{0,1},{1,0},{2,3},{3,2},{4,5},{5,4},{6,7},{7,6},{8,9},{9,8},{10,11... | collective-permute-start | bytes 98312 | tf_op jit(solution)/shard_map/ppermute | solution.py:32
  51.7 7.4 %collective-permute-start.7 = (f32[2,64,1]{2,1,0:T(8,128)S(1)}, f32[2,64,1]{2,1,0:T(8,128)S(1)}, u32[]{:S(2)}, u32[]{:S(2)}) collective-permute-start(f32[2,64,1]{2,1,0:T(8,128)S(1)} %get-tuple-element.61), channel_id=1, source_target_pairs={{0,1},{1,2},{2,3},{3,4},{4,5},{5,6},{6,7},{7,8},{8,9},{9,10},{10,1... | collective-permute-start | bytes 1544 | tf_op jit(solution)/shard_map/ppermute | solution.py:42
  51.8 7.3 %collective-permute-start.8 = (f32[2,64,1]{2,1,0:T(8,128)S(1)}, f32[2,64,1]{2,1,0:T(8,128)S(1)}, u32[]{:S(2)}, u32[]{:S(2)}) collective-permute-start(f32[2,64,1]{2,1,0:T(8,128)S(1)} %get-tuple-element.62), channel_id=1, source_target_pairs={{1,0},{2,1},{3,2},{4,3},{5,4},{6,5},{7,6},{8,7},{9,8},{10,9},{11,1... | collective-permute-start | bytes 1544 | tf_op jit(solution)/shard_map/ppermute | solution.py:43
  59.5 0.7 copy-start.12
  59.8 0.7 copy-start.6
  59.8 0.7 copy-start.7
  60.5 4.7 %collective-permute-start.9 = (f32[3,64,128]{2,1,0:T(8,128)S(1)}, f32[3,64,128]{2,1,0:T(8,128)S(1)}, u32[]{:S(2)}, u32[]{:S(2)}) collective-permute-start(f32[3,64,128]{2,1,0:T(8,128)S(1)} %select_reduce_fusion), channel_id=1, source_target_pairs={{0,1},{1,0},{2,3},{3,2},{4,5},{5,4},{6,7},{7,6},{8,9},{9,8},{10,11... | collective-permute-start | bytes 294920 | tf_op jit(solution)/shard_map/ppermute | solution.py:32
  60.6 5.3 %copy-start.18 = (pred[3]{0:T(512)(128)(4,1)S(1)}, pred[3]{0:T(512)(128)(4,1)}, u32[]{:S(2)}) copy-start(pred[3]{0:T(512)(128)(4,1)} %copy-done.17) | copy-start | bytes 13
  66.5 6.7 %collective-permute-start.10 = (f32[18,64,1]{1,2,0:T(1,128)S(1)}, f32[18,64,1]{1,2,0:T(1,128)S(1)}, u32[]{:S(2)}, u32[]{:S(2)}) collective-permute-start(f32[18,64,1]{1,2,0:T(1,128)S(1)} %copy.180), channel_id=1, source_target_pairs={{0,1},{1,2},{2,3},{3,4},{4,5},{5,6},{6,7},{7,8},{8,9},{9,10},{10,1... | collective-permute-start | bytes 13832 | tf_op jit(solution)/shard_map/ppermute | solution.py:42
  66.8 6.9 %collective-permute-start.11 = (f32[18,64,1]{1,2,0:T(1,128)S(1)}, f32[18,64,1]{1,2,0:T(1,128)S(1)}, u32[]{:S(2)}, u32[]{:S(2)}) collective-permute-start(f32[18,64,1]{1,2,0:T(1,128)S(1)} %copy.181), channel_id=1, source_target_pairs={{1,0},{2,1},{3,2},{4,3},{5,4},{6,5},{7,6},{8,7},{9,8},{10,9},{11,1... | collective-permute-start | bytes 13832 | tf_op jit(solution)/shard_map/ppermute | solution.py:43
where the time goes:
time: 81.4 us; the launch traced here: 81 us
  starting transfers between devices  25.4 us (31%)
  waiting for transfers between devices  21.9 us (27%)
  other arithmetic  16 us (20%)
  local copies, waits for them, and re-layouts  9.98 us (12%)
  matrix products  6.26 us (8%)
  between operations  1.51 us (2%)
    ppermute x4, starting transfers between devices, with_halo(): after = lax.ppermute(leading, axis, down)  19.8 us
    ppermute x4, waiting for transfers between devices, partner(): return lax.ppermute(value, axis, pairs)  11.7 us
    ppermute x4, waiting for transfers between devices, with_halo(): before = lax.ppermute(last, axis, up)  9.99 us
    dot_general x2, matrix products, profile_change(): jnp.einsum('ij,jlc->ilc', kinetic_matrix, depth_blended_fields, precision...  6.26 us
    ppermute x4, starting transfers between devices, partner(): return lax.ppermute(value, axis, pairs)  3.86 us
    ppermute x4, starting transfers between devices, with_halo(): before = lax.ppermute(last, axis, up)  1.73 us
    unnamed x49, local copies, waits for them, and re-layouts  1.69 us
  transfers between devices with their start and end apart: 12, of which 8 were waited for; matrix products, arithmetic and copies ran while one was open for 7% of the time, Pallas kernels for 0%

commit v1 on v0

v1 whole, which is shorter than its diff:
```python
import functools

import jax
import jax.numpy as jnp
from jax import lax
from jax.experimental import pallas as pl
from jax.experimental.pallas import tpu as pltpu
from jax.sharding import PartitionSpec as P

LANES = 128
STEPS = 2
WET_DEV = 3
OCEAN_DEV = 4

DT_OCEAN = 0.25
PRESSURE = 1.0
HORIZ_VISC = 0.2
VERT_VISC = 0.2
HEATING = 0.2
KAPPA_BASE = 0.05
KAPPA_SPAN = 0.35
DT_TRACER = 0.3
DT_MIX = 1.0
KINETIC_DELTA = 0.5
SURFACE_LIGHT = 10.0
WATER_ATT = 0.04
PIGMENT_ATT = 0.08
GROWTH = 0.05
THERMAL_GAIN = 0.1

SEG = 40
HALF = SEG // 2
FIX = 8
PAD = 8
F32, BF16 = jnp.float32, jnp.bfloat16


def facts(dev_ref, wet_ref):
    f = {}
    k = dev_ref[0]
    odd = lax.rem(k, 2)
    first, base = WET_DEV * k, OCEAN_DEV * k
    listed = wet_ref.shape[0]
    tiles = listed // WET_DEV * OCEAN_DEV
    is_odd = odd == 1
    w = [wet_ref[first + s] for s in range(WET_DEV)]
    probe = wet_ref[first + jnp.where(is_odd, -1, 3)]
    gives = jnp.logical_and(probe >= base, probe < base + OCEAN_DEV)
    before = jnp.where(k == 0, listed - 1, first - 1)
    after = jnp.where(first + WET_DEV == listed, 0, first + WET_DEV)
    outer_tile = jnp.where(
        is_odd,
        jnp.where(base + OCEAN_DEV == tiles, 0, base + OCEAN_DEV),
        jnp.where(k == 0, tiles - 1, base - 1),
    )
    f["odd"], f["is_odd"], f["gives"], f["w"], f["base"] = odd, is_odd, gives, w, base
    f["outer_far_wet"] = wet_ref[jnp.where(is_odd, after, before)] == outer_tile
    f["outer_own_wet"] = jnp.where(is_odd, w[2] == base + 3, w[0] == base)
    f["x_slot"] = 2 - 2 * odd
    f["x_tile"] = 3 - 3 * odd
    f["outer_slot"] = 2 * odd
    f["outer_tile"] = 3 * odd
    f["beside_tile"] = jnp.where(gives, 2 - odd, 3 - 3 * odd)
    f["beside_slot"] = jnp.where(gives, 2 - 2 * odd, 1)
    f["beside_wet"] = jnp.logical_or(gives, w[1] == base + 3 - 3 * odd)
    far_listed = wet_ref[first + jnp.where(is_odd, -2, 4)] == base + jnp.where(is_odd, -1, 4)
    f["beyond_wet"] = jnp.logical_or(jnp.logical_not(gives), far_listed)
    return f


def lane_of(rows):
    return lax.broadcasted_iota(jnp.int32, (rows, LANES), 1)


def lane_roll(x, shift):
    return pltpu.roll(x, shift, x.ndim - 1)


def upper(x):
    row = lax.broadcasted_iota(jnp.int32, x.shape, 0)
    return jnp.where(row == 0, x, pltpu.roll(x, 1, 0))


def lower(x):
    n = x.shape[0]
    row = lax.broadcasted_iota(jnp.int32, x.shape, 0)
    return jnp.where(row == n - 1, x, pltpu.roll(x, n - 1, 0))


def absorbed_light(pigment):
    att = WATER_ATT + PIGMENT_ATT * pigment * pigment
    depth = att
    rows = att.shape[0]
    row = lax.broadcasted_iota(jnp.int32, att.shape, 0)
    step = 1
    while step < rows:
        depth = depth + jnp.where(row >= step, pltpu.roll(depth, step, 0), 0.0)
        step *= 2
    return SURFACE_LIGHT * (jnp.exp(att - depth) - jnp.exp(-depth))


def new_velocity(u, u_left, u_right, b, b_right):
    horiz = u_left + u_right - 2.0 * u
    vert = upper(u) + lower(u) - 2.0 * u
    return u + DT_OCEAN * (HORIZ_VISC * horiz + VERT_VISC * vert - PRESSURE * (b_right - b))


def diffusivity(u, b):
    rows = u.shape[0]
    row = lax.broadcasted_iota(jnp.int32, u.shape, 0)
    shear = u - lower(u)
    strat = b - lower(b)
    kappa = KAPPA_BASE + KAPPA_SPAN * (1.0 / (1.0 + jnp.exp(-4.0 * (shear * shear - strat))))
    return jnp.where(row == rows - 1, 0.0, kappa)


def face_parts(u, face_open):
    w = DT_TRACER * u * face_open
    return jnp.maximum(w, 0.0), jnp.minimum(w, 0.0)


def advect(state, adv, t, left, right, coeffs, fields, levels):
    centre, from_left, from_right = coeffs
    chunk = 16
    lane = lane_of(chunk)
    for r in range(0, levels, chunk):
        here = state[:fields, t, r : r + chunk, :]
        to_left, to_right = here, here
        if right != t:
            to_left = jnp.where(lane == 0, state[:fields, right, r : r + chunk, :], here)
        if left != t:
            to_right = jnp.where(lane == LANES - 1, state[:fields, left, r : r + chunk, :], here)
        s = slice(r, r + chunk)
        adv[:fields, t, PAD + r : PAD + r + chunk, :] = (
            here * centre[s] + lane_roll(to_left, LANES - 1) * from_right[s] + lane_roll(to_right, 1) * from_left[s]
        )


def mix_and_react(adv, t, kappa, warmth, light, kron, fields, levels, emit):
    chunk = 16
    above = jnp.where(lax.broadcasted_iota(jnp.int32, kappa.shape, 0) == 0, 0.0, pltpu.roll(kappa, 1, 0))
    stay = 1.0 - DT_MIX * (kappa + above)
    rows = (fields + (18 - fields)) * 8
    k_hi = kron[:rows, :]
    k_both = kron[...]
    for r in range(0, levels, chunk):
        s = slice(r, r + chunk)
        at = PAD + r
        here = adv[:fields, t, at : at + chunk, :]
        up = adv[:fields, t, at - 1 : at - 1 + chunk, :]
        down = adv[:fields, t, at + 1 : at + 1 + chunk, :]
        mixed = here * stay[s] + (DT_MIX * kappa[s]) * down + (DT_MIX * above[s]) * up
        halves = []
        for h in range(2):
            part = mixed[:, 8 * h : 8 * h + 8, :].reshape(fields * 8, LANES)
            if fields < 18:
                part = jnp.concatenate([part, jnp.zeros(((18 - fields) * 8, LANES), F32)], axis=0)
            halves.append(part)
        wide = jnp.concatenate(halves, axis=1)
        hi = wide.astype(BF16)
        lo = (wide - hi.astype(F32)).astype(BF16)
        by_hi = jnp.dot(k_both, hi, preferred_element_type=F32)
        by_lo = jnp.dot(k_hi, lo, preferred_element_type=F32)
        drift = by_hi[:rows] + (by_hi[rows:] + by_lo)
        out = []
        for h in range(2):
            d = drift[:, LANES * h : LANES * h + LANES].reshape(18, 8, LANES)[:fields]
            sh = slice(r + 8 * h, r + 8 * h + 8)
            new = mixed[:, 8 * h : 8 * h + 8, :] + warmth[sh] * d
            first = new[:1] + GROWTH * light[sh][None]
            out.append(jnp.concatenate([first, new[1:]], axis=0))
        emit(r, jnp.concatenate(out, axis=1))


def pack_kernel(dev, wet, kin, u, b, tracers, inner, outer):
    f = facts(dev, wet)
    levels = u.shape[0]
    half = levels // 2
    n = tracers.shape[0]
    lane = lane_of(half)
    combos = []
    for s in range(WET_DEV):
        total = None
        for j in range(n):
            term = kin[0, j] * tracers[j, :, LANES * s : LANES * (s + 1)].astype(F32)
            total = term if total is None else total + term
        combos.append(total)

    def tile_of(ref, index):
        return ref[:, pl.ds(pl.multiple_of(index * LANES, LANES), LANES)]

    def strip(slot, tile, right):
        acc = jnp.zeros((half, LANES), F32)

        def put(acc, value, at, width):
            shift = at + (width if right else 0)
            for h in range(2):
                part = value[half * h : half * (h + 1)]
                to = at + 64 * h
                here = jnp.logical_and(lane >= to, lane < to + width)
                acc = jnp.where(here, lane_roll(part, (shift + 64 * h) % LANES), acc)
            return acc

        for j in range(n):
            acc = put(acc, tracers[j, :, LANES * slot : LANES * (slot + 1)].astype(F32), 2 * j, 2)
        acc = put(acc, combos[slot], 2 * n, 2)
        at = 2 * (n + 1)
        acc = put(acc, tile_of(u, tile), at, 3)
        acc = put(acc, tile_of(b, tile), at + 3, 3)
        acc = put(acc, tracers[0, :, LANES : 2 * LANES].astype(F32), at + 6, 2)
        acc = put(acc, combos[1], at + 8, 2)
        return acc

    odd_gives = jnp.logical_and(f["is_odd"], f["gives"])
    even_gives = jnp.logical_and(jnp.logical_not(f["is_odd"]), f["gives"])
    facing_left = strip(0, jnp.where(odd_gives, 1, 0), False)
    facing_right = strip(2, jnp.where(even_gives, 2, 3), True)
    outer[...] = jnp.where(f["is_odd"], facing_right, facing_left)
    inner[:half] = jnp.where(f["is_odd"], facing_left, facing_right)
    t0 = jnp.where(f["is_odd"], tracers[0, :, :LANES].astype(F32), tracers[0, :, 2 * LANES :].astype(F32))
    tk = jnp.where(f["is_odd"], combos[0], combos[2])
    inner[half : half + levels] = jnp.where(f["gives"], tile_of(u, f["x_tile"]), t0)
    inner[half + levels :] = jnp.where(f["gives"], tile_of(b, f["x_tile"]), tk)


def expand_kinetics(kin, kron):
    n = kin.shape[0]
    rows = (n + 1) * 8
    to_rows = lax.broadcasted_iota(jnp.int32, (rows, n), 0) // 8 == lax.broadcasted_iota(jnp.int32, (rows, n), 1)
    to_cols = lax.broadcasted_iota(jnp.int32, (n, rows), 1) // 8 == lax.broadcasted_iota(jnp.int32, (n, rows), 0)
    tall = jnp.dot(to_rows.astype(F32), kin[...], precision=lax.Precision.HIGHEST, preferred_element_type=F32)
    full = jnp.dot(tall, to_cols.astype(F32), precision=lax.Precision.HIGHEST, preferred_element_type=F32)
    row = lax.broadcasted_iota(jnp.int32, (rows, rows), 0)
    col = lax.broadcasted_iota(jnp.int32, (rows, rows), 1)
    full = jnp.where(lax.rem(row, 8) == lax.rem(col, 8), full, 0.0)
    with_combo = jnp.where(row < 8, jnp.where(col - 8 * n == row, 1.0, 0.0), full)
    for i, m in enumerate((with_combo, full)):
        hi = m.astype(BF16)
        kron[i, :rows, :] = hi
        kron[i, rows:, :] = (m - hi.astype(F32)).astype(BF16)


def own_kernel(dev, wet, kin, u0, b0, tracers, u_out, b_out, t_out, kron, u, b, state, adv):
    f = facts(dev, wet)
    levels = u0.shape[0]
    n = tracers.shape[0]
    lane = lane_of(levels)
    expand_kinetics(kin, kron)
    takes = jnp.logical_not(f["gives"])
    is_x = [jnp.logical_and(takes, f["x_slot"] == s) for s in range(WET_DEV)]
    tile = [jnp.clip(f["w"][s] - f["base"], 0, OCEAN_DEV - 1) for s in range(WET_DEV)]
    joined = []
    for s in range(WET_DEV - 1):
        apart = jnp.logical_or(is_x[s], is_x[s + 1])
        joined.append(jnp.logical_and(f["w"][s + 1] - f["w"][s] == 1, jnp.logical_not(apart)))
    joined.append(jnp.zeros((), jnp.bool_))
    for t in range(OCEAN_DEV):
        u[t] = u0[:, LANES * t : LANES * (t + 1)]
        b[t] = b0[:, LANES * t : LANES * (t + 1)]
    for s in range(WET_DEV):
        state[:, s] = tracers[:, :, LANES * s : LANES * (s + 1)].astype(F32)
        for row in (0, PAD + levels):
            adv[:, s, row : row + 8, :] = jnp.zeros((n, 8, LANES), F32)
    for step in range(STEPS):
        last = step == STEPS - 1
        light = []
        for s in range(WET_DEV):
            light.append(absorbed_light(state[0, s]))
            b[tile[s]] = b[tile[s]] + jnp.where(is_x[s], 0.0, HEATING) * light[s]
        us = [u[t] for t in range(OCEAN_DEV)]
        bs = [b[t] for t in range(OCEAN_DEV)]
        for t in range(OCEAN_DEV):
            nxt, prv = (t + 1) % OCEAN_DEV, (t - 1) % OCEAN_DEV
            u_right = lane_roll(jnp.where(lane == 0, us[nxt], us[t]), LANES - 1)
            u_left = lane_roll(jnp.where(lane == LANES - 1, us[prv], us[t]), 1)
            b_right = lane_roll(jnp.where(lane == 0, bs[nxt], bs[t]), LANES - 1)
            u[t] = new_velocity(us[t], u_left, u_right, bs[t], b_right)
            if last:
                u_out[:, LANES * t : LANES * (t + 1)] = u[t]
                b_out[:, LANES * t : LANES * (t + 1)] = bs[t]
        parts = []
        for s in range(WET_DEV):
            shut = jnp.logical_and(lane == LANES - 1, jnp.logical_not(joined[s]))
            parts.append(face_parts(u[tile[s]], jnp.where(shut, 0.0, 1.0)))
        for s in range(WET_DEV):
            pos, neg = parts[s]
            before = parts[s - 1] if s else (jnp.zeros_like(pos), jnp.zeros_like(neg))
            pos_left = lane_roll(jnp.where(lane == LANES - 1, before[0], pos), 1)
            neg_left = lane_roll(jnp.where(lane == LANES - 1, before[1], neg), 1)
            coeffs = (1.0 - pos + neg_left, pos_left, -neg)
            advect(state, adv, s, max(s - 1, 0), min(s + 1, WET_DEV - 1), coeffs, n, levels)
        for s in range(WET_DEV):
            ub, bb = u[tile[s]], b[tile[s]]
            kappa = diffusivity(ub, bb)
            warmth = KINETIC_DELTA * jnp.exp(THERMAL_GAIN * bb)

            def emit(r, values, s=s):
                if last:
                    t_out[:, r : r + 16, LANES * s : LANES * (s + 1)] = values.astype(BF16)
                else:
                    state[:, s, r : r + 16, :] = values

            mix_and_react(adv, s, kappa, warmth, light[s], kron.at[1], n, levels, emit)


def edge_kernel(
    dev, wet, kin, kron, u0, b0, tracers, inner, outer, u_in, b_in, t_in, u_out, b_out, t_out, u, b, state, adv
):
    f = facts(dev, wet)
    levels = u0.shape[0]
    half = levels // 2
    n = tracers.shape[0]
    fields = n + 1
    lane = lane_of(levels)
    gives, is_odd = f["gives"], f["is_odd"]
    X, PATCH = 0, 1

    def tile_of(ref, index):
        return ref[:, pl.ds(pl.multiple_of(index * LANES, LANES), LANES)]

    def slot_of(j, index):
        return tracers[j, :, pl.ds(pl.multiple_of(index * LANES, LANES), LANES)].astype(F32)

    def combo_of(index):
        total = None
        for j in range(n):
            term = kin[0, j] * slot_of(j, index)
            total = term if total is None else total + term
        return total

    def from_strip(ref, at, width, to_right_half):
        shift = jnp.where(to_right_half, 0, width)
        parts = []
        for h in range(2):
            amount = lax.rem(2 * LANES - at - 64 * h - shift, LANES)
            parts.append(lane_roll(ref[:half], amount))
        return jnp.concatenate(parts, axis=0)

    from_outer = functools.partial(from_strip, outer, to_right_half=is_odd)
    from_inner = functools.partial(from_strip, inner, to_right_half=jnp.logical_not(is_odd))
    in_right = jnp.where(is_odd, LANES - 1 - lane, lane) < LANES // 2
    in_1 = jnp.logical_and(lane >= HALF, lane < HALF + SEG)
    in_2 = jnp.logical_and(lane >= HALF + SEG, lane < HALF + 2 * SEG)

    def patch_of(own, far, beside, x_side, x, beyond):
        seg0 = jnp.where(in_right, own, far)
        seg1 = jnp.where(in_right, x_side, beside)
        seg2 = jnp.where(in_right, beyond, x)
        return jnp.where(in_1, lane_roll(seg1, SEG), jnp.where(in_2, lane_roll(seg2, 2 * SEG), seg0))

    tile1 = inner[half : half + levels]
    tile2 = inner[half + levels :]
    at = 2 * fields
    x_u = jnp.where(gives, tile_of(u0, f["x_tile"]), tile1)
    x_b = jnp.where(gives, tile_of(b0, f["x_tile"]), tile2)
    u[X] = x_u
    b[X] = x_b
    u[PATCH] = patch_of(
        tile_of(u0, f["outer_tile"]),
        from_outer(at, 3),
        tile_of(u0, f["beside_tile"]),
        x_u,
        x_u,
        from_inner(at, 3),
    )
    b[PATCH] = patch_of(
        tile_of(b0, f["outer_tile"]),
        from_outer(at + 3, 3),
        tile_of(b0, f["beside_tile"]),
        x_b,
        x_b,
        from_inner(at + 3, 3),
    )
    for j in range(fields):
        load = (lambda index, j=j: slot_of(j, index)) if j < n else combo_of
        x = load(f["x_slot"])
        own = load(f["outer_slot"])
        beside = load(f["beside_slot"])
        strip = from_inner(2 * j, 2)
        x_side = jnp.where(gives, strip, x)
        beyond = strip
        if j in (0, n):
            x = x_side = jnp.where(gives, tile1 if j == 0 else tile2, x)
            beyond = jnp.where(gives, from_inner(at + (6 if j == 0 else 8), 2), strip)
        state[j, X] = x
        state[j, PATCH] = patch_of(own, from_outer(2 * j, 2), beside, x_side, x, beyond)
    for t in range(2):
        for row in (0, PAD + levels):
            adv[:, t, row : row + 8, :] = jnp.zeros((fields, 8, LANES), F32)

    def flag(x):
        return jnp.where(x, 1.0, 0.0) * jnp.ones((levels, LANES), F32)

    one = jnp.ones((levels, LANES), F32)
    wet_here = patch_of(
        flag(f["outer_own_wet"]), flag(f["outer_far_wet"]), flag(f["beside_wet"]), one, one, flag(f["beyond_wet"])
    )
    open_0 = jnp.logical_and(f["outer_own_wet"], f["outer_far_wet"])
    patch_open = jnp.where(
        lane == LANES - 1,
        flag(open_0),
        jnp.where(
            lane == SEG - 1,
            flag(f["beside_wet"]),
            jnp.where(lane == 2 * SEG - 1, flag(f["beyond_wet"]), 1.0),
        ),
    )
    x_open = jnp.where(lane == LANES - 1, 0.0, 1.0)
    heat = (one, wet_here)
    opens = (x_open, patch_open)
    results = [[None] * 2, [None] * 2]
    for step in range(STEPS):
        last = step == STEPS - 1
        light = []
        for t in range(2):
            light.append(absorbed_light(state[0, t]))
            bb = b[t] + HEATING * heat[t] * light[t]
            b[t] = bb
            uu = u[t]
            uu = new_velocity(uu, lane_roll(uu, 1), lane_roll(uu, LANES - 1), bb, lane_roll(bb, LANES - 1))
            u[t] = uu
        count = n if last else fields
        for t in range(2):
            pos, neg = face_parts(u[t], opens[t])
            pos_left, neg_left = lane_roll(pos, 1), lane_roll(neg, 1)
            advect(state, adv, t, t, t, (1.0 - pos + neg_left, pos_left, -neg), count, levels)
        for t in range(2):
            kappa = diffusivity(u[t], b[t])
            warmth = KINETIC_DELTA * jnp.exp(THERMAL_GAIN * b[t])

            def emit(r, values, t=t):
                state[:n, t, r : r + 16, :] = values[:n]

            mix_and_react(adv, t, kappa, warmth, light[t], kron.at[step], count, levels, emit)

    def fix_mask(rows, at_left):
        here = lane_of(rows)
        return jnp.where(at_left, here, LANES - 1 - here) < FIX

    not_odd = jnp.logical_not(is_odd)

    def ocean_fix(final, incoming, out, scratch):
        out[...] = incoming[...]
        patch = scratch[PATCH]
        seg1 = lane_roll(patch, LANES - SEG)
        seg2 = lane_roll(patch, LANES - 2 * SEG)

        def put(index, value):
            out[:, pl.ds(pl.multiple_of(index * LANES, LANES), LANES)] = value

        put(f["outer_tile"], jnp.where(fix_mask(levels, not_odd), patch, tile_of(incoming, f["outer_tile"])))
        put(f["beside_tile"], jnp.where(fix_mask(levels, is_odd), seg1, tile_of(incoming, f["beside_tile"])))
        x = jnp.where(fix_mask(levels, not_odd), seg1, jnp.where(fix_mask(levels, is_odd), seg2, scratch[X]))

        @pl.when(gives)
        def _():
            put(f["x_tile"], x)

    ocean_fix(None, u_in, u_out, u)
    ocean_fix(None, b_in, b_out, b)

    rows = 16
    t_out[...] = t_in[...]
    takes = jnp.logical_not(gives)
    outer_fix = jnp.logical_and(fix_mask(rows, not_odd), f["outer_own_wet"])
    beside_fix = jnp.logical_and(fix_mask(rows, is_odd), f["beside_wet"])
    near_fix, far_fix = fix_mask(rows, not_odd), fix_mask(rows, is_odd)

    def slot_at(index):
        return pl.ds(pl.multiple_of(index * LANES, LANES), LANES)

    for r in range(0, levels, rows):
        s = slice(r, r + rows)
        patch = state[:n, PATCH, s, :]
        seg1 = lane_roll(patch, LANES - SEG)
        where = slot_at(f["outer_slot"])
        t_out[:, s, where] = jnp.where(outer_fix, patch, t_in[:, s, where].astype(F32)).astype(BF16)
        where = slot_at(f["beside_slot"])
        t_out[:, s, where] = jnp.where(beside_fix, seg1, t_in[:, s, where].astype(F32)).astype(BF16)

    @pl.when(takes)
    def _():
        for r in range(0, levels, rows):
            s = slice(r, r + rows)
            patch = state[:n, PATCH, s, :]
            seg1 = lane_roll(patch, LANES - SEG)
            seg2 = lane_roll(patch, LANES - 2 * SEG)
            x = jnp.where(near_fix, seg1, jnp.where(far_fix, seg2, state[:n, X, s, :]))
            t_out[:, s, slot_at(f["x_slot"])] = x.astype(BF16)


def call(kernel, outs, scratch, args, spaces, aliases=None, flops=0, name=None):
    where = {"s": pltpu.SMEM, "v": pltpu.VMEM}
    return pl.pallas_call(
        kernel,
        out_shape=tuple(jax.ShapeDtypeStruct(s, d) for s, d in outs),
        in_specs=[pl.BlockSpec(memory_space=where[c]) for c in spaces],
        out_specs=tuple(pl.BlockSpec(memory_space=pltpu.VMEM) for _ in outs),
        scratch_shapes=[pltpu.VMEM(s, F32) for s in scratch],
        input_output_aliases=aliases or {},
        compiler_params=pltpu.CompilerParams(vmem_limit_bytes=48 * 2**20),
        cost_estimate=pl.CostEstimate(flops=flops, bytes_accessed=4_000_000, transcendentals=0),
        name=name,
    )(*args)


def on_device(ocean_u, ocean_b, tracers, wet_tiles, kinetic):
    axes = ("sec", "tile")
    devices = lax.axis_size("sec") * lax.axis_size("tile")
    levels, n = ocean_u.shape[0], tracers.shape[0]
    dev = (lax.axis_index("sec") * lax.axis_size("tile") + lax.axis_index("tile")).astype(jnp.int32).reshape(1)
    strip = levels // 2
    inner, outer = call(
        pack_kernel,
        [((strip + 2 * levels, LANES), F32), ((strip, LANES), F32)],
        [],
        (dev, wet_tiles, kinetic, ocean_u, ocean_b, tracers),
        "sssvvv",
        flops=10_000_000,
        name="pack",
    )
    in_pairs = [(i, i ^ 1) for i in range(devices)]
    across = [(i, (i + 1) % devices if i % 2 else (i - 1) % devices) for i in range(devices)]
    inner = lax.ppermute(inner, axes, in_pairs)
    outer = lax.ppermute(outer, axes, across)
    fields = n + 1
    u, b, t, kron = call(
        own_kernel,
        [
            (ocean_u.shape, F32),
            (ocean_b.shape, F32),
            (tracers.shape, BF16),
            ((2, 2 * fields * 8, fields * 8), BF16),
        ],
        [
            (OCEAN_DEV, levels, LANES),
            (OCEAN_DEV, levels, LANES),
            (n, WET_DEV, levels, LANES),
            (n, WET_DEV, levels + 2 * PAD, LANES),
        ],
        (dev, wet_tiles, kinetic, ocean_u, ocean_b, tracers),
        "ssvvvv",
        flops=2_000_000_000,
        name="own_tiles",
    )
    return tuple(
        call(
            edge_kernel,
            [(ocean_u.shape, F32), (ocean_b.shape, F32), (tracers.shape, BF16)],
            [
                (2, levels, LANES),
                (2, levels, LANES),
                (fields, 2, levels, LANES),
                (fields, 2, levels + 2 * PAD, LANES),
            ],
            (dev, wet_tiles, kinetic, kron, ocean_u, ocean_b, tracers, inner, outer, u, b, t),
            "sss" + "v" * 9,
            flops=1_000_000_000,
            name="edges",
        )
    )


def solution(mesh):
    spread = P(None, ("sec", "tile"))
    tracer_spread = P(None, None, ("sec", "tile"))

    def program(ocean_u, ocean_b, tracers, wet_tiles, kinetic_matrix):
        u, b, t = jax.shard_map(
            on_device,
            mesh=mesh,
            in_specs=(spread, spread, tracer_spread, P(), P()),
            out_specs=(spread, spread, tracer_spread),
            check_vma=False,
        )(ocean_u, ocean_b, tracers, wet_tiles, kinetic_matrix)
        return t, u, b

    return program
```

time: 81.4 us -> 23.1 us (0.28)
  waiting for transfers between devices: 21.9 us -> 0.01 us
  starting transfers between devices: 25.4 us -> 6.44 us
  other arithmetic: 16 us -> 0 us
  Pallas kernels: 0 us -> 12 us
  local copies, waits for them, and re-layouts: 9.98 us -> 3.65 us
  matrix products: 6.26 us -> 0 us
  between operations: 1.51 us -> 0.69 us
    ppermute x12 -> x2, waiting for transfers between devices: 21.9 us -> 0.01 us  [the longest x1 0.01 us: on_device(): outer = lax.ppermute(outer, axes, across)]
    ppermute x12 -> x2, starting transfers between devices: 25.4 us -> 6.44 us  [the longest x1 6.44 us: on_device(): outer = lax.ppermute(outer, axes, across)]
    pallas_call x0 -> x3, Pallas kernels: none -> 12 us  [call(): pl.pallas_call(kernel, out_shape=tuple((jax.ShapeDtypeStruct(s, d) for s,...]
    dot_general x2 -> x0, matrix products: 6.26 us -> none  [profile_change(): jnp.einsum('ij,jlc->ilc', kinetic_matrix, depth_blended_fields, precision...]
    gather x6 -> x0, local copies, waits for them, and re-layouts: 3.78 us -> none  [the longest x2 1.25 us: on_device(): jnp.take(choose, slot_block, axis=2).reshape(3, levels, WET_DEV * TILE_COLS)]
    another operation x7 -> x0, other arithmetic: 3.71 us -> none
    slice x19 -> x0, local copies, waits for them, and re-layouts: 2.88 us -> none  [the longest x1 0.81 us: absorption_of(): pigment = tracer_state[0]]
    add x10 -> x0, other arithmetic: 2.86 us -> none  [the longest x2 0.84 us: profile_change(): transported_solutes + DT_MIX * (vert_flux - upper_flux)]
  transfers between devices with their start and end apart: 12 -> 2, of which waited for: 8 -> 0; matrix products, arithmetic and copies ran while one was open for 7% -> 0% of each run, Pallas kernels for 0% -> 20%
where the time goes in v1:
time: 23.1 us; the launch traced here: 22.8 us
  Pallas kernels  12 us (52%)
  starting transfers between devices  6.44 us (28%)
  local copies, waits for them, and re-layouts  3.65 us (16%)
  between operations  0.69 us (3%)
    pallas_call x3, Pallas kernels, call(): pl.pallas_call(kernel, out_shape=tuple((jax.ShapeDtypeStruct(s, d) for s,...  12 us
    ppermute x1, starting transfers between devices, on_device(): outer = lax.ppermute(outer, axes, across)  6.44 us
    unnamed x10, local copies, waits for them, and re-layouts  3.65 us
  transfers between devices with their start and end apart: 2, of which 0 were waited for; matrix products, arithmetic and copies ran while one was open for 0% of the time, Pallas kernels for 20%

profile of v1, /device:TPU:0, one launch (start us, length us, event | category | flops | bytes accessed | tf_op | source)
XLA Modules:
  0.0 22.8 jit_solution(17417682884867629557)
XLA Ops:
  0.6 0.0 copy-start.3
  0.6 0.0 copy-start.4
  0.7 0.7 %copy-done.3 = f32[17,17]{1,0:T(8,128)S(1)} copy-done((f32[17,17]{1,0:T(8,128)S(1)}, f32[17,17]{1,0:T(8,128)}, u32[]{:S(2)}) %copy-start.3) | copy-done | bytes 1180
  1.3 0.0 copy-done.4
  1.3 0.0 copy-start
  1.3 1.1 %copy-done = bf16[17,64,384]{2,1,0:T(8,128)(2,1)S(1)} copy-done((bf16[17,64,384]{2,1,0:T(8,128)(2,1)S(1)}, bf16[17,64,384]{2,1,0:T(8,128)(2,1)}, u32[]{:S(2)}) %copy-start) | copy-done | bytes 835608
  2.5 0.0 copy-start.1
  2.5 0.9 %copy-done.1 = f32[64,512]{1,0:T(8,128)S(1)} copy-done((f32[64,512]{1,0:T(8,128)S(1)}, f32[64,512]{1,0:T(8,128)}, u32[]{:S(2)}) %copy-start.1) | copy-done | bytes 131096
  3.4 0.0 copy-start.2
  3.4 0.9 %copy-done.2 = f32[64,512]{1,0:T(8,128)S(1)} copy-done((f32[64,512]{1,0:T(8,128)S(1)}, f32[64,512]{1,0:T(8,128)}, u32[]{:S(2)}) %copy-start.2) | copy-done | bytes 131096
  4.3 1.1 %pack.1 = (f32[160,128]{1,0:T(8,128)S(1)}, f32[32,128]{1,0:T(8,128)S(1)}) custom-call(s32[1]{0:T(128)} %bitcast.dev, s32[96]{0:T(128)S(1)} %copy-done.4, f32[17,17]{1,0:T(8,128)S(1)} %copy-done.3, f32[64,512]{1,0:T(8,128)S(1)} %copy-done.1, f32[64,512]{1,0:T(8,128)S(1)} %copy-done.2, bf16[17,64,384]{2,1,0:T(8,128)(2,1)S(1)} %copy-done), custom_call_target="tpu_custom_call" | custom-call | flops 10000000 | bytes 4000000 | tf_op jit(solution)/shard_map/pack/pallas_call | solution.py:494
  5.4 6.4 %collective-permute-start.1 = (f32[32,128]{1,0:T(8,128)S(1)}, f32[32,128]{1,0:T(8,128)S(1)}, u32[]{:S(2)}, u32[]{:S(2)}) collective-permute-start(f32[32,128]{1,0:T(8,128)S(1)} %get-tuple-element.11), channel_id=1, source_target_pairs={{0,31},{1,2},{2,1},{3,4},{4,3},{5,6},{6,5},{7,8},{8,7},{9,10},{10,... | collective-permute-start | bytes 49160 | tf_op jit(solution)/shard_map/ppermute | solution.py:525
  11.8 0.0 collective-permute-start
  11.8 4.6 %own_tiles.1 = (f32[64,512]{1,0:T(8,128)S(1)}, f32[64,512]{1,0:T(8,128)S(1)}, bf16[17,64,384]{2,1,0:T(8,128)(2,1)S(1)}, bf16[2,288,144]{2,1,0:T(8,128)(2,1)S(1)}) custom-call(s32[1]{0:T(128)} %bitcast.dev, s32[96]{0:T(128)S(1)} %copy-done.4, f32[17,17]{1,0:T(8,128)S(1)} %copy-done.3, f32[64,512]{1,0:T(8,128)S(1)} %copy-done.1, f32[64,512]{1,0:T(8,128)S(1)} %copy-done.2, ...), custom_call_target="tpu_custom_call" | custom-call | flops 2000000000 | bytes 4000000 | tf_op jit(solution)/shard_map/own_tiles/pallas_call | solution.py:494
  16.4 0.0 collective-permute-done.1.outer
  16.4 0.0 collective-permute-done.inner
  16.4 6.4 %edges.1 = (f32[64,512]{1,0:T(8,128)}, f32[64,512]{1,0:T(8,128)}, bf16[17,64,384]{2,1,0:T(8,128)(2,1)}) custom-call(s32[1]{0:T(128)} %bitcast.dev, s32[96]{0:T(128)S(1)} %copy-done.4, f32[17,17]{1,0:T(8,128)S(1)} %copy-done.3, bf16[2,288,144]{2,1,0:T(8,128)(2,1)S(1)} %get-tuple-element.9.kron, f32[64,512]{1,0:T(8,128)S(1)} %copy-done.1, ...), custom_call_target="tpu_custom_call" | custom-call | flops 1000000000 | bytes 4000000 | tf_op jit(solution)/shard_map/edges/pallas_call | solution.py:494
Async XLA Ops:
  0.6 0.7 %copy-start.3 = (f32[17,17]{1,0:T(8,128)S(1)}, f32[17,17]{1,0:T(8,128)}, u32[]{:S(2)}) copy-start(f32[17,17]{1,0:T(8,128)} %kin.5) | copy-start | bytes 3472
  0.6 0.7 %copy-start.4 = (s32[96]{0:T(128)S(1)}, s32[96]{0:T(128)}, u32[]{:S(2)}) copy-start(s32[96]{0:T(128)} %wet.5) | copy-start | bytes 1156
  1.3 1.2 %copy-start = (bf16[17,64,384]{2,1,0:T(8,128)(2,1)S(1)}, bf16[17,64,384]{2,1,0:T(8,128)(2,1)}, u32[]{:S(2)}) copy-start(bf16[17,64,384]{2,1,0:T(8,128)(2,1)} %tracers.5) | copy-start | bytes 2506756
  2.5 0.9 %copy-start.1 = (f32[64,512]{1,0:T(8,128)S(1)}, f32[64,512]{1,0:T(8,128)}, u32[]{:S(2)}) copy-start(f32[64,512]{1,0:T(8,128)} %u0.3) | copy-start | bytes 393220
  3.4 0.9 %copy-start.2 = (f32[64,512]{1,0:T(8,128)S(1)}, f32[64,512]{1,0:T(8,128)}, u32[]{:S(2)}) copy-start(f32[64,512]{1,0:T(8,128)} %b0.3) | copy-start | bytes 393220
  5.4 11.0 %collective-permute-start.1 = (f32[32,128]{1,0:T(8,128)S(1)}, f32[32,128]{1,0:T(8,128)S(1)}, u32[]{:S(2)}, u32[]{:S(2)}) collective-permute-start(f32[32,128]{1,0:T(8,128)S(1)} %get-tuple-element.11), channel_id=1, source_target_pairs={{0,31},{1,2},{2,1},{3,4},{4,3},{5,6},{6,5},{7,8},{8,7},{9,10},{10,... | collective-permute-start | bytes 49160 | tf_op jit(solution)/shard_map/ppermute | solution.py:525
  11.8 4.6 %collective-permute-start = (f32[160,128]{1,0:T(8,128)S(1)}, f32[160,128]{1,0:T(8,128)S(1)}, u32[]{:S(2)}, u32[]{:S(2)}) collective-permute-start(f32[160,128]{1,0:T(8,128)S(1)} %get-tuple-element.10), channel_id=1, source_target_pairs={{0,1},{1,0},{2,3},{3,2},{4,5},{5,4},{6,7},{7,6},{8,9},{9,8},{10,11... | collective-permute-start | bytes 245768 | tf_op jit(solution)/shard_map/ppermute | solution.py:524

commit v2 on v1

v2 whole, which is shorter than its diff:
```python
import functools

import jax
import jax.numpy as jnp
from jax import lax
from jax.experimental import pallas as pl
from jax.experimental.pallas import tpu as pltpu
from jax.sharding import PartitionSpec as P

LANES = 128
STEPS = 2
WET_DEV = 3
OCEAN_DEV = 4

DT_OCEAN = 0.25
PRESSURE = 1.0
HORIZ_VISC = 0.2
VERT_VISC = 0.2
HEATING = 0.2
KAPPA_BASE = 0.05
KAPPA_SPAN = 0.35
DT_TRACER = 0.3
DT_MIX = 1.0
KINETIC_DELTA = 0.5
SURFACE_LIGHT = 10.0
WATER_ATT = 0.04
PIGMENT_ATT = 0.08
GROWTH = 0.05
THERMAL_GAIN = 0.1

SEG = 40
HALF = SEG // 2
FIX = 8
PAD = 8
F32, BF16 = jnp.float32, jnp.bfloat16


FACTS = (
    "odd",
    "gives",
    "x_slot",
    "x_tile",
    "outer_slot",
    "outer_tile",
    "beside_slot",
    "beside_tile",
    "outer_own_wet",
    "outer_far_wet",
    "beside_wet",
    "beyond_wet",
    "tile0",
    "tile1",
    "tile2",
    "joined0",
    "joined1",
)


def find_facts(dev_ref, wet_ref, out_ref):
    k = dev_ref[0]
    odd = lax.rem(k, 2)
    first, base = WET_DEV * k, OCEAN_DEV * k
    listed = wet_ref.shape[0]
    tiles = listed // WET_DEV * OCEAN_DEV
    is_odd = odd == 1
    w = [wet_ref[first + s] for s in range(WET_DEV)]
    probe = wet_ref[first + jnp.where(is_odd, -1, 3)]
    gives = jnp.logical_and(probe >= base, probe < base + OCEAN_DEV)
    before = jnp.where(k == 0, listed - 1, first - 1)
    after = jnp.where(first + WET_DEV == listed, 0, first + WET_DEV)
    outer_far = jnp.where(
        is_odd,
        jnp.where(base + OCEAN_DEV == tiles, 0, base + OCEAN_DEV),
        jnp.where(k == 0, tiles - 1, base - 1),
    )
    far_listed = wet_ref[first + jnp.where(is_odd, -2, 4)] == base + jnp.where(is_odd, -1, 4)
    f = {"odd": odd, "gives": gives, "x_slot": 2 - 2 * odd, "x_tile": 3 - 3 * odd}
    f["outer_slot"], f["outer_tile"] = 2 * odd, 3 * odd
    f["beside_slot"] = jnp.where(gives, 2 - 2 * odd, 1)
    f["beside_tile"] = jnp.where(gives, 2 - odd, 3 - 3 * odd)
    f["outer_own_wet"] = jnp.where(is_odd, w[2] == base + 3, w[0] == base)
    f["outer_far_wet"] = wet_ref[jnp.where(is_odd, after, before)] == outer_far
    f["beside_wet"] = jnp.logical_or(gives, w[1] == base + 3 - 3 * odd)
    f["beyond_wet"] = jnp.logical_or(jnp.logical_not(gives), far_listed)
    for s in range(WET_DEV):
        f[f"tile{s}"] = jnp.clip(w[s] - base, 0, OCEAN_DEV - 1)
    for s in range(WET_DEV - 1):
        x_here = jnp.logical_or(f["x_slot"] == s, f["x_slot"] == s + 1)
        f[f"joined{s}"] = jnp.logical_and(w[s + 1] - w[s] == 1, jnp.logical_or(gives, jnp.logical_not(x_here)))
    for i, name in enumerate(FACTS):
        out_ref[i] = f[name].astype(jnp.int32)


def read_facts(ref):
    return {name: ref[i] for i, name in enumerate(FACTS)}


def lane_of(rows):
    return lax.broadcasted_iota(jnp.int32, (rows, LANES), 1)


def lane_roll(x, shift):
    return pltpu.roll(x, shift, x.ndim - 1)


def upper(x):
    row = lax.broadcasted_iota(jnp.int32, x.shape, 0)
    return jnp.where(row == 0, x, pltpu.roll(x, 1, 0))


def lower(x):
    n = x.shape[0]
    row = lax.broadcasted_iota(jnp.int32, x.shape, 0)
    return jnp.where(row == n - 1, x, pltpu.roll(x, n - 1, 0))


def absorbed_light(pigment):
    att = WATER_ATT + PIGMENT_ATT * pigment * pigment
    depth = att
    rows = att.shape[0]
    row = lax.broadcasted_iota(jnp.int32, att.shape, 0)
    step = 1
    while step < rows:
        depth = depth + jnp.where(row >= step, pltpu.roll(depth, step, 0), 0.0)
        step *= 2
    return SURFACE_LIGHT * (jnp.exp(att - depth) - jnp.exp(-depth))


def new_velocity(u, u_left, u_right, b, b_right):
    horiz = u_left + u_right - 2.0 * u
    vert = upper(u) + lower(u) - 2.0 * u
    return u + DT_OCEAN * (HORIZ_VISC * horiz + VERT_VISC * vert - PRESSURE * (b_right - b))


def diffusivity(u, b):
    rows = u.shape[0]
    row = lax.broadcasted_iota(jnp.int32, u.shape, 0)
    shear = u - lower(u)
    strat = b - lower(b)
    kappa = KAPPA_BASE + KAPPA_SPAN * (1.0 / (1.0 + jnp.exp(-4.0 * (shear * shear - strat))))
    return jnp.where(row == rows - 1, 0.0, kappa)


def face_parts(u, face_open):
    w = DT_TRACER * u * face_open
    return jnp.maximum(w, 0.0), jnp.minimum(w, 0.0)


def advect(state, adv, t, left, right, coeffs, fields, levels):
    centre, from_left, from_right = coeffs
    chunk = 16
    lane = lane_of(chunk)
    for r in range(0, levels, chunk):
        here = state[:fields, t, r : r + chunk, :]
        to_left, to_right = here, here
        if right != t:
            to_left = jnp.where(lane == 0, state[:fields, right, r : r + chunk, :], here)
        if left != t:
            to_right = jnp.where(lane == LANES - 1, state[:fields, left, r : r + chunk, :], here)
        s = slice(r, r + chunk)
        adv[:fields, t, PAD + r : PAD + r + chunk, :] = (
            here * centre[s] + lane_roll(to_left, LANES - 1) * from_right[s] + lane_roll(to_right, 1) * from_left[s]
        )


def mix_and_react(adv, t, kappa, warmth, light, kron, fields, levels, emit):
    chunk = 16
    above = jnp.where(lax.broadcasted_iota(jnp.int32, kappa.shape, 0) == 0, 0.0, pltpu.roll(kappa, 1, 0))
    stay = 1.0 - DT_MIX * (kappa + above)
    rows = (fields + (18 - fields)) * 8
    k_hi = kron[:rows, :]
    k_both = kron[...]
    for r in range(0, levels, chunk):
        s = slice(r, r + chunk)
        at = PAD + r
        here = adv[:fields, t, at : at + chunk, :]
        up = adv[:fields, t, at - 1 : at - 1 + chunk, :]
        down = adv[:fields, t, at + 1 : at + 1 + chunk, :]
        mixed = here * stay[s] + (DT_MIX * kappa[s]) * down + (DT_MIX * above[s]) * up
        halves = []
        for h in range(2):
            part = mixed[:, 8 * h : 8 * h + 8, :].reshape(fields * 8, LANES)
            if fields < 18:
                part = jnp.concatenate([part, jnp.zeros(((18 - fields) * 8, LANES), F32)], axis=0)
            halves.append(part)
        wide = jnp.concatenate(halves, axis=1)
        hi = wide.astype(BF16)
        lo = (wide - hi.astype(F32)).astype(BF16)
        by_hi = jnp.dot(k_both, hi, preferred_element_type=F32)
        by_lo = jnp.dot(k_hi, lo, preferred_element_type=F32)
        drift = by_hi[:rows] + (by_hi[rows:] + by_lo)
        out = []
        for h in range(2):
            d = drift[:, LANES * h : LANES * h + LANES].reshape(18, 8, LANES)[:fields]
            sh = slice(r + 8 * h, r + 8 * h + 8)
            new = mixed[:, 8 * h : 8 * h + 8, :] + warmth[sh] * d
            first = new[:1] + GROWTH * light[sh][None]
            out.append(jnp.concatenate([first, new[1:]], axis=0))
        emit(r, jnp.concatenate(out, axis=1))


def tile_of(ref, index):
    return ref[:, pl.ds(pl.multiple_of(index * LANES, LANES), LANES)]


def slot_of(ref, j, index):
    return ref[j, :, pl.ds(pl.multiple_of(index * LANES, LANES), LANES)].astype(F32)


U_AT, B_AT, T0_AT, COMBO_AT, WIDE = 40, 44, 48, 50, 3


def pack_kernel(dev, wet_hbm, kin_hbm, u_hbm, b_hbm, t_hbm, inner, outer, u, b, tracers, kin_v, found, wet, kin, sems):
    pairs = ((wet_hbm, wet), (kin_hbm, kin), (t_hbm, tracers), (u_hbm, u), (b_hbm, b), (kin_hbm, kin_v))
    copies = [pltpu.make_async_copy(src, dst, sems.at[i]) for i, (src, dst) in enumerate(pairs)]
    for c in copies:
        c.start()
    for c in copies:
        c.wait()
    find_facts(dev, wet, found)
    f = read_facts(found)
    levels = u.shape[0]
    half = levels // 2
    n = tracers.shape[0]
    lane = lane_of(half)

    def combo_of(index):
        total = None
        for j in range(n):
            term = kin[0, j] * slot_of(tracers, j, index)
            total = term if total is None else total + term
        return total

    def put(acc, value, at, width, right):
        for h in range(2):
            to = at + 64 * h
            here = jnp.bitwise_and(lane + right * width - to, LANES - 1) < width
            acc = jnp.where(here, lane_roll(value[half * h : half * (h + 1)], to), acc)
        return acc

    def strip(slot, tile, combo, right):
        acc = jnp.zeros((half, LANES), F32)
        for j in range(n):
            acc = put(acc, slot_of(tracers, j, slot), 2 * j, 2, right)
        acc = put(acc, combo, 2 * n, 2, right)
        acc = put(acc, tile_of(u, tile), U_AT, WIDE, right)
        return put(acc, tile_of(b, tile), B_AT, WIDE, right)

    outer[...] = strip(f["outer_slot"], f["outer_tile"], combo_of(f["outer_slot"]), f["odd"])
    x_combo = combo_of(f["x_slot"])
    acc = strip(f["x_slot"], f["beside_tile"], x_combo, 1 - f["odd"])
    acc = put(acc, slot_of(tracers, 0, 1), T0_AT, 2, 1 - f["odd"])
    inner[:half] = put(acc, combo_of(1), COMBO_AT, 2, 1 - f["odd"])
    gives = f["gives"] == 1
    inner[half : half + levels] = jnp.where(gives, tile_of(u, f["x_tile"]), slot_of(tracers, 0, f["x_slot"]))
    inner[half + levels :] = jnp.where(gives, tile_of(b, f["x_tile"]), x_combo)


def patch_masks(f, rows):
    lane = lane_of(rows)
    near = jnp.where(f["odd"] == 1, LANES - 1 - lane, lane) < LANES // 2
    in_1 = jnp.logical_and(lane >= HALF, lane < HALF + SEG)
    in_2 = jnp.logical_and(lane >= HALF + SEG, lane < HALF + 2 * SEG)
    return near, in_1, in_2


def expand_kinetics(kin, kron):
    n = kin.shape[0]
    rows = (n + 1) * 8
    to_rows = lax.broadcasted_iota(jnp.int32, (rows, n), 0) // 8 == lax.broadcasted_iota(jnp.int32, (rows, n), 1)
    to_cols = lax.broadcasted_iota(jnp.int32, (n, rows), 1) // 8 == lax.broadcasted_iota(jnp.int32, (n, rows), 0)
    tall = jnp.dot(to_rows.astype(F32), kin[...], precision=lax.Precision.HIGHEST, preferred_element_type=F32)
    full = jnp.dot(tall, to_cols.astype(F32), precision=lax.Precision.HIGHEST, preferred_element_type=F32)
    row = lax.broadcasted_iota(jnp.int32, (rows, rows), 0)
    col = lax.broadcasted_iota(jnp.int32, (rows, rows), 1)
    full = jnp.where(lax.rem(row, 8) == lax.rem(col, 8), full, 0.0)
    with_combo = jnp.where(row < 8, jnp.where(col - 8 * n == row, 1.0, 0.0), full)
    for i, m in enumerate((with_combo, full)):
        hi = m.astype(BF16)
        kron[i, :rows, :] = hi
        kron[i, rows:, :] = (m - hi.astype(F32)).astype(BF16)


def start_tile(state, adv, t, fields, levels):
    for row in (0, PAD + levels):
        adv[:, t, row : row + 8, :] = jnp.zeros((fields, 8, LANES), F32)


def own_kernel(
    facts, kin, u0, b0, tracers, u_out, b_out, t_out, kron, p_state, p_u, p_b, u, b, state, adv
):
    f = read_facts(facts)
    levels = u0.shape[0]
    n = tracers.shape[0]
    lane = lane_of(levels)
    expand_kinetics(kin, kron)
    gives = f["gives"] == 1
    is_x = [jnp.logical_and(f["gives"] == 0, f["x_slot"] == s) for s in range(WET_DEV)]
    tile = [f[f"tile{s}"] for s in range(WET_DEV)]
    joined = [f["joined0"] == 1, f["joined1"] == 1, None]
    for t in range(OCEAN_DEV):
        u[t] = u0[:, LANES * t : LANES * (t + 1)]
        b[t] = b0[:, LANES * t : LANES * (t + 1)]
    for s in range(WET_DEV):
        state[:, s] = tracers[:, :, LANES * s : LANES * (s + 1)].astype(F32)
        start_tile(state, adv, s, n, levels)

    near, in_1, in_2 = patch_masks(f, levels)

    def lay(own, beside, x):
        seg1 = lane_roll(jnp.where(near, x, beside), SEG)
        return jnp.where(in_1, seg1, jnp.where(in_2, lane_roll(x, 2 * SEG), own))

    for p, field in ((p_u, u), (p_b, b)):
        p[...] = lay(field[f["outer_tile"]], field[f["beside_tile"]], field[f["x_tile"]])
    combos = [None] * 3
    for j in range(n):
        tiles = [state[j, f[name]] for name in ("outer_slot", "beside_slot", "x_slot")]
        p_state[j] = lay(*tiles)
        combos = [
            kin[0:1, j : j + 1] * x if c is None else c + kin[0:1, j : j + 1] * x for c, x in zip(combos, tiles)
        ]
    p_state[n] = lay(*combos)

    for step in range(STEPS):
        last = step == STEPS - 1
        light = []
        for s in range(WET_DEV):
            light.append(absorbed_light(state[0, s]))
            b[tile[s]] = b[tile[s]] + jnp.where(is_x[s], 0.0, HEATING) * light[s]
        us = [u[t] for t in range(OCEAN_DEV)]
        bs = [b[t] for t in range(OCEAN_DEV)]
        for t in range(OCEAN_DEV):
            nxt, prv = (t + 1) % OCEAN_DEV, (t - 1) % OCEAN_DEV
            u_right = lane_roll(jnp.where(lane == 0, us[nxt], us[t]), LANES - 1)
            u_left = lane_roll(jnp.where(lane == LANES - 1, us[prv], us[t]), 1)
            b_right = lane_roll(jnp.where(lane == 0, bs[nxt], bs[t]), LANES - 1)
            u[t] = new_velocity(us[t], u_left, u_right, bs[t], b_right)
            if last:
                u_out[t] = u[t]
                b_out[t] = bs[t]
        parts = []
        for s in range(WET_DEV):
            shut = lane == LANES - 1
            if joined[s] is not None:
                shut = jnp.logical_and(shut, jnp.logical_not(joined[s]))
            parts.append(face_parts(u[tile[s]], jnp.where(shut, 0.0, 1.0)))
        for s in range(WET_DEV):
            pos, neg = parts[s]
            before = parts[s - 1] if s else (jnp.zeros_like(pos), jnp.zeros_like(neg))
            pos_left = lane_roll(jnp.where(lane == LANES - 1, before[0], pos), 1)
            neg_left = lane_roll(jnp.where(lane == LANES - 1, before[1], neg), 1)
            coeffs = (1.0 - pos + neg_left, pos_left, -neg)
            advect(state, adv, s, max(s - 1, 0), min(s + 1, WET_DEV - 1), coeffs, n, levels)
        for s in range(WET_DEV):
            ub, bb = u[tile[s]], b[tile[s]]
            kappa = diffusivity(ub, bb)
            warmth = KINETIC_DELTA * jnp.exp(THERMAL_GAIN * bb)

            def emit(r, values, s=s):
                if last:
                    t_out[:, s, r : r + 16, :] = values.astype(BF16)
                else:
                    state[:, s, r : r + 16, :] = values

            mix_and_react(adv, s, kappa, warmth, light[s], kron.at[1], n, levels, emit)


def advance_alone(state, adv, u, b, heat, face_open, kron, n, levels, emit):
    for step in range(STEPS):
        last = step == STEPS - 1
        light = absorbed_light(state[0, 0])
        b = b + HEATING * heat * light
        u = new_velocity(u, lane_roll(u, 1), lane_roll(u, LANES - 1), b, lane_roll(b, LANES - 1))
        if last:
            emit(None, (u, b))
        count = n if last else n + 1
        pos, neg = face_parts(u, face_open)
        pos_left, neg_left = lane_roll(pos, 1), lane_roll(neg, 1)
        advect(state, adv, 0, 0, 0, (1.0 - pos + neg_left, pos_left, -neg), count, levels)
        kappa = diffusivity(u, b)
        warmth = KINETIC_DELTA * jnp.exp(THERMAL_GAIN * b)

        def put(r, values):
            state[:n, 0, r : r + 16, :] = values[:n]

        mix_and_react(adv, 0, kappa, warmth, light, kron.at[step], count, levels, emit if last else put)


def from_strip(ref, half, shift):
    return jnp.concatenate(
        [lane_roll(ref[:half], lax.rem(shift + 3 * LANES - 64 * h, LANES)) for h in range(2)], axis=0
    )


def x_kernel(
    facts, kin, kron, u0, b0, tracers, inner, pre_state, pre_u, pre_b, x_t, x_u, x_b, p_state, p_u, p_b, state, adv
):
    f = read_facts(facts)
    levels = u0.shape[0]
    half = levels // 2
    n = tracers.shape[0]
    gives = f["gives"] == 1
    lane = lane_of(levels)
    tile1 = inner[half : half + levels]
    tile2 = inner[half + levels :]
    u = jnp.where(gives, tile_of(u0, f["x_tile"]), tile1)
    b = jnp.where(gives, tile_of(b0, f["x_tile"]), tile2)
    start_tile(state, adv, 0, n + 1, levels)

    near, in_1, in_2 = patch_masks(f, levels)
    x_in_1 = jnp.logical_and(in_1, pltpu.roll(jnp.where(near, 1, 0), SEG, 1) == 1)
    beyond = jnp.logical_and(in_2, pltpu.roll(jnp.where(near, 1, 0), 2 * SEG, 1) == 1)
    strip_goes = jnp.where(gives, jnp.where(x_in_1, 1, 0), jnp.where(beyond, 1, 0)) == 1
    strip_seg = jnp.where(gives, SEG, 2 * SEG)

    def x_whole(patch, x):
        patch = jnp.where(x_in_1, lane_roll(x, SEG), patch)
        return jnp.where(in_2, lane_roll(x, 2 * SEG), patch)

    for p, pre, x, at in ((p_u, pre_u, u, U_AT), (p_b, pre_b, b, B_AT)):
        p[...] = jnp.where(beyond, from_strip(inner, half, 2 * SEG - at), x_whole(pre[...], x))
    for j in range(n):
        x = slot_of(tracers, j, f["x_slot"])
        patch = jnp.where(strip_goes, from_strip(inner, half, strip_seg - 2 * j), pre_state[j])
        if j == 0:
            x = jnp.where(gives, tile1, x)
            far = from_strip(inner, half, 2 * SEG - jnp.where(gives, T0_AT, 0))
            patch = jnp.where(beyond, far, x_whole(pre_state[j], x))
        p_state[j] = patch
        state[j, 0] = x
    far = from_strip(inner, half, 2 * SEG - jnp.where(gives, COMBO_AT, 2 * n))
    total = None
    for j in range(n):
        term = kin[0:1, j : j + 1] * slot_of(tracers, j, f["x_slot"])
        total = term if total is None else total + term
    combo = jnp.where(gives, tile2, total)
    state[n, 0] = combo
    p_state[n] = jnp.where(beyond, far, x_whole(pre_state[n], combo))

    def emit(r, values):
        if r is None:
            x_u[...], x_b[...] = values
        else:
            x_t[:, r : r + 16, :] = values

    face_open = jnp.where(lane == LANES - 1, 0.0, 1.0)
    advance_alone(state, adv, u, b, 1.0, face_open, kron, n, levels, emit)


def last_kernel(
    facts, kron, outer, pre_state, p_u, p_b, own_u, own_b, own_t, x_u, x_b, x_t,
    u_out, b_out, t_out, state, adv, whole_u, whole_b, merged, sems,
):
    f = read_facts(facts)
    levels = p_u.shape[0]
    half = levels // 2
    n = own_t.shape[0]
    gives, odd = f["gives"] == 1, f["odd"] == 1
    lane = lane_of(levels)
    near, in_1, in_2 = patch_masks(f, levels)
    halo = jnp.logical_not(jnp.logical_or(near, jnp.logical_or(in_1, in_2)))
    start_tile(state, adv, 0, n + 1, levels)
    u = jnp.where(halo, from_strip(outer, half, -U_AT), p_u[...])
    b = jnp.where(halo, from_strip(outer, half, -B_AT), p_b[...])
    for j in range(n + 1):
        state[j, 0] = jnp.where(halo, from_strip(outer, half, -2 * j), pre_state[j])

    def sides(here, there, boundary_at):
        return lane_roll(jnp.where(near, here.astype(F32), there.astype(F32)), boundary_at)

    one = jnp.int32(1)
    heat = jnp.where(
        in_1,
        sides(one, f["beside_wet"], SEG),
        jnp.where(in_2, sides(f["beyond_wet"], one, 2 * SEG), sides(f["outer_own_wet"], f["outer_far_wet"], 0)),
    )
    outer_open = (f["outer_own_wet"] * f["outer_far_wet"]).astype(F32)
    face_open = jnp.where(
        lane == LANES - 1,
        outer_open,
        jnp.where(
            lane == SEG - 1,
            f["beside_wet"].astype(F32),
            jnp.where(lane == 2 * SEG - 1, f["beyond_wet"].astype(F32), 1.0),
        ),
    )
    copies = []

    def send(src, dst):
        copies.append(pltpu.make_async_copy(src, dst, sems.at[len(copies)]))
        copies[-1].start()

    def at(index):
        return pl.ds(pl.multiple_of(index * LANES, LANES), LANES)

    def edge(rows, at_left):
        here = lane_of(rows)
        return jnp.where(at_left, here, LANES - 1 - here) < FIX

    left, right = edge(16, jnp.logical_not(odd)), edge(16, odd)
    outer_fix = jnp.logical_and(left, f["outer_own_wet"] == 1)
    beside_fix = jnp.logical_and(right, f["beside_wet"] == 1)
    third = jnp.where(gives, 1, f["x_slot"])

    def emit(r, values):
        if r is None:
            for i, (patch, own, x, whole, out) in enumerate(
                ((values[0], own_u, x_u, whole_u, u_out), (values[1], own_b, x_b, whole_b, b_out))
            ):
                seg1, seg2 = lane_roll(patch, LANES - SEG), lane_roll(patch, LANES - 2 * SEG)
                left_w, right_w = edge(levels, jnp.logical_not(odd)), edge(levels, odd)
                for t in range(OCEAN_DEV):
                    whole[:, LANES * t : LANES * (t + 1)] = own[t]

                x = jnp.where(left_w, seg1, jnp.where(right_w, seg2, x[...]))
                x = jnp.where(gives, x, own[f["x_tile"]])
                whole[:, at(f["x_tile"])] = x
                whole[:, at(f["outer_tile"])] = jnp.where(left_w, patch, own[f["outer_tile"]])
                whole[:, at(f["beside_tile"])] = jnp.where(right_w, seg1, own[f["beside_tile"]])
                send(whole, out)
            return
        s = slice(r, r + 16)
        seg1, seg2 = lane_roll(values, LANES - SEG), lane_roll(values, LANES - 2 * SEG)
        merged[:, 0, s, :] = jnp.where(outer_fix, values, own_t[:, f["outer_slot"], s, :].astype(F32)).astype(BF16)
        merged[:, 1, s, :] = jnp.where(beside_fix, seg1, own_t[:, f["beside_slot"], s, :].astype(F32)).astype(BF16)
        x = jnp.where(left, seg1, jnp.where(right, seg2, x_t[:, s, :]))
        merged[:, 2, s, :] = jnp.where(gives, own_t[:, 1, s, :].astype(F32), x).astype(BF16)

    advance_alone(state, adv, u, b, heat, face_open, kron, n, levels, emit)
    for i, slot in enumerate((f["outer_slot"], f["beside_slot"], third)):
        send(merged.at[:, i], t_out.at[:, :, at(slot)])
    for c in copies:
        c.wait()


def call(kernel, outs, scratch, args, spaces, out_spaces=None, flops=0, name=None):
    where = {"s": pltpu.SMEM, "v": pltpu.VMEM, "h": pltpu.HBM}
    out_spaces = out_spaces or "v" * len(outs)
    return pl.pallas_call(
        kernel,
        out_shape=tuple(
            pltpu.SMEM(s, d) if c == "s" else jax.ShapeDtypeStruct(s, d) for (s, d), c in zip(outs, out_spaces)
        ),
        in_specs=[pl.BlockSpec(memory_space=where[c]) for c in spaces],
        out_specs=tuple(pl.BlockSpec(memory_space=where[c]) for c in out_spaces),
        scratch_shapes=[pltpu.VMEM(s, F32) if isinstance(s, tuple) else s for s in scratch],
        compiler_params=pltpu.CompilerParams(vmem_limit_bytes=48 * 2**20),
        cost_estimate=pl.CostEstimate(flops=flops, bytes_accessed=4_000_000, transcendentals=0),
        name=name,
    )(*(pltpu.with_memory_space_constraint(a, pltpu.HBM) if c == "h" else a for a, c in zip(args, spaces)))


def on_device(ocean_u, ocean_b, tracers, wet_tiles, kinetic):
    axes = ("sec", "tile")
    devices = lax.axis_size("sec") * lax.axis_size("tile")
    levels, n = ocean_u.shape[0], tracers.shape[0]
    dev = (lax.axis_index("sec") * lax.axis_size("tile") + lax.axis_index("tile")).astype(jnp.int32).reshape(1)
    strip = levels // 2
    fields = n + 1
    ocean, tile = ocean_u.shape, (levels, LANES)
    wet_smem, kin_smem = pltpu.SMEM(wet_tiles.shape, jnp.int32), pltpu.SMEM(kinetic.shape, F32)
    inner, outer, u0, b0, t0, kinetic_v, facts = call(
        pack_kernel,
        [
            ((strip + 2 * levels, LANES), F32),
            ((strip, LANES), F32),
            (ocean, F32),
            (ocean, F32),
            (tracers.shape, BF16),
            (kinetic.shape, F32),
            ((len(FACTS),), jnp.int32),
        ],
        [wet_smem, kin_smem, pltpu.SemaphoreType.DMA((6,))],
        (dev, wet_tiles, kinetic, ocean_u, ocean_b, tracers),
        "shhhhh",
        "vvvvvvs",
        flops=10_000_000,
        name="pack",
    )
    in_pairs = [(i, i ^ 1) for i in range(devices)]
    across = [(i, (i + 1) % devices if i % 2 else (i - 1) % devices) for i in range(devices)]
    inner = lax.ppermute(inner, axes, in_pairs)
    outer = lax.ppermute(outer, axes, across)
    own_u, own_b, own_t, kron, p_state, p_u, p_b = call(
        own_kernel,
        [
            ((OCEAN_DEV, *tile), F32),
            ((OCEAN_DEV, *tile), F32),
            ((n, WET_DEV, *tile), BF16),
            ((2, 2 * fields * 8, fields * 8), BF16),
            ((fields, *tile), F32),
            (tile, F32),
            (tile, F32),
        ],
        [
            (OCEAN_DEV, *tile),
            (OCEAN_DEV, *tile),
            (n, WET_DEV, *tile),
            (n, WET_DEV, levels + 2 * PAD, LANES),
        ],
        (facts, kinetic_v, u0, b0, t0),
        "svvvv",
        flops=2_000_000_000,
        name="own_tiles",
    )
    alone = [(fields, 1, *tile), (fields, 1, levels + 2 * PAD, LANES)]
    x_t, x_u, x_b, p_state, p_u, p_b = call(
        x_kernel,
        [((n, *tile), F32), (tile, F32), (tile, F32), ((fields, *tile), F32), (tile, F32), (tile, F32)],
        alone,
        (facts, kinetic_v, kron, u0, b0, t0, inner, p_state, p_u, p_b),
        "s" + "v" * 9,
        flops=1_000_000_000,
        name="x_tile",
    )
    return tuple(
        call(
            last_kernel,
            [(ocean, F32), (ocean, F32), (tracers.shape, BF16)],
            [*alone, ocean, ocean, pltpu.VMEM((n, WET_DEV, *tile), BF16), pltpu.SemaphoreType.DMA((5,))],
            (facts, kron, outer, p_state, p_u, p_b, own_u, own_b, own_t, x_u, x_b, x_t),
            "s" + "v" * 11,
            "hhh",
            flops=1_000_000_000,
            name="boundaries",
        )
    )


def solution(mesh):
    spread = P(None, ("sec", "tile"))
    tracer_spread = P(None, None, ("sec", "tile"))

    def program(ocean_u, ocean_b, tracers, wet_tiles, kinetic_matrix):
        u, b, t = jax.shard_map(
            on_device,
            mesh=mesh,
            in_specs=(spread, spread, tracer_spread, P(), P()),
            out_specs=(spread, spread, tracer_spread),
            check_vma=False,
        )(ocean_u, ocean_b, tracers, wet_tiles, kinetic_matrix)
        return t, u, b

    return program
```

time: 23.1 us -> 17.9 us (0.77)
  local copies, waits for them, and re-layouts: 3.65 us -> 0 us
  Pallas kernels: 12 us -> 10.6 us
    unnamed x10 -> x0, local copies, waits for them, and re-layouts: 3.65 us -> none
    pallas_call x3 -> x4, Pallas kernels: 12 us -> 10.6 us  [call(): pl.pallas_call(kernel, out_shape=tuple((pltpu.SMEM(s, d) if c == 's' else...]
  transfers between devices with their start and end apart: 2 -> 2, of which waited for: 0 -> 0; matrix products, arithmetic and copies ran while one was open for 0% -> 0% of each run, Pallas kernels for 20% -> 34%
where the time goes in v2:
time: 17.9 us; the launch traced here: 17.8 us
  Pallas kernels  10.6 us (59%)
  starting transfers between devices  6.44 us (36%)
  between operations  0.67 us (4%)
    pallas_call x4, Pallas kernels, call(): pl.pallas_call(kernel, out_shape=tuple((pltpu.SMEM(s, d) if c == 's' else...  10.6 us
    ppermute x1, starting transfers between devices, on_device(): outer = lax.ppermute(outer, axes, across)  6.44 us
  transfers between devices with their start and end apart: 2, of which 0 were waited for; matrix products, arithmetic and copies ran while one was open for 0% of the time, Pallas kernels for 34%

profile of v2, /device:TPU:0, one launch (start us, length us, event | category | flops | bytes accessed | tf_op | source)
XLA Modules:
  0.0 17.8 jit_solution(7583262125677715894)
XLA Ops:
  0.6 1.6 %pack.1 = (f32[160,128]{1,0:T(8,128)S(1)}, f32[32,128]{1,0:T(8,128)S(1)}, f32[64,512]{1,0:T(8,128)S(1)}, f32[64,512]{1,0:T(8,128)S(1)}, bf16[17,64,384]{2,1,0:T(...) custom-call(s32[1]{0:T(128)} %bitcast.dev, s32[96]{0:T(128)} %wet_hbm.1, f32[17,17]{1,0:T(8,128)} %kin_hbm.1, ...), custom_call_target="tpu_custom_call" | custom-call | flops 10000000 | bytes 4000000 | tf_op jit(solution)/shard_map/pack/pallas_call | solution.py:540
  2.2 6.4 %collective-permute-start = (f32[32,128]{1,0:T(8,128)S(1)}, f32[32,128]{1,0:T(8,128)S(1)}, u32[]{:S(2)}, u32[]{:S(2)}) collective-permute-start(f32[32,128]{1,0:T(8,128)S(1)} %get-tuple-element.29), channel_id=1, source_target_pairs={{0,31},{1,2},{2,1},{3,4},{4,3},{5,6},{6,5},{7,8},{8,7},{9,10},{10,... | collective-permute-start | bytes 49160 | tf_op jit(solution)/shard_map/ppermute | solution.py:584
  8.7 0.0 collective-permute-start.1
  8.7 4.4 %own_tiles.1 = (f32[4,64,128]{2,1,0:T(8,128)S(1)}, f32[4,64,128]{2,1,0:T(8,128)S(1)}, bf16[17,3,64,128]{3,2,1,0:T(8,128)(2,1)S(1)}, bf16[2,288,144]{2,1,0:T(8,12...) custom-call(s32[17]{0:T(128)S(4)} %get-tuple-element.23.facts, ...), custom_call_target="tpu_custom_call" | custom-call | flops 2000000000 | bytes 4000000 | tf_op jit(solution)/shard_map/own_tiles/pallas_call | solution.py:540
  13.1 0.0 collective-permute-done.1.inner
  13.1 1.7 %x_tile.1 = (f32[17,64,128]{2,1,0:T(8,128)S(1)}, f32[64,128]{1,0:T(8,128)S(1)}, f32[64,128]{1,0:T(8,128)S(1)}, f32[18,64,128]{2,1,0:T(8,128)S(1)}, f32[64,128]{1,0:T(8,128)S(1)}, /*index=5*/f32[64,128]{1,0:T(8,128)S(1)}) custom-call(s32[17]{0:T(128)S(4)} %get-tuple-element.23.facts, f32[17,17]{1,0:T(8,128)S(1)} %get-tuple-element.24.kin, ...), custom_call_target="tpu_custom_call" | custom-call | flops 1000000000 | bytes 4000000 | tf_op jit(solution)/shard_map/x_tile/pallas_call | solution.py:540
  14.8 0.0 collective-permute-done.outer
  14.8 2.9 %boundaries.1 = (f32[64,512]{1,0:T(8,128)}, f32[64,512]{1,0:T(8,128)}, bf16[17,64,384]{2,1,0:T(8,128)(2,1)}) custom-call(s32[17]{0:T(128)S(4)} %get-tuple-element.23.facts, bf16[2,288,144]{2,1,0:T(8,128)(2,1)S(1)} %get-tuple-element.28.kron, f32[32,128]{1,0:T(8,128)S(1)} %collective-permute-done.outer, f32[18,64,128]{2,1,0:T(8,128)S(1)} %get-tuple-element.34.pre_state, ...), custom_call_target="tpu_custom_call" | custom-call | flops 1000000000 | bytes 4000000 | tf_op jit(solution)/shard_map/boundaries/pallas_call | solution.py:540
Async XLA Ops:
  2.2 12.6 %collective-permute-start = (f32[32,128]{1,0:T(8,128)S(1)}, f32[32,128]{1,0:T(8,128)S(1)}, u32[]{:S(2)}, u32[]{:S(2)}) collective-permute-start(f32[32,128]{1,0:T(8,128)S(1)} %get-tuple-element.29), channel_id=1, source_target_pairs={{0,31},{1,2},{2,1},{3,4},{4,3},{5,6},{6,5},{7,8},{8,7},{9,10},{10,... | collective-permute-start | bytes 49160 | tf_op jit(solution)/shard_map/ppermute | solution.py:584
  8.7 4.4 %collective-permute-start.1 = (f32[160,128]{1,0:T(8,128)S(1)}, f32[160,128]{1,0:T(8,128)S(1)}, u32[]{:S(2)}, u32[]{:S(2)}) collective-permute-start(f32[160,128]{1,0:T(8,128)S(1)} %get-tuple-element.30), channel_id=1, source_target_pairs={{0,1},{1,0},{2,3},{3,2},{4,5},{5,4},{6,7},{7,6},{8,9},{9,8},{10,11... | collective-permute-start | bytes 245768 | tf_op jit(solution)/shard_map/ppermute | solution.py:583

commit v3 on v2

--- a/solution.py
+++ b/solution.py
@@ -53,10 +53,11 @@
     "tile2",
     "joined0",
     "joined1",
+    "early",
 )
 
 
-def find_facts(dev_ref, wet_ref, out_ref):
+def find_facts(share, dev_ref, wet_ref, out_ref):
     k = dev_ref[0]
     odd = lax.rem(k, 2)
     first, base = WET_DEV * k, OCEAN_DEV * k
@@ -74,7 +75,7 @@
         jnp.where(k == 0, tiles - 1, base - 1),
     )
     far_listed = wet_ref[first + jnp.where(is_odd, -2, 4)] == base + jnp.where(is_odd, -1, 4)
-    f = {"odd": odd, "gives": gives, "x_slot": 2 - 2 * odd, "x_tile": 3 - 3 * odd}
+    f = {"odd": odd, "early": lax.rem(k, share) == 0, "gives": gives, "x_slot": 2 - 2 * odd, "x_tile": 3 - 3 * odd}
     f["outer_slot"], f["outer_tile"] = 2 * odd, 3 * odd
     f["beside_slot"] = jnp.where(gives, 2 - 2 * odd, 1)
     f["beside_tile"] = jnp.where(gives, 2 - odd, 3 - 3 * odd)
@@ -146,21 +147,21 @@
     return jnp.maximum(w, 0.0), jnp.minimum(w, 0.0)
 
 
-def advect(state, adv, t, left, right, coeffs, fields, levels):
+def advect(state, adv, t, src, left, right, coeffs, fields, levels):
     centre, from_left, from_right = coeffs
     chunk = 16
     lane = lane_of(chunk)
     for r in range(0, levels, chunk):
-        here = state[:fields, t, r : r + chunk, :]
-        to_left, to_right = here, here
-        if right != t:
-            to_left = jnp.where(lane == 0, state[:fields, right, r : r + chunk, :], here)
-        if left != t:
-            to_right = jnp.where(lane == LANES - 1, state[:fields, left, r : r + chunk, :], here)
         s = slice(r, r + chunk)
-        adv[:fields, t, PAD + r : PAD + r + chunk, :] = (
-            here * centre[s] + lane_roll(to_left, LANES - 1) * from_right[s] + lane_roll(to_right, 1) * from_left[s]
-        )
+        for f in range(fields):
+            here = to_left = to_right = state[f, src, s, :]
+            if right is not None:
+                to_left = jnp.where(lane == 0, state[f, right, s, :], here)
+            if left is not None:
+                to_right = jnp.where(lane == LANES - 1, state[f, left, s, :], here)
+            adv[f, t, PAD + r : PAD + r + chunk, :] = (
+                here * centre[s] + lane_roll(to_left, LANES - 1) * from_right[s] + lane_roll(to_right, 1) * from_left[s]
+            )
 
 
 def mix_and_react(adv, t, kappa, warmth, light, kron, fields, levels, emit):
@@ -210,14 +211,16 @@
 U_AT, B_AT, T0_AT, COMBO_AT, WIDE = 40, 44, 48, 50, 3
 
 
-def pack_kernel(dev, wet_hbm, kin_hbm, u_hbm, b_hbm, t_hbm, inner, outer, u, b, tracers, kin_v, found, wet, kin, sems):
+def pack_kernel(
+    share, dev, wet_hbm, kin_hbm, u_hbm, b_hbm, t_hbm, inner, outer, u, b, tracers, kin_v, found, wet, kin, sems
+):
     pairs = ((wet_hbm, wet), (kin_hbm, kin), (t_hbm, tracers), (u_hbm, u), (b_hbm, b), (kin_hbm, kin_v))
     copies = [pltpu.make_async_copy(src, dst, sems.at[i]) for i, (src, dst) in enumerate(pairs)]
     for c in copies:
         c.start()
     for c in copies:
         c.wait()
-    find_facts(dev, wet, found)
+    find_facts(share, dev, wet, found)
     f = read_facts(found)
     levels = u.shape[0]
     half = levels // 2
@@ -238,17 +241,16 @@
             acc = jnp.where(here, lane_roll(value[half * h : half * (h + 1)], to), acc)
         return acc
 
-    def strip(slot, tile, combo, right):
+    def strip(slot, tile, right):
         acc = jnp.zeros((half, LANES), F32)
         for j in range(n):
             acc = put(acc, slot_of(tracers, j, slot), 2 * j, 2, right)
-        acc = put(acc, combo, 2 * n, 2, right)
         acc = put(acc, tile_of(u, tile), U_AT, WIDE, right)
         return put(acc, tile_of(b, tile), B_AT, WIDE, right)
 
-    outer[...] = strip(f["outer_slot"], f["outer_tile"], combo_of(f["outer_slot"]), f["odd"])
+    outer[...] = strip(f["outer_slot"], f["outer_tile"], f["odd"])
     x_combo = combo_of(f["x_slot"])
-    acc = strip(f["x_slot"], f["beside_tile"], x_combo, 1 - f["odd"])
+    acc = strip(f["x_slot"], f["beside_tile"], 1 - f["odd"])
     acc = put(acc, slot_of(tracers, 0, 1), T0_AT, 2, 1 - f["odd"])
     inner[:half] = put(acc, combo_of(1), COMBO_AT, 2, 1 - f["odd"])
     gives = f["gives"] == 1
@@ -286,48 +288,44 @@
         adv[:, t, row : row + 8, :] = jnp.zeros((fields, 8, LANES), F32)
 
 
-def own_kernel(
-    facts, kin, u0, b0, tracers, u_out, b_out, t_out, kron, p_state, p_u, p_b, u, b, state, adv
-):
+def own_kernel(part, facts, kin, u0, b0, tracers, *refs):
+    u, b, state, kron, p_state, p_u, p_b = refs[-9:-2] if part == 0 else refs[-8:-1]
+    adv = refs[-1]
+    if part == 0:
+        refs[-2][...] = refs[0][...]
     f = read_facts(facts)
     levels = u0.shape[0]
     n = tracers.shape[0]
     lane = lane_of(levels)
-    expand_kinetics(kin, kron)
     gives = f["gives"] == 1
-    is_x = [jnp.logical_and(f["gives"] == 0, f["x_slot"] == s) for s in range(WET_DEV)]
     tile = [f[f"tile{s}"] for s in range(WET_DEV)]
-    joined = [f["joined0"] == 1, f["joined1"] == 1, None]
-    for t in range(OCEAN_DEV):
-        u[t] = u0[:, LANES * t : LANES * (t + 1)]
-        b[t] = b0[:, LANES * t : LANES * (t + 1)]
-    for s in range(WET_DEV):
-        state[:, s] = tracers[:, :, LANES * s : LANES * (s + 1)].astype(F32)
-        start_tile(state, adv, s, n, levels)
-
-    near, in_1, in_2 = patch_masks(f, levels)
-
-    def lay(own, beside, x):
-        seg1 = lane_roll(jnp.where(near, x, beside), SEG)
-        return jnp.where(in_1, seg1, jnp.where(in_2, lane_roll(x, 2 * SEG), own))
-
-    for p, field in ((p_u, u), (p_b, b)):
-        p[...] = lay(field[f["outer_tile"]], field[f["beside_tile"]], field[f["x_tile"]])
-    combos = [None] * 3
-    for j in range(n):
-        tiles = [state[j, f[name]] for name in ("outer_slot", "beside_slot", "x_slot")]
-        p_state[j] = lay(*tiles)
-        combos = [
-            kin[0:1, j : j + 1] * x if c is None else c + kin[0:1, j : j + 1] * x for c, x in zip(combos, tiles)
-        ]
-    p_state[n] = lay(*combos)
-
-    for step in range(STEPS):
-        last = step == STEPS - 1
+    joined = [f["joined0"], f["joined1"]]
+
+    def start():
+        expand_kinetics(kin, kron)
+        for t in range(OCEAN_DEV):
+            u[t] = u0[:, LANES * t : LANES * (t + 1)]
+            b[t] = b0[:, LANES * t : LANES * (t + 1)]
+        for s in range(WET_DEV):
+            state[:, s] = tracers[:, :, LANES * s : LANES * (s + 1)].astype(F32)
+
+        near, in_1, in_2 = patch_masks(f, levels)
+
+        def lay(own, beside, x):
+            seg1 = lane_roll(jnp.where(near, x, beside), SEG)
+            return jnp.where(in_1, seg1, jnp.where(in_2, lane_roll(x, 2 * SEG), own))
+
+        for p, field in ((p_u, u), (p_b, b)):
+            p[...] = lay(field[f["outer_tile"]], field[f["beside_tile"]], field[f["x_tile"]])
+        for j in range(n):
+            p_state[j] = lay(*[state[j, f[name]] for name in ("outer_slot", "beside_slot", "x_slot")])
+
+    def one_step(count, first, tile, joined):
         light = []
-        for s in range(WET_DEV):
-            light.append(absorbed_light(state[0, s]))
-            b[tile[s]] = b[tile[s]] + jnp.where(is_x[s], 0.0, HEATING) * light[s]
+        for s in range(count):
+            start_tile(state, adv, s, n, levels)
+            light.append(absorbed_light(state[0, first + s]))
+            b[tile[s]] = b[tile[s]] + HEATING * light[s]
         us = [u[t] for t in range(OCEAN_DEV)]
         bs = [b[t] for t in range(OCEAN_DEV)]
         for t in range(OCEAN_DEV):
@@ -336,37 +334,50 @@
             u_left = lane_roll(jnp.where(lane == LANES - 1, us[prv], us[t]), 1)
             b_right = lane_roll(jnp.where(lane == 0, bs[nxt], bs[t]), LANES - 1)
             u[t] = new_velocity(us[t], u_left, u_right, bs[t], b_right)
-            if last:
-                u_out[t] = u[t]
-                b_out[t] = bs[t]
         parts = []
-        for s in range(WET_DEV):
+        for s in range(count):
             shut = lane == LANES - 1
-            if joined[s] is not None:
-                shut = jnp.logical_and(shut, jnp.logical_not(joined[s]))
+            if s < count - 1:
+                shut = jnp.logical_and(shut, joined[s] == 0)
             parts.append(face_parts(u[tile[s]], jnp.where(shut, 0.0, 1.0)))
-        for s in range(WET_DEV):
+        for s in range(count):
             pos, neg = parts[s]
             before = parts[s - 1] if s else (jnp.zeros_like(pos), jnp.zeros_like(neg))
             pos_left = lane_roll(jnp.where(lane == LANES - 1, before[0], pos), 1)
             neg_left = lane_roll(jnp.where(lane == LANES - 1, before[1], neg), 1)
             coeffs = (1.0 - pos + neg_left, pos_left, -neg)
-            advect(state, adv, s, max(s - 1, 0), min(s + 1, WET_DEV - 1), coeffs, n, levels)
-        for s in range(WET_DEV):
+            left = first + s - 1 if s else None
+            right = first + s + 1 if s < count - 1 else None
+            advect(state, adv, s, first + s, left, right, coeffs, n, levels)
+        for s in range(count):
             ub, bb = u[tile[s]], b[tile[s]]
             kappa = diffusivity(ub, bb)
             warmth = KINETIC_DELTA * jnp.exp(THERMAL_GAIN * bb)
 
             def emit(r, values, s=s):
-                if last:
-                    t_out[:, s, r : r + 16, :] = values.astype(BF16)
-                else:
-                    state[:, s, r : r + 16, :] = values
+                state[:, first + s, r : r + 16, :] = values
 
             mix_and_react(adv, s, kappa, warmth, light[s], kron.at[1], n, levels, emit)
 
-
-def advance_alone(state, adv, u, b, heat, face_open, kron, n, levels, emit):
+    early = f["early"] == 1
+    if part == 0:
+        pl.when(early)(start)
+    else:
+        pl.when(jnp.logical_not(early))(start)
+
+        @pl.when(gives)
+        def _():
+            pl.loop(0, STEPS)(lambda _: one_step(WET_DEV, 0, tile, joined))
+
+        @pl.when(jnp.logical_not(gives))
+        def _():
+            odd = f["odd"]
+            tiles = [jnp.where(odd == 1, tile[s + 1], tile[s]) for s in range(WET_DEV - 1)]
+            pairs = [jnp.where(odd == 1, joined[1], joined[0])]
+            pl.loop(0, STEPS)(lambda _: one_step(WET_DEV - 1, odd, tiles, pairs))
+
+
+def advance_alone(state, adv, u, b, heat, face_open, kron, n, levels, emit, combined):
     for step in range(STEPS):
         last = step == STEPS - 1
         light = absorbed_light(state[0, 0])
@@ -374,17 +385,18 @@
         u = new_velocity(u, lane_roll(u, 1), lane_roll(u, LANES - 1), b, lane_roll(b, LANES - 1))
         if last:
             emit(None, (u, b))
-        count = n if last else n + 1
+        by_field = combined and not last
+        count = n + 1 if by_field else n
         pos, neg = face_parts(u, face_open)
         pos_left, neg_left = lane_roll(pos, 1), lane_roll(neg, 1)
-        advect(state, adv, 0, 0, 0, (1.0 - pos + neg_left, pos_left, -neg), count, levels)
+        advect(state, adv, 0, 0, None, None, (1.0 - pos + neg_left, pos_left, -neg), count, levels)
         kappa = diffusivity(u, b)
         warmth = KINETIC_DELTA * jnp.exp(THERMAL_GAIN * b)
 
         def put(r, values):
             state[:n, 0, r : r + 16, :] = values[:n]
 
-        mix_and_react(adv, 0, kappa, warmth, light, kron.at[step], count, levels, emit if last else put)
+        mix_and_react(adv, 0, kappa, warmth, light, kron.at[0 if by_field else 1], count, levels, emit if last else put)
 
 
 def from_strip(ref, half, shift):
@@ -394,7 +406,8 @@
 
 
 def x_kernel(
-    facts, kin, kron, u0, b0, tracers, inner, pre_state, pre_u, pre_b, x_t, x_u, x_b, p_state, p_u, p_b, state, adv
+    facts, kron, u0, b0, tracers, inner, pre_state, pre_u, pre_b,
+    x_t, x_u, x_b, p_state, p_combo, p_u, p_b, state, adv,
 ):
     f = read_facts(facts)
     levels = u0.shape[0]
@@ -404,52 +417,69 @@
     lane = lane_of(levels)
     tile1 = inner[half : half + levels]
     tile2 = inner[half + levels :]
-    u = jnp.where(gives, tile_of(u0, f["x_tile"]), tile1)
-    b = jnp.where(gives, tile_of(b0, f["x_tile"]), tile2)
-    start_tile(state, adv, 0, n + 1, levels)
+    start_tile(state, adv, 0, n, levels)
 
     near, in_1, in_2 = patch_masks(f, levels)
-    x_in_1 = jnp.logical_and(in_1, pltpu.roll(jnp.where(near, 1, 0), SEG, 1) == 1)
-    beyond = jnp.logical_and(in_2, pltpu.roll(jnp.where(near, 1, 0), 2 * SEG, 1) == 1)
-    strip_goes = jnp.where(gives, jnp.where(x_in_1, 1, 0), jnp.where(beyond, 1, 0)) == 1
-    strip_seg = jnp.where(gives, SEG, 2 * SEG)
+    x_in_1 = jnp.logical_and(in_1, lane_roll(jnp.where(near, 1, 0), SEG) == 1)
+    beyond = jnp.logical_and(in_2, lane_roll(jnp.where(near, 1, 0), 2 * SEG) == 1)
+    face_open = jnp.where(lane == LANES - 1, 0.0, 1.0)
 
     def x_whole(patch, x):
         patch = jnp.where(x_in_1, lane_roll(x, SEG), patch)
         return jnp.where(in_2, lane_roll(x, 2 * SEG), patch)
 
-    for p, pre, x, at in ((p_u, pre_u, u, U_AT), (p_b, pre_b, b, B_AT)):
-        p[...] = jnp.where(beyond, from_strip(inner, half, 2 * SEG - at), x_whole(pre[...], x))
-    for j in range(n):
-        x = slot_of(tracers, j, f["x_slot"])
-        patch = jnp.where(strip_goes, from_strip(inner, half, strip_seg - 2 * j), pre_state[j])
-        if j == 0:
-            x = jnp.where(gives, tile1, x)
-            far = from_strip(inner, half, 2 * SEG - jnp.where(gives, T0_AT, 0))
-            patch = jnp.where(beyond, far, x_whole(pre_state[j], x))
-        p_state[j] = patch
-        state[j, 0] = x
-    far = from_strip(inner, half, 2 * SEG - jnp.where(gives, COMBO_AT, 2 * n))
-    total = None
-    for j in range(n):
-        term = kin[0:1, j : j + 1] * slot_of(tracers, j, f["x_slot"])
-        total = term if total is None else total + term
-    combo = jnp.where(gives, tile2, total)
-    state[n, 0] = combo
-    p_state[n] = jnp.where(beyond, far, x_whole(pre_state[n], combo))
-
-    def emit(r, values):
-        if r is None:
-            x_u[...], x_b[...] = values
-        else:
-            x_t[:, r : r + 16, :] = values
-
-    face_open = jnp.where(lane == LANES - 1, 0.0, 1.0)
-    advance_alone(state, adv, u, b, 1.0, face_open, kron, n, levels, emit)
+    def with_far(patch, at):
+        return jnp.where(beyond, from_strip(inner, half, 2 * SEG - at), patch)
+
+    @pl.when(gives)
+    def _():
+        p_u[...] = with_far(pre_u[...], U_AT)
+        p_b[...] = with_far(pre_b[...], B_AT)
+        for j in range(1, n):
+            p_state[j] = jnp.where(x_in_1, from_strip(inner, half, SEG - 2 * j), pre_state[j])
+        p_state[0] = with_far(x_whole(pre_state[0], tile1), T0_AT)
+        p_combo[...] = with_far(x_whole(pre_state[0], tile2), COMBO_AT)
+        state[0, 0], state[1, 0] = tile1, tile2
+        u, b = tile_of(u0, f["x_tile"]), tile_of(b0, f["x_tile"])
+        for step in range(STEPS):
+            light = absorbed_light(state[0, 0])
+            b = b + HEATING * light
+            u = new_velocity(u, lane_roll(u, 1), lane_roll(u, LANES - 1), b, lane_roll(b, LANES - 1))
+            if step < STEPS - 1:
+                pos, neg = face_parts(u, face_open)
+                pos_left, neg_left = lane_roll(pos, 1), lane_roll(neg, 1)
+                advect(state, adv, 0, 0, None, None, (1.0 - pos + neg_left, pos_left, -neg), 2, levels)
+                kappa = diffusivity(u, b)
+                mixed = []
+                for i in range(2):
+                    field = adv[i, 0, PAD : PAD + levels, :]
+                    flux = kappa * (lower(field) - field)
+                    row = lax.broadcasted_iota(jnp.int32, flux.shape, 0)
+                    mixed.append(field + DT_MIX * (flux - jnp.where(row == 0, 0.0, pltpu.roll(flux, 1, 0))))
+                warmth = KINETIC_DELTA * jnp.exp(THERMAL_GAIN * b)
+                state[0, 0] = mixed[0] + warmth * mixed[1] + GROWTH * light
+        x_u[...], x_b[...] = u, b
+
+    @pl.when(jnp.logical_not(gives))
+    def _():
+        p_u[...] = with_far(x_whole(pre_u[...], tile1), U_AT)
+        p_b[...] = with_far(x_whole(pre_b[...], tile2), B_AT)
+        for j in range(n):
+            p_state[j] = with_far(pre_state[j], 2 * j)
+            state[j, 0] = slot_of(tracers, j, f["x_slot"])
+        p_combo[...] = pre_state[0]
+
+        def emit(r, values):
+            if r is None:
+                x_u[...], x_b[...] = values
+            else:
+                x_t[:, r : r + 16, :] = values
+
+        advance_alone(state, adv, tile1, tile2, 1.0, face_open, kron, n, levels, emit, False)
 
 
 def last_kernel(
-    facts, kron, outer, pre_state, p_u, p_b, own_u, own_b, own_t, x_u, x_b, x_t,
+    facts, kin, kron, outer, pre_state, p_combo, p_u, p_b, own_u, own_b, own_t, x_u, x_b, x_t,
     u_out, b_out, t_out, state, adv, whole_u, whole_b, merged, sems,
 ):
     f = read_facts(facts)
@@ -463,8 +493,14 @@
     start_tile(state, adv, 0, n + 1, levels)
     u = jnp.where(halo, from_strip(outer, half, -U_AT), p_u[...])
     b = jnp.where(halo, from_strip(outer, half, -B_AT), p_b[...])
-    for j in range(n + 1):
-        state[j, 0] = jnp.where(halo, from_strip(outer, half, -2 * j), pre_state[j])
+    combo = None
+    for j in range(n):
+        x = jnp.where(halo, from_strip(outer, half, -2 * j), pre_state[j])
+        state[j, 0] = x
+        combo = kin[0:1, j : j + 1] * x if combo is None else combo + kin[0:1, j : j + 1] * x
+    x_in_1 = jnp.logical_and(in_1, lane_roll(jnp.where(near, 1, 0), SEG) == 1)
+    handed = jnp.logical_and(gives, jnp.logical_or(x_in_1, in_2))
+    state[n, 0] = jnp.where(handed, p_combo[...], combo)
 
     def sides(here, there, boundary_at):
         return lane_roll(jnp.where(near, here.astype(F32), there.astype(F32)), boundary_at)
@@ -522,19 +558,19 @@
             return
         s = slice(r, r + 16)
         seg1, seg2 = lane_roll(values, LANES - SEG), lane_roll(values, LANES - 2 * SEG)
-        merged[:, 0, s, :] = jnp.where(outer_fix, values, own_t[:, f["outer_slot"], s, :].astype(F32)).astype(BF16)
-        merged[:, 1, s, :] = jnp.where(beside_fix, seg1, own_t[:, f["beside_slot"], s, :].astype(F32)).astype(BF16)
+        merged[:, 0, s, :] = jnp.where(outer_fix, values, own_t[:, f["outer_slot"], s, :]).astype(BF16)
+        merged[:, 1, s, :] = jnp.where(beside_fix, seg1, own_t[:, f["beside_slot"], s, :]).astype(BF16)
         x = jnp.where(left, seg1, jnp.where(right, seg2, x_t[:, s, :]))
-        merged[:, 2, s, :] = jnp.where(gives, own_t[:, 1, s, :].astype(F32), x).astype(BF16)
-
-    advance_alone(state, adv, u, b, heat, face_open, kron, n, levels, emit)
+        merged[:, 2, s, :] = jnp.where(gives, own_t[:, 1, s, :], x).astype(BF16)
+
+    advance_alone(state, adv, u, b, heat, face_open, kron, n, levels, emit, True)
     for i, slot in enumerate((f["outer_slot"], f["beside_slot"], third)):
         send(merged.at[:, i], t_out.at[:, :, at(slot)])
     for c in copies:
         c.wait()
 
 
-def call(kernel, outs, scratch, args, spaces, out_spaces=None, flops=0, name=None):
+def call(kernel, outs, scratch, args, spaces, out_spaces=None, aliases=None, flops=0, name=None):
     where = {"s": pltpu.SMEM, "v": pltpu.VMEM, "h": pltpu.HBM}
     out_spaces = out_spaces or "v" * len(outs)
     return pl.pallas_call(
@@ -545,6 +581,7 @@
         in_specs=[pl.BlockSpec(memory_space=where[c]) for c in spaces],
         out_specs=tuple(pl.BlockSpec(memory_space=where[c]) for c in out_spaces),
         scratch_shapes=[pltpu.VMEM(s, F32) if isinstance(s, tuple) else s for s in scratch],
+        input_output_aliases=aliases or {},
         compiler_params=pltpu.CompilerParams(vmem_limit_bytes=48 * 2**20),
         cost_estimate=pl.CostEstimate(flops=flops, bytes_accessed=4_000_000, transcendentals=0),
         name=name,
@@ -555,13 +592,14 @@
     axes = ("sec", "tile")
     devices = lax.axis_size("sec") * lax.axis_size("tile")
     levels, n = ocean_u.shape[0], tracers.shape[0]
-    dev = (lax.axis_index("sec") * lax.axis_size("tile") + lax.axis_index("tile")).astype(jnp.int32).reshape(1)
+    share = lax.axis_size("tile")
+    dev = (lax.axis_index("sec") * share + lax.axis_index("tile")).astype(jnp.int32).reshape(1)
     strip = levels // 2
     fields = n + 1
     ocean, tile = ocean_u.shape, (levels, LANES)
     wet_smem, kin_smem = pltpu.SMEM(wet_tiles.shape, jnp.int32), pltpu.SMEM(kinetic.shape, F32)
     inner, outer, u0, b0, t0, kinetic_v, facts = call(
-        pack_kernel,
+        functools.partial(pack_kernel, share),
         [
             ((strip + 2 * levels, LANES), F32),
             ((strip, LANES), F32),
@@ -581,36 +619,43 @@
     in_pairs = [(i, i ^ 1) for i in range(devices)]
     across = [(i, (i + 1) % devices if i % 2 else (i - 1) % devices) for i in range(devices)]
     inner = lax.ppermute(inner, axes, in_pairs)
+    shapes = [
+        ((OCEAN_DEV, *tile), F32),
+        ((OCEAN_DEV, *tile), F32),
+        ((n, WET_DEV, *tile), F32),
+        ((2, 2 * fields * 8, fields * 8), BF16),
+        ((n, *tile), F32),
+        (tile, F32),
+        (tile, F32),
+    ]
+    adv = [(n, WET_DEV, levels + 2 * PAD, LANES)]
+    *carried, outer = call(
+        functools.partial(own_kernel, 0),
+        [*shapes, (outer.shape, F32)],
+        adv,
+        (facts, kinetic_v, u0, b0, t0, outer),
+        "svvvvv",
+        flops=1_000_000_000,
+        name="own_tiles_early",
+    )
     outer = lax.ppermute(outer, axes, across)
-    own_u, own_b, own_t, kron, p_state, p_u, p_b = call(
-        own_kernel,
-        [
-            ((OCEAN_DEV, *tile), F32),
-            ((OCEAN_DEV, *tile), F32),
-            ((n, WET_DEV, *tile), BF16),
-            ((2, 2 * fields * 8, fields * 8), BF16),
-            ((fields, *tile), F32),
-            (tile, F32),
-            (tile, F32),
-        ],
-        [
-            (OCEAN_DEV, *tile),
-            (OCEAN_DEV, *tile),
-            (n, WET_DEV, *tile),
-            (n, WET_DEV, levels + 2 * PAD, LANES),
-        ],
-        (facts, kinetic_v, u0, b0, t0),
-        "svvvv",
+    carried = call(
+        functools.partial(own_kernel, 1),
+        shapes,
+        adv,
+        (facts, kinetic_v, u0, b0, t0, *carried),
+        "svvvv" + "v" * len(carried),
+        aliases={5 + i: i for i in range(len(carried))},
         flops=2_000_000_000,
         name="own_tiles",
     )
-    alone = [(fields, 1, *tile), (fields, 1, levels + 2 * PAD, LANES)]
-    x_t, x_u, x_b, p_state, p_u, p_b = call(
+    own_u, own_b, own_t, kron, p_state, p_u, p_b = carried
+    x_t, x_u, x_b, p_state, p_combo, p_u, p_b = call(
         x_kernel,
-        [((n, *tile), F32), (tile, F32), (tile, F32), ((fields, *tile), F32), (tile, F32), (tile, F32)],
-        alone,
-        (facts, kinetic_v, kron, u0, b0, t0, inner, p_state, p_u, p_b),
-        "s" + "v" * 9,
+        [((n, *tile), F32), (tile, F32), (tile, F32), ((n, *tile), F32), (tile, F32), (tile, F32), (tile, F32)],
+        [(n, 1, *tile), (n, 1, levels + 2 * PAD, LANES)],
+        (facts, kron, u0, b0, t0, inner, p_state, p_u, p_b),
+        "s" + "v" * 8,
         flops=1_000_000_000,
         name="x_tile",
     )
@@ -618,9 +663,16 @@
         call(
             last_kernel,
             [(ocean, F32), (ocean, F32), (tracers.shape, BF16)],
-            [*alone, ocean, ocean, pltpu.VMEM((n, WET_DEV, *tile), BF16), pltpu.SemaphoreType.DMA((5,))],
-            (facts, kron, outer, p_state, p_u, p_b, own_u, own_b, own_t, x_u, x_b, x_t),
-            "s" + "v" * 11,
+            [
+                (fields, 1, *tile),
+                (fields, 1, levels + 2 * PAD, LANES),
+                ocean,
+                ocean,
+                pltpu.VMEM((n, WET_DEV, *tile), BF16),
+                pltpu.SemaphoreType.DMA((2 + WET_DEV * (levels // 16),)),
+            ],
+            (facts, kinetic_v, kron, outer, p_state, p_combo, p_u, p_b, own_u, own_b, own_t, x_u, x_b, x_t),
+            "s" + "v" * 13,
             "hhh",
             flops=1_000_000_000,
             name="boundaries",

time: 17.9 us -> 16.8 us (0.939)
  Pallas kernels: 10.6 us -> 9.83 us
  starting transfers between devices: 6.44 us -> 6.08 us
    ppermute x1, starting transfers between devices: 6.44 us -> 3.04 us  [on_device(): outer = lax.ppermute(outer, axes, across)]
    ppermute x1, starting transfers between devices: 0.01 us -> 3.03 us  [on_device(): inner = lax.ppermute(inner, axes, in_pairs)]
    pallas_call x4 -> x5, Pallas kernels: 10.6 us -> 9.83 us  [call(): pl.pallas_call(kernel, out_shape=tuple((pltpu.SMEM(s, d) if c == 's' else...]
  transfers between devices with their start and end apart: 2 -> 2, of which waited for: 0 -> 0; matrix products, arithmetic and copies ran while one was open for 0% -> 0% of each run, Pallas kernels for 34% -> 32%
where the time goes in v3:
time: 16.8 us; the launch traced here: 16.6 us
  Pallas kernels  9.83 us (59%)
  starting transfers between devices  6.08 us (36%)
  between operations  0.68 us (4%)
    pallas_call x5, Pallas kernels, call(): pl.pallas_call(kernel, out_shape=tuple((pltpu.SMEM(s, d) if c == 's' else...  9.83 us
    ppermute x1, starting transfers between devices, on_device(): outer = lax.ppermute(outer, axes, across)  3.04 us
    ppermute x1, starting transfers between devices, on_device(): inner = lax.ppermute(inner, axes, in_pairs)  3.03 us
  transfers between devices with their start and end apart: 2, of which 0 were waited for; matrix products, arithmetic and copies ran while one was open for 0% of the time, Pallas kernels for 32%

profile of v3, /device:TPU:0, one launch (start us, length us, event | category | flops | bytes accessed | tf_op | source)
XLA Modules:
  0.0 16.6 jit_solution(1082680541746170258)
XLA Ops:
  0.6 1.6 %pack.1 = (f32[160,128]{1,0:T(8,128)S(1)}, f32[32,128]{1,0:T(8,128)S(1)}, f32[64,512]{1,0:T(8,128)S(1)}, f32[64,512]{1,0:T(8,128)S(1)}, bf16[17,64,384]{2,1,0:T(...) custom-call(s32[1]{0:T(128)} %bitcast.dev, s32[96]{0:T(128)} %wet_hbm.1, f32[17,17]{1,0:T(8,128)} %kin_hbm.1, ...), custom_call_target="tpu_custom_call" | custom-call | flops 10000000 | bytes 4000000 | tf_op jit(solution)/shard_map/pack/pallas_call | solution.py:576
  2.2 3.0 %collective-permute-start.1 = (f32[160,128]{1,0:T(8,128)S(1)}, f32[160,128]{1,0:T(8,128)S(1)}, u32[]{:S(2)}, u32[]{:S(2)}) collective-permute-start(f32[160,128]{1,0:T(8,128)S(1)} %get-tuple-element.47), channel_id=1, source_target_pairs={{0,1},{1,0},{2,3},{3,2},{4,5},{5,4},{6,7},{7,6},{8,9},{9,8},{10,11... | collective-permute-start | bytes 245768 | tf_op jit(solution)/shard_map/ppermute | solution.py:621
  5.2 0.6 %own_tiles_early.1 = (f32[4,64,128]{2,1,0:T(8,128)S(1)}, f32[4,64,128]{2,1,0:T(8,128)S(1)}, f32[17,3,64,128]{3,2,1,0:T(8,128)S(1)}, bf16[2,288,144]{2,1,0:T(8,12...) custom-call(s32[18]{0:T(128)S(4)} %get-tuple-element.32.facts, ...), custom_call_target="tpu_custom_call" | custom-call | flops 1000000000 | bytes 4000000 | tf_op jit(solution)/shard_map/own_tiles_early/pallas_call | solution.py:576
  5.8 3.0 %collective-permute-start = (f32[32,128]{1,0:T(8,128)S(1)}, f32[32,128]{1,0:T(8,128)S(1)}, u32[]{:S(2)}, u32[]{:S(2)}) collective-permute-start(f32[32,128]{1,0:T(8,128)S(1)} %get-tuple-element.46), channel_id=1, source_target_pairs={{0,31},{1,2},{2,1},{3,4},{4,3},{5,6},{6,5},{7,8},{8,7},{9,10},{10,... | collective-permute-start | bytes 49160 | tf_op jit(solution)/shard_map/ppermute | solution.py:641
  8.9 2.9 %own_tiles.1 = (f32[4,64,128]{2,1,0:T(8,128)S(1)}, f32[4,64,128]{2,1,0:T(8,128)S(1)}, f32[17,3,64,128]{3,2,1,0:T(8,128)S(1)}, bf16[2,288,144]{2,1,0:T(8,128)(2,1...) custom-call(s32[18]{0:T(128)S(4)} %get-tuple-element.32.facts, ...), custom_call_target="tpu_custom_call", output_to_operand_aliasing={{0}: (5, {}), {1}: (6, {}), {2}: (7, {}), {3}: (8, {}), {4}... | custom-call | flops 2000000000 | bytes 4000000 | tf_op jit(solution)/shard_map/own_tiles/pallas_call | solution.py:576
  11.8 0.0 collective-permute-done.1.inner
  11.8 1.7 %x_tile.1 = (f32[17,64,128]{2,1,0:T(8,128)S(1)}, f32[64,128]{1,0:T(8,128)S(1)}, f32[64,128]{1,0:T(8,128)S(1)}, f32[17,64,128]{2,1,0:T(8,128)S(1)}, f32[64,128]{1...) custom-call(s32[18]{0:T(128)S(4)} %get-tuple-element.32.facts, ...), custom_call_target="tpu_custom_call" | custom-call | flops 1000000000 | bytes 4000000 | tf_op jit(solution)/shard_map/x_tile/pallas_call | solution.py:576
  13.6 0.0 collective-permute-done.outer
  13.6 3.0 %boundaries.1 = (f32[64,512]{1,0:T(8,128)}, f32[64,512]{1,0:T(8,128)}, bf16[17,64,384]{2,1,0:T(8,128)(2,1)}) custom-call(s32[18]{0:T(128)S(4)} %get-tuple-element.32.facts, f32[17,17]{1,0:T(8,128)S(1)} %get-tuple-element.33.kin, bf16[2,288,144]{2,1,0:T(8,128)(2,1)S(1)} %get-tuple-element.45.kron, f32[32,128]{1,0:T(8,128)S(1)} %collective-permute-done.outer, ...), custom_call_target="tpu_custom_call" | custom-call | flops 1000000000 | bytes 4000000 | tf_op jit(solution)/shard_map/boundaries/pallas_call | solution.py:576
Async XLA Ops:
  2.2 9.6 %collective-permute-start.1 = (f32[160,128]{1,0:T(8,128)S(1)}, f32[160,128]{1,0:T(8,128)S(1)}, u32[]{:S(2)}, u32[]{:S(2)}) collective-permute-start(f32[160,128]{1,0:T(8,128)S(1)} %get-tuple-element.47), channel_id=1, source_target_pairs={{0,1},{1,0},{2,3},{3,2},{4,5},{5,4},{6,7},{7,6},{8,9},{9,8},{10,11... | collective-permute-start | bytes 245768 | tf_op jit(solution)/shard_map/ppermute | solution.py:621
  5.8 7.7 %collective-permute-start = (f32[32,128]{1,0:T(8,128)S(1)}, f32[32,128]{1,0:T(8,128)S(1)}, u32[]{:S(2)}, u32[]{:S(2)}) collective-permute-start(f32[32,128]{1,0:T(8,128)S(1)} %get-tuple-element.46), channel_id=1, source_target_pairs={{0,31},{1,2},{2,1},{3,4},{4,3},{5,6},{6,5},{7,8},{8,7},{9,10},{10,... | collective-permute-start | bytes 49160 | tf_op jit(solution)/shard_map/ppermute | solution.py:641

commit v4 on v3

--- a/solution.py
+++ b/solution.py
@@ -28,6 +28,7 @@
 GROWTH = 0.05
 THERMAL_GAIN = 0.1
 
+EARLY_STEPS = 1
 SEG = 40
 HALF = SEG // 2
 FIX = 8
@@ -289,10 +290,11 @@
 
 
 def own_kernel(part, facts, kin, u0, b0, tracers, *refs):
-    u, b, state, kron, p_state, p_u, p_b = refs[-9:-2] if part == 0 else refs[-8:-1]
+    u, b, state, kron, p_state, p_u, p_b = refs[-10:-3] if part == 0 else refs[-8:-1]
     adv = refs[-1]
     if part == 0:
-        refs[-2][...] = refs[0][...]
+        refs[-3][...] = refs[0][...]
+        refs[-2][...] = refs[1][...]
     f = read_facts(facts)
     levels = u0.shape[0]
     n = tracers.shape[0]
@@ -359,22 +361,33 @@
 
             mix_and_react(adv, s, kappa, warmth, light[s], kron.at[1], n, levels, emit)
 
-    early = f["early"] == 1
-    if part == 0:
-        pl.when(early)(start)
-    else:
-        pl.when(jnp.logical_not(early))(start)
-
+    def steps(begin, end):
         @pl.when(gives)
         def _():
-            pl.loop(0, STEPS)(lambda _: one_step(WET_DEV, 0, tile, joined))
+            pl.loop(begin, end)(lambda _: one_step(WET_DEV, 0, tile, joined))
 
         @pl.when(jnp.logical_not(gives))
         def _():
             odd = f["odd"]
             tiles = [jnp.where(odd == 1, tile[s + 1], tile[s]) for s in range(WET_DEV - 1)]
             pairs = [jnp.where(odd == 1, joined[1], joined[0])]
-            pl.loop(0, STEPS)(lambda _: one_step(WET_DEV - 1, odd, tiles, pairs))
+            pl.loop(begin, end)(lambda _: one_step(WET_DEV - 1, odd, tiles, pairs))
+
+    if part == 0:
+
+        @pl.when(f["early"] == 1)
+        def _():
+            start()
+            steps(0, EARLY_STEPS)
+
+    else:
+        pl.when(f["early"] == 0)(start)
+        steps(f["early"] * EARLY_STEPS, STEPS)
+
+
+def gate_kernel(strip, out, passed):
+    out[...] = strip[...]
+    passed[...] = strip[:8]
 
 
 def advance_alone(state, adv, u, b, heat, face_open, kron, n, levels, emit, combined):
@@ -583,7 +596,7 @@
         scratch_shapes=[pltpu.VMEM(s, F32) if isinstance(s, tuple) else s for s in scratch],
         input_output_aliases=aliases or {},
         compiler_params=pltpu.CompilerParams(vmem_limit_bytes=48 * 2**20),
-        cost_estimate=pl.CostEstimate(flops=flops, bytes_accessed=4_000_000, transcendentals=0),
+        cost_estimate=pl.CostEstimate(flops=flops, bytes_accessed=0, transcendentals=0),
         name=name,
     )(*(pltpu.with_memory_space_constraint(a, pltpu.HBM) if c == "h" else a for a, c in zip(args, spaces)))
 
@@ -618,7 +631,6 @@
     )
     in_pairs = [(i, i ^ 1) for i in range(devices)]
     across = [(i, (i + 1) % devices if i % 2 else (i - 1) % devices) for i in range(devices)]
-    inner = lax.ppermute(inner, axes, in_pairs)
     shapes = [
         ((OCEAN_DEV, *tile), F32),
         ((OCEAN_DEV, *tile), F32),
@@ -629,24 +641,34 @@
         (tile, F32),
     ]
     adv = [(n, WET_DEV, levels + 2 * PAD, LANES)]
-    *carried, outer = call(
+    *carried, inner, outer = call(
         functools.partial(own_kernel, 0),
-        [*shapes, (outer.shape, F32)],
+        [*shapes, (inner.shape, F32), (outer.shape, F32)],
         adv,
-        (facts, kinetic_v, u0, b0, t0, outer),
-        "svvvvv",
+        (facts, kinetic_v, u0, b0, t0, inner, outer),
+        "svvvvvv",
         flops=1_000_000_000,
         name="own_tiles_early",
+    )
+    inner = lax.ppermute(inner, axes, in_pairs)
+    outer, passed = call(
+        gate_kernel,
+        [(outer.shape, F32), ((8, LANES), F32)],
+        [],
+        (outer,),
+        "v",
+        flops=8_000_000_000,
+        name="outer_strip",
     )
     outer = lax.ppermute(outer, axes, across)
     carried = call(
         functools.partial(own_kernel, 1),
         shapes,
         adv,
-        (facts, kinetic_v, u0, b0, t0, *carried),
-        "svvvv" + "v" * len(carried),
+        (facts, kinetic_v, u0, b0, t0, *carried, passed),
+        "svvvv" + "v" * len(carried) + "v",
         aliases={5 + i: i for i in range(len(carried))},
-        flops=2_000_000_000,
+        flops=0,
         name="own_tiles",
     )
     own_u, own_b, own_t, kron, p_state, p_u, p_b = carried
@@ -656,7 +678,7 @@
         [(n, 1, *tile), (n, 1, levels + 2 * PAD, LANES)],
         (facts, kron, u0, b0, t0, inner, p_state, p_u, p_b),
         "s" + "v" * 8,
-        flops=1_000_000_000,
+        flops=0,
         name="x_tile",
     )
     return tuple(

time: 16.8 us -> 15.3 us (0.911)
  starting transfers between devices: 6.08 us -> 4.64 us
    ppermute x1, starting transfers between devices: 3.03 us -> 1.02 us  [on_device(): inner = lax.ppermute(inner, axes, in_pairs)]
    ppermute x1, starting transfers between devices: 3.04 us -> 3.63 us  [on_device(): outer = lax.ppermute(outer, axes, across)]
    pallas_call x5 -> x6, Pallas kernels: 9.83 us -> 9.8 us  [call(): pl.pallas_call(kernel, out_shape=tuple((pltpu.SMEM(s, d) if c == 's' else...]
  transfers between devices with their start and end apart: 2 -> 2, of which waited for: 0 -> 0; matrix products, arithmetic and copies ran while one was open for 0% -> 0% of each run, Pallas kernels for 32% -> 21%
where the time goes in v4:
time: 15.3 us; the launch traced here: 15.1 us
  Pallas kernels  9.8 us (64%)
  starting transfers between devices  4.64 us (30%)
  between operations  0.69 us (5%)
    pallas_call x6, Pallas kernels, call(): pl.pallas_call(kernel, out_shape=tuple((pltpu.SMEM(s, d) if c == 's' else...  9.8 us
    ppermute x1, starting transfers between devices, on_device(): outer = lax.ppermute(outer, axes, across)  3.63 us
    ppermute x1, starting transfers between devices, on_device(): inner = lax.ppermute(inner, axes, in_pairs)  1.02 us
  transfers between devices with their start and end apart: 2, of which 0 were waited for; matrix products, arithmetic and copies ran while one was open for 0% of the time, Pallas kernels for 21%

profile of v4, /device:TPU:0, one launch (start us, length us, event | category | flops | bytes accessed | tf_op | source)
XLA Modules:
  0.0 15.1 jit_solution(3380585547041607673)
XLA Ops:
  0.6 1.6 %pack.1 = (f32[160,128]{1,0:T(8,128)S(1)}, f32[32,128]{1,0:T(8,128)S(1)}, f32[64,512]{1,0:T(8,128)S(1)}, f32[64,512]{1,0:T(8,128)S(1)}, bf16[17,64,384]{2,1,0:T(...) custom-call(s32[1]{0:T(128)} %bitcast.dev, s32[96]{0:T(128)} %wet_hbm.1, f32[17,17]{1,0:T(8,128)} %kin_hbm.1, ...), custom_call_target="tpu_custom_call" | custom-call | flops 10000000 | tf_op jit(solution)/shard_map/pack/pallas_call | solution.py:589
  2.2 2.0 %own_tiles_early.1 = (f32[4,64,128]{2,1,0:T(8,128)S(1)}, f32[4,64,128]{2,1,0:T(8,128)S(1)}, f32[17,3,64,128]{3,2,1,0:T(8,128)S(1)}, bf16[2,288,144]{2,1,0:T(8,12...) custom-call(s32[18]{0:T(128)S(4)} %get-tuple-element.35.facts, ...), custom_call_target="tpu_custom_call" | custom-call | flops 1000000000 | tf_op jit(solution)/shard_map/own_tiles_early/pallas_call | solution.py:589
  4.3 1.0 %collective-permute-start.1 = (f32[160,128]{1,0:T(8,128)S(1)}, f32[160,128]{1,0:T(8,128)S(1)}, u32[]{:S(2)}, u32[]{:S(2)}) collective-permute-start(f32[160,128]{1,0:T(8,128)S(1)} %get-tuple-element.53), channel_id=1, source_target_pairs={{0,1},{1,0},{2,3},{3,2},{4,5},{5,4},{6,7},{7,6},{8,9},{9,8},{10,11... | collective-permute-start | bytes 245768 | tf_op jit(solution)/shard_map/ppermute | solution.py:653
  5.3 3.6 %collective-permute-start = (f32[32,128]{1,0:T(8,128)S(1)}, f32[32,128]{1,0:T(8,128)S(1)}, u32[]{:S(2)}, u32[]{:S(2)}) collective-permute-start(f32[32,128]{1,0:T(8,128)S(1)} %get-tuple-element.52), channel_id=1, source_target_pairs={{0,31},{1,2},{2,1},{3,4},{4,3},{5,6},{6,5},{7,8},{8,7},{9,10},{10,... | collective-permute-start | bytes 49160 | tf_op jit(solution)/shard_map/ppermute | solution.py:663
  8.9 1.5 %own_tiles.1 = (f32[4,64,128]{2,1,0:T(8,128)S(1)}, f32[4,64,128]{2,1,0:T(8,128)S(1)}, f32[17,3,64,128]{3,2,1,0:T(8,128)S(1)}, bf16[2,288,144]{2,1,0:T(8,128)(2,1...) custom-call(s32[18]{0:T(128)S(4)} %get-tuple-element.35.facts, ...), custom_call_target="tpu_custom_call", output_to_operand_aliasing={{0}: (5, {}), {1}: (6, {}), {2}: (7, {}), {3}: (8, {}), {4}... | custom-call | tf_op jit(solution)/shard_map/own_tiles/pallas_call | solution.py:589
  10.4 0.0 collective-permute-done.1.inner
  10.4 1.7 %x_tile.1 = (f32[17,64,128]{2,1,0:T(8,128)S(1)}, f32[64,128]{1,0:T(8,128)S(1)}, f32[64,128]{1,0:T(8,128)S(1)}, f32[17,64,128]{2,1,0:T(8,128)S(1)}, f32[64,128]{1...) custom-call(s32[18]{0:T(128)S(4)} %get-tuple-element.35.facts, ...), custom_call_target="tpu_custom_call" | custom-call | tf_op jit(solution)/shard_map/x_tile/pallas_call | solution.py:589
  12.1 0.0 collective-permute-done.outer
  12.1 3.0 %boundaries.1 = (f32[64,512]{1,0:T(8,128)}, f32[64,512]{1,0:T(8,128)}, bf16[17,64,384]{2,1,0:T(8,128)(2,1)}) custom-call(s32[18]{0:T(128)S(4)} %get-tuple-element.35.facts, f32[17,17]{1,0:T(8,128)S(1)} %get-tuple-element.36.kin, bf16[2,288,144]{2,1,0:T(8,128)(2,1)S(1)} %get-tuple-element.51.kron, f32[32,128]{1,0:T(8,128)S(1)} %collective-permute-done.outer, ...), custom_call_target="tpu_custom_call" | custom-call | flops 1000000000 | tf_op jit(solution)/shard_map/boundaries/pallas_call | solution.py:589
  (1 shorter events, 0.0 us)
Async XLA Ops:
  4.3 6.1 %collective-permute-start.1 = (f32[160,128]{1,0:T(8,128)S(1)}, f32[160,128]{1,0:T(8,128)S(1)}, u32[]{:S(2)}, u32[]{:S(2)}) collective-permute-start(f32[160,128]{1,0:T(8,128)S(1)} %get-tuple-element.53), channel_id=1, source_target_pairs={{0,1},{1,0},{2,3},{3,2},{4,5},{5,4},{6,7},{7,6},{8,9},{9,8},{10,11... | collective-permute-start | bytes 245768 | tf_op jit(solution)/shard_map/ppermute | solution.py:653
  5.3 6.8 %collective-permute-start = (f32[32,128]{1,0:T(8,128)S(1)}, f32[32,128]{1,0:T(8,128)S(1)}, u32[]{:S(2)}, u32[]{:S(2)}) collective-permute-start(f32[32,128]{1,0:T(8,128)S(1)} %get-tuple-element.52), channel_id=1, source_target_pairs={{0,31},{1,2},{2,1},{3,4},{4,3},{5,6},{6,5},{7,8},{8,7},{9,10},{10,... | collective-permute-start | bytes 49160 | tf_op jit(solution)/shard_map/ppermute | solution.py:663

commit v5 on v4

--- a/solution.py
+++ b/solution.py
@@ -29,9 +29,11 @@
 THERMAL_GAIN = 0.1
 
 EARLY_STEPS = 1
-SEG = 40
+GROUPS = 4
+GROUP = LANES // GROUPS
+SEG = 10
 HALF = SEG // 2
-FIX = 8
+FIX_FIRST, FIX_LAST = 3, 2
 PAD = 8
 F32, BF16 = jnp.float32, jnp.bfloat16
 
@@ -105,42 +107,65 @@
     return pltpu.roll(x, shift, x.ndim - 1)
 
 
-def upper(x):
-    row = lax.broadcasted_iota(jnp.int32, x.shape, 0)
-    return jnp.where(row == 0, x, pltpu.roll(x, 1, 0))
-
-
-def lower(x):
+def row_of(x):
+    return lax.broadcasted_iota(jnp.int32, x.shape, 0)
+
+
+def upper(x, groups=1):
+    row, rolled = row_of(x), pltpu.roll(x, 1, 0)
+    if groups == 1:
+        return jnp.where(row == 0, x, rolled)
+    other = jnp.where(lane_of(x.shape[0]) < GROUP, x, lane_roll(rolled, GROUP))
+    return jnp.where(row == 0, other, rolled)
+
+
+def lower(x, groups=1):
     n = x.shape[0]
-    row = lax.broadcasted_iota(jnp.int32, x.shape, 0)
-    return jnp.where(row == n - 1, x, pltpu.roll(x, n - 1, 0))
-
-
-def absorbed_light(pigment):
+    row, rolled = row_of(x), pltpu.roll(x, n - 1, 0)
+    if groups == 1:
+        return jnp.where(row == n - 1, x, rolled)
+    other = jnp.where(lane_of(n) >= LANES - GROUP, x, lane_roll(rolled, LANES - GROUP))
+    return jnp.where(row == n - 1, other, rolled)
+
+
+def at_top(x, groups):
+    top = row_of(x) == 0
+    return top if groups == 1 else jnp.logical_and(top, lane_of(x.shape[0]) < GROUP)
+
+
+def at_bottom(x, groups):
+    bottom = row_of(x) == x.shape[0] - 1
+    return bottom if groups == 1 else jnp.logical_and(bottom, lane_of(x.shape[0]) >= LANES - GROUP)
+
+
+def absorbed_light(pigment, groups=1):
     att = WATER_ATT + PIGMENT_ATT * pigment * pigment
     depth = att
     rows = att.shape[0]
-    row = lax.broadcasted_iota(jnp.int32, att.shape, 0)
+    row = row_of(att)
     step = 1
     while step < rows:
         depth = depth + jnp.where(row >= step, pltpu.roll(depth, step, 0), 0.0)
         step *= 2
+    if groups > 1:
+        total = jnp.broadcast_to(depth[rows - 1 :], depth.shape)
+        lane = lane_of(rows)
+        for g in range(1, groups):
+            depth = depth + jnp.where(lane >= GROUP * g, lane_roll(total, GROUP * g), 0.0)
     return SURFACE_LIGHT * (jnp.exp(att - depth) - jnp.exp(-depth))
 
 
-def new_velocity(u, u_left, u_right, b, b_right):
+def new_velocity(u, u_left, u_right, b, b_right, groups=1):
     horiz = u_left + u_right - 2.0 * u
-    vert = upper(u) + lower(u) - 2.0 * u
+    vert = upper(u, groups) + lower(u, groups) - 2.0 * u
     return u + DT_OCEAN * (HORIZ_VISC * horiz + VERT_VISC * vert - PRESSURE * (b_right - b))
 
 
-def diffusivity(u, b):
-    rows = u.shape[0]
-    row = lax.broadcasted_iota(jnp.int32, u.shape, 0)
-    shear = u - lower(u)
-    strat = b - lower(b)
+def diffusivity(u, b, groups=1):
+    shear = u - lower(u, groups)
+    strat = b - lower(b, groups)
     kappa = KAPPA_BASE + KAPPA_SPAN * (1.0 / (1.0 + jnp.exp(-4.0 * (shear * shear - strat))))
-    return jnp.where(row == rows - 1, 0.0, kappa)
+    return jnp.where(at_bottom(kappa, groups), 0.0, kappa)
 
 
 def face_parts(u, face_open):
@@ -148,7 +173,7 @@
     return jnp.maximum(w, 0.0), jnp.minimum(w, 0.0)
 
 
-def advect(state, adv, t, src, left, right, coeffs, fields, levels):
+def advect(state, adv, t, src, left, right, coeffs, fields, levels, groups=1):
     centre, from_left, from_right = coeffs
     chunk = 16
     lane = lane_of(chunk)
@@ -160,18 +185,23 @@
                 to_left = jnp.where(lane == 0, state[f, right, s, :], here)
             if left is not None:
                 to_right = jnp.where(lane == LANES - 1, state[f, left, s, :], here)
-            adv[f, t, PAD + r : PAD + r + chunk, :] = (
+            new = (
                 here * centre[s] + lane_roll(to_left, LANES - 1) * from_right[s] + lane_roll(to_right, 1) * from_left[s]
             )
-
-
-def mix_and_react(adv, t, kappa, warmth, light, kron, fields, levels, emit):
+            adv[f, t, PAD + r : PAD + r + chunk, :] = new
+            if groups > 1:
+                assert levels == chunk
+                adv[f, t, :PAD, :] = lane_roll(new[chunk - PAD :], GROUP)
+                adv[f, t, PAD + chunk :, :] = lane_roll(new[:PAD], LANES - GROUP)
+
+
+def mix_and_react(adv, t, kappa, warmth, light, kron, fields, levels, emit, groups=1):
     chunk = 16
-    above = jnp.where(lax.broadcasted_iota(jnp.int32, kappa.shape, 0) == 0, 0.0, pltpu.roll(kappa, 1, 0))
+    above = jnp.where(at_top(kappa, groups), 0.0, upper(kappa, groups))
     stay = 1.0 - DT_MIX * (kappa + above)
-    rows = (fields + (18 - fields)) * 8
-    k_hi = kron[:rows, :]
-    k_both = kron[...]
+    rows = kron.shape[1]
+    n = rows // 8 - 1
+    k_hi, k_both = kron[:rows, :], kron[...]
     for r in range(0, levels, chunk):
         s = slice(r, r + chunk)
         at = PAD + r
@@ -181,10 +211,8 @@
         mixed = here * stay[s] + (DT_MIX * kappa[s]) * down + (DT_MIX * above[s]) * up
         halves = []
         for h in range(2):
-            part = mixed[:, 8 * h : 8 * h + 8, :].reshape(fields * 8, LANES)
-            if fields < 18:
-                part = jnp.concatenate([part, jnp.zeros(((18 - fields) * 8, LANES), F32)], axis=0)
-            halves.append(part)
+            part = mixed[:n, 8 * h : 8 * h + 8, :].reshape(n * 8, LANES)
+            halves.append(jnp.concatenate([part, jnp.zeros((8, LANES), F32)], axis=0))
         wide = jnp.concatenate(halves, axis=1)
         hi = wide.astype(BF16)
         lo = (wide - hi.astype(F32)).astype(BF16)
@@ -193,11 +221,11 @@
         drift = by_hi[:rows] + (by_hi[rows:] + by_lo)
         out = []
         for h in range(2):
-            d = drift[:, LANES * h : LANES * h + LANES].reshape(18, 8, LANES)[:fields]
+            d = drift[:, LANES * h : LANES * h + LANES].reshape(n + 1, 8, LANES)
+            part = mixed[:, 8 * h : 8 * h + 8, :]
             sh = slice(r + 8 * h, r + 8 * h + 8)
-            new = mixed[:, 8 * h : 8 * h + 8, :] + warmth[sh] * d
-            first = new[:1] + GROWTH * light[sh][None]
-            out.append(jnp.concatenate([first, new[1:]], axis=0))
+            first = part[:1] + warmth[sh] * (d[:1] if fields == n else part[n:]) + GROWTH * light[sh][None]
+            out.append(jnp.concatenate([first, part[1:n] + warmth[sh] * d[1:n]], axis=0))
         emit(r, jnp.concatenate(out, axis=1))
 
 
@@ -259,29 +287,49 @@
     inner[half + levels :] = jnp.where(gives, tile_of(b, f["x_tile"]), x_combo)
 
 
+def near_half(f, rows):
+    lane = lane_of(rows)
+    return jnp.where(f["odd"] == 1, LANES - 1 - lane, lane) < LANES // 2
+
+
 def patch_masks(f, rows):
-    lane = lane_of(rows)
-    near = jnp.where(f["odd"] == 1, LANES - 1 - lane, lane) < LANES // 2
-    in_1 = jnp.logical_and(lane >= HALF, lane < HALF + SEG)
-    in_2 = jnp.logical_and(lane >= HALF + SEG, lane < HALF + 2 * SEG)
-    return near, in_1, in_2
+    lane = jnp.bitwise_and(lane_of(rows), GROUP - 1)
+    in_1 = jnp.logical_and(lane >= SEG, lane < 2 * SEG)
+    in_2 = lane >= 2 * SEG
+    within = lane - jnp.where(in_2, 2 * SEG, jnp.where(in_1, SEG, 0))
+    near = jnp.where(f["odd"] == 1, SEG - 1 - within, within) >= HALF
+    return near, in_1, in_2, within
+
+
+def fold(x, seg):
+    rows = x.shape[0] // GROUPS
+    group = lane_of(rows) // GROUP
+    out = None
+    for g in range(GROUPS):
+        part = lane_roll(x[rows * g : rows * (g + 1)], GROUP * g + SEG * seg + HALF)
+        out = part if out is None else jnp.where(group == g, part, out)
+    return out
+
+
+def unfold(patch, seg, g):
+    return lane_roll(patch, LANES - (GROUP * g + SEG * seg + HALF))
 
 
 def expand_kinetics(kin, kron):
     n = kin.shape[0]
-    rows = (n + 1) * 8
+    rows = kron.shape[1]
     to_rows = lax.broadcasted_iota(jnp.int32, (rows, n), 0) // 8 == lax.broadcasted_iota(jnp.int32, (rows, n), 1)
     to_cols = lax.broadcasted_iota(jnp.int32, (n, rows), 1) // 8 == lax.broadcasted_iota(jnp.int32, (n, rows), 0)
-    tall = jnp.dot(to_rows.astype(F32), kin[...], precision=lax.Precision.HIGHEST, preferred_element_type=F32)
-    full = jnp.dot(tall, to_cols.astype(F32), precision=lax.Precision.HIGHEST, preferred_element_type=F32)
+    to_rows, to_cols = (jnp.where(m, 1.0, 0.0).astype(BF16) for m in (to_rows, to_cols))
     row = lax.broadcasted_iota(jnp.int32, (rows, rows), 0)
     col = lax.broadcasted_iota(jnp.int32, (rows, rows), 1)
-    full = jnp.where(lax.rem(row, 8) == lax.rem(col, 8), full, 0.0)
-    with_combo = jnp.where(row < 8, jnp.where(col - 8 * n == row, 1.0, 0.0), full)
-    for i, m in enumerate((with_combo, full)):
-        hi = m.astype(BF16)
-        kron[i, :rows, :] = hi
-        kron[i, rows:, :] = (m - hi.astype(F32)).astype(BF16)
+    same = jnp.bitwise_and(row, 7) == jnp.bitwise_and(col, 7)
+    hi = kin[...].astype(BF16)
+    lo = (kin[...] - hi.astype(F32)).astype(BF16)
+    for i, part in enumerate((hi, lo)):
+        tall = jnp.dot(to_rows, part, preferred_element_type=F32).astype(BF16)
+        full = jnp.dot(tall, to_cols, preferred_element_type=F32)
+        kron[rows * i : rows * (i + 1), :] = jnp.where(same, full, 0.0).astype(BF16)
 
 
 def start_tile(state, adv, t, fields, levels):
@@ -311,11 +359,12 @@
         for s in range(WET_DEV):
             state[:, s] = tracers[:, :, LANES * s : LANES * (s + 1)].astype(F32)
 
-        near, in_1, in_2 = patch_masks(f, levels)
+        _, in_1, in_2, _ = patch_masks(f, levels // GROUPS)
+        near = near_half(f, levels)
 
         def lay(own, beside, x):
-            seg1 = lane_roll(jnp.where(near, x, beside), SEG)
-            return jnp.where(in_1, seg1, jnp.where(in_2, lane_roll(x, 2 * SEG), own))
+            seg1 = fold(jnp.where(near, x, beside), 1)
+            return jnp.where(in_1, seg1, jnp.where(in_2, fold(x, 2), fold(own, 0)))
 
         for p, field in ((p_u, u), (p_b, b)):
             p[...] = lay(field[f["outer_tile"]], field[f["beside_tile"]], field[f["x_tile"]])
@@ -359,7 +408,7 @@
             def emit(r, values, s=s):
                 state[:, first + s, r : r + 16, :] = values
 
-            mix_and_react(adv, s, kappa, warmth, light[s], kron.at[1], n, levels, emit)
+            mix_and_react(adv, s, kappa, warmth, light[s], kron, n, levels, emit)
 
     def steps(begin, end):
         @pl.when(gives)
@@ -390,32 +439,32 @@
     passed[...] = strip[:8]
 
 
-def advance_alone(state, adv, u, b, heat, face_open, kron, n, levels, emit, combined):
+def advance_alone(state, adv, u, b, heat, face_open, kron, n, levels, emit, combined, groups=1):
     for step in range(STEPS):
         last = step == STEPS - 1
-        light = absorbed_light(state[0, 0])
+        light = absorbed_light(state[0, 0], groups)
         b = b + HEATING * heat * light
-        u = new_velocity(u, lane_roll(u, 1), lane_roll(u, LANES - 1), b, lane_roll(b, LANES - 1))
+        u = new_velocity(u, lane_roll(u, 1), lane_roll(u, LANES - 1), b, lane_roll(b, LANES - 1), groups)
         if last:
             emit(None, (u, b))
         by_field = combined and not last
         count = n + 1 if by_field else n
         pos, neg = face_parts(u, face_open)
         pos_left, neg_left = lane_roll(pos, 1), lane_roll(neg, 1)
-        advect(state, adv, 0, 0, None, None, (1.0 - pos + neg_left, pos_left, -neg), count, levels)
-        kappa = diffusivity(u, b)
+        advect(state, adv, 0, 0, None, None, (1.0 - pos + neg_left, pos_left, -neg), count, levels, groups)
+        kappa = diffusivity(u, b, groups)
         warmth = KINETIC_DELTA * jnp.exp(THERMAL_GAIN * b)
 
         def put(r, values):
-            state[:n, 0, r : r + 16, :] = values[:n]
-
-        mix_and_react(adv, 0, kappa, warmth, light, kron.at[0 if by_field else 1], count, levels, emit if last else put)
-
-
-def from_strip(ref, half, shift):
-    return jnp.concatenate(
-        [lane_roll(ref[:half], lax.rem(shift + 3 * LANES - 64 * h, LANES)) for h in range(2)], axis=0
-    )
+            state[:n, 0, r : r + 16, :] = values
+
+        mix_and_react(adv, 0, kappa, warmth, light, kron, count, levels, emit if last else put, groups)
+
+
+def from_strip(ref, rows, at, seg):
+    shift = SEG * seg + HALF - at + 2 * LANES
+    parts = [lane_roll(ref[rows * q : rows * (q + 1)], lax.rem(shift + GROUP * q, LANES)) for q in range(2)]
+    return jnp.where(jnp.bitwise_and(lane_of(rows), GROUP) == 0, parts[0], parts[1])
 
 
 def x_kernel(
@@ -432,24 +481,25 @@
     tile2 = inner[half + levels :]
     start_tile(state, adv, 0, n, levels)
 
-    near, in_1, in_2 = patch_masks(f, levels)
-    x_in_1 = jnp.logical_and(in_1, lane_roll(jnp.where(near, 1, 0), SEG) == 1)
-    beyond = jnp.logical_and(in_2, lane_roll(jnp.where(near, 1, 0), 2 * SEG) == 1)
+    rows = levels // GROUPS
+    near, in_1, in_2, _ = patch_masks(f, rows)
+    x_in_1 = jnp.logical_and(in_1, near)
+    beyond = jnp.logical_and(in_2, near)
     face_open = jnp.where(lane == LANES - 1, 0.0, 1.0)
 
     def x_whole(patch, x):
-        patch = jnp.where(x_in_1, lane_roll(x, SEG), patch)
-        return jnp.where(in_2, lane_roll(x, 2 * SEG), patch)
+        patch = jnp.where(x_in_1, fold(x, 1), patch)
+        return jnp.where(in_2, fold(x, 2), patch)
 
     def with_far(patch, at):
-        return jnp.where(beyond, from_strip(inner, half, 2 * SEG - at), patch)
+        return jnp.where(beyond, from_strip(inner, rows, at, 2), patch)
 
     @pl.when(gives)
     def _():
         p_u[...] = with_far(pre_u[...], U_AT)
         p_b[...] = with_far(pre_b[...], B_AT)
         for j in range(1, n):
-            p_state[j] = jnp.where(x_in_1, from_strip(inner, half, SEG - 2 * j), pre_state[j])
+            p_state[j] = jnp.where(x_in_1, from_strip(inner, rows, 2 * j, 1), pre_state[j])
         p_state[0] = with_far(x_whole(pre_state[0], tile1), T0_AT)
         p_combo[...] = with_far(x_whole(pre_state[0], tile2), COMBO_AT)
         state[0, 0], state[1, 0] = tile1, tile2
@@ -496,44 +546,37 @@
     u_out, b_out, t_out, state, adv, whole_u, whole_b, merged, sems,
 ):
     f = read_facts(facts)
-    levels = p_u.shape[0]
-    half = levels // 2
+    rows = p_u.shape[0]
+    levels = rows * GROUPS
     n = own_t.shape[0]
     gives, odd = f["gives"] == 1, f["odd"] == 1
-    lane = lane_of(levels)
-    near, in_1, in_2 = patch_masks(f, levels)
+    near, in_1, in_2, within = patch_masks(f, rows)
     halo = jnp.logical_not(jnp.logical_or(near, jnp.logical_or(in_1, in_2)))
-    start_tile(state, adv, 0, n + 1, levels)
-    u = jnp.where(halo, from_strip(outer, half, -U_AT), p_u[...])
-    b = jnp.where(halo, from_strip(outer, half, -B_AT), p_b[...])
+    u = jnp.where(halo, from_strip(outer, rows, U_AT, 0), p_u[...])
+    b = jnp.where(halo, from_strip(outer, rows, B_AT, 0), p_b[...])
     combo = None
     for j in range(n):
-        x = jnp.where(halo, from_strip(outer, half, -2 * j), pre_state[j])
+        x = jnp.where(halo, from_strip(outer, rows, 2 * j, 0), pre_state[j])
         state[j, 0] = x
         combo = kin[0:1, j : j + 1] * x if combo is None else combo + kin[0:1, j : j + 1] * x
-    x_in_1 = jnp.logical_and(in_1, lane_roll(jnp.where(near, 1, 0), SEG) == 1)
+    x_in_1 = jnp.logical_and(in_1, near)
     handed = jnp.logical_and(gives, jnp.logical_or(x_in_1, in_2))
     state[n, 0] = jnp.where(handed, p_combo[...], combo)
 
-    def sides(here, there, boundary_at):
-        return lane_roll(jnp.where(near, here.astype(F32), there.astype(F32)), boundary_at)
+    def sides(here, there):
+        return jnp.where(near, here.astype(F32), there.astype(F32))
 
     one = jnp.int32(1)
     heat = jnp.where(
         in_1,
-        sides(one, f["beside_wet"], SEG),
-        jnp.where(in_2, sides(f["beyond_wet"], one, 2 * SEG), sides(f["outer_own_wet"], f["outer_far_wet"], 0)),
+        sides(one, f["beside_wet"]),
+        jnp.where(in_2, sides(f["beyond_wet"], one), sides(f["outer_own_wet"], f["outer_far_wet"])),
     )
     outer_open = (f["outer_own_wet"] * f["outer_far_wet"]).astype(F32)
-    face_open = jnp.where(
-        lane == LANES - 1,
-        outer_open,
-        jnp.where(
-            lane == SEG - 1,
-            f["beside_wet"].astype(F32),
-            jnp.where(lane == 2 * SEG - 1, f["beyond_wet"].astype(F32), 1.0),
-        ),
-    )
+    boundary_open = jnp.where(
+        in_1, f["beside_wet"].astype(F32), jnp.where(in_2, f["beyond_wet"].astype(F32), outer_open)
+    )
+    face_open = jnp.where(within == HALF - 1, boundary_open, 1.0)
     copies = []
 
     def send(src, dst):
@@ -543,40 +586,41 @@
     def at(index):
         return pl.ds(pl.multiple_of(index * LANES, LANES), LANES)
 
-    def edge(rows, at_left):
-        here = lane_of(rows)
-        return jnp.where(at_left, here, LANES - 1 - here) < FIX
-
-    left, right = edge(16, jnp.logical_not(odd)), edge(16, odd)
+    def edge(count, at_left):
+        lane = lane_of(count)
+        return jnp.where(at_left, jnp.where(lane < FIX_FIRST, 1, 0), jnp.where(lane >= LANES - FIX_LAST, 1, 0)) == 1
+
+    left, right = edge(rows, jnp.logical_not(odd)), edge(rows, odd)
     outer_fix = jnp.logical_and(left, f["outer_own_wet"] == 1)
     beside_fix = jnp.logical_and(right, f["beside_wet"] == 1)
     third = jnp.where(gives, 1, f["x_slot"])
 
     def emit(r, values):
         if r is None:
-            for i, (patch, own, x, whole, out) in enumerate(
-                ((values[0], own_u, x_u, whole_u, u_out), (values[1], own_b, x_b, whole_b, b_out))
+            for patch, own, x_ref, whole, out in (
+                (values[0], own_u, x_u, whole_u, u_out),
+                (values[1], own_b, x_b, whole_b, b_out),
             ):
-                seg1, seg2 = lane_roll(patch, LANES - SEG), lane_roll(patch, LANES - 2 * SEG)
-                left_w, right_w = edge(levels, jnp.logical_not(odd)), edge(levels, odd)
                 for t in range(OCEAN_DEV):
                     whole[:, LANES * t : LANES * (t + 1)] = own[t]
-
-                x = jnp.where(left_w, seg1, jnp.where(right_w, seg2, x[...]))
-                x = jnp.where(gives, x, own[f["x_tile"]])
-                whole[:, at(f["x_tile"])] = x
-                whole[:, at(f["outer_tile"])] = jnp.where(left_w, patch, own[f["outer_tile"]])
-                whole[:, at(f["beside_tile"])] = jnp.where(right_w, seg1, own[f["beside_tile"]])
+                for g in range(GROUPS):
+                    s = slice(rows * g, rows * (g + 1))
+                    seg0, seg1, seg2 = (unfold(patch, seg, g) for seg in range(3))
+                    x = jnp.where(left, seg1, jnp.where(right, seg2, x_ref[s]))
+                    whole[s, at(f["x_tile"])] = jnp.where(gives, x, own[f["x_tile"], s, :])
+                    whole[s, at(f["outer_tile"])] = jnp.where(left, seg0, own[f["outer_tile"], s, :])
+                    whole[s, at(f["beside_tile"])] = jnp.where(right, seg1, own[f["beside_tile"], s, :])
                 send(whole, out)
             return
-        s = slice(r, r + 16)
-        seg1, seg2 = lane_roll(values, LANES - SEG), lane_roll(values, LANES - 2 * SEG)
-        merged[:, 0, s, :] = jnp.where(outer_fix, values, own_t[:, f["outer_slot"], s, :]).astype(BF16)
-        merged[:, 1, s, :] = jnp.where(beside_fix, seg1, own_t[:, f["beside_slot"], s, :]).astype(BF16)
-        x = jnp.where(left, seg1, jnp.where(right, seg2, x_t[:, s, :]))
-        merged[:, 2, s, :] = jnp.where(gives, own_t[:, 1, s, :], x).astype(BF16)
-
-    advance_alone(state, adv, u, b, heat, face_open, kron, n, levels, emit, True)
+        for g in range(GROUPS):
+            s = slice(rows * g, rows * (g + 1))
+            seg0, seg1, seg2 = (unfold(values, seg, g) for seg in range(3))
+            merged[:, 0, s, :] = jnp.where(outer_fix, seg0, own_t[:, f["outer_slot"], s, :]).astype(BF16)
+            merged[:, 1, s, :] = jnp.where(beside_fix, seg1, own_t[:, f["beside_slot"], s, :]).astype(BF16)
+            x = jnp.where(left, seg1, jnp.where(right, seg2, x_t[:, s, :]))
+            merged[:, 2, s, :] = jnp.where(gives, own_t[:, 1, s, :], x).astype(BF16)
+
+    advance_alone(state, adv, u, b, heat, face_open, kron, n, rows, emit, True, GROUPS)
     for i, slot in enumerate((f["outer_slot"], f["beside_slot"], third)):
         send(merged.at[:, i], t_out.at[:, :, at(slot)])
     for c in copies:
@@ -609,7 +653,7 @@
     dev = (lax.axis_index("sec") * share + lax.axis_index("tile")).astype(jnp.int32).reshape(1)
     strip = levels // 2
     fields = n + 1
-    ocean, tile = ocean_u.shape, (levels, LANES)
+    ocean, tile, patch = ocean_u.shape, (levels, LANES), (levels // GROUPS, LANES)
     wet_smem, kin_smem = pltpu.SMEM(wet_tiles.shape, jnp.int32), pltpu.SMEM(kinetic.shape, F32)
     inner, outer, u0, b0, t0, kinetic_v, facts = call(
         functools.partial(pack_kernel, share),
@@ -635,10 +679,10 @@
         ((OCEAN_DEV, *tile), F32),
         ((OCEAN_DEV, *tile), F32),
         ((n, WET_DEV, *tile), F32),
-        ((2, 2 * fields * 8, fields * 8), BF16),
-        ((n, *tile), F32),
-        (tile, F32),
-        (tile, F32),
+        ((2 * fields * 8, fields * 8), BF16),
+        ((n, *patch), F32),
+        (patch, F32),
+        (patch, F32),
     ]
     adv = [(n, WET_DEV, levels + 2 * PAD, LANES)]
     *carried, inner, outer = call(
@@ -674,7 +718,7 @@
     own_u, own_b, own_t, kron, p_state, p_u, p_b = carried
     x_t, x_u, x_b, p_state, p_combo, p_u, p_b = call(
         x_kernel,
-        [((n, *tile), F32), (tile, F32), (tile, F32), ((n, *tile), F32), (tile, F32), (tile, F32), (tile, F32)],
+        [((n, *tile), F32), (tile, F32), (tile, F32), ((n, *patch), F32), (patch, F32), (patch, F32), (patch, F32)],
         [(n, 1, *tile), (n, 1, levels + 2 * PAD, LANES)],
         (facts, kron, u0, b0, t0, inner, p_state, p_u, p_b),
         "s" + "v" * 8,
@@ -686,8 +730,8 @@
             last_kernel,
             [(ocean, F32), (ocean, F32), (tracers.shape, BF16)],
             [
-                (fields, 1, *tile),
-                (fields, 1, levels + 2 * PAD, LANES),
+                (fields, 1, *patch),
+                (fields, 1, levels // GROUPS + 2 * PAD, LANES),
                 ocean,
                 ocean,
                 pltpu.VMEM((n, WET_DEV, *tile), BF16),

time: 15.3 us -> 14.8 us (0.967)
  starting transfers between devices: 4.64 us -> 3.93 us
  waiting for transfers between devices: 0.01 us -> 0.6 us
  Pallas kernels: 9.8 us -> 9.42 us
    ppermute x1, starting transfers between devices: 1.02 us -> 0.3 us  [on_device(): inner = lax.ppermute(inner, axes, in_pairs)]
    ppermute x1, waiting for transfers between devices: 0.01 us -> 0.6 us  [on_device(): outer = lax.ppermute(outer, axes, across)]
    pallas_call x6, Pallas kernels: 9.8 us -> 9.42 us  [call(): pl.pallas_call(kernel, out_shape=tuple((pltpu.SMEM(s, d) if c == 's' else...]
  transfers between devices with their start and end apart: 2 -> 2, of which waited for: 0 -> 1; matrix products, arithmetic and copies ran while one was open for 0% -> 0% of each run, Pallas kernels for 21% -> 17%
where the time goes in v5:
time: 14.8 us; the launch traced here: 14.6 us
  Pallas kernels  9.42 us (64%)
  starting transfers between devices  3.93 us (27%)
  between operations  0.68 us (5%)
  waiting for transfers between devices  0.6 us (4%)
    pallas_call x6, Pallas kernels, call(): pl.pallas_call(kernel, out_shape=tuple((pltpu.SMEM(s, d) if c == 's' else...  9.42 us
    ppermute x1, starting transfers between devices, on_device(): outer = lax.ppermute(outer, axes, across)  3.63 us
    ppermute x1, waiting for transfers between devices, on_device(): outer = lax.ppermute(outer, axes, across)  0.6 us
    ppermute x1, starting transfers between devices, on_device(): inner = lax.ppermute(inner, axes, in_pairs)  0.3 us
  transfers between devices with their start and end apart: 2, of which 1 were waited for; matrix products, arithmetic and copies ran while one was open for 0% of the time, Pallas kernels for 17%

profile of v5, /device:TPU:0, one launch (start us, length us, event | category | flops | bytes accessed | tf_op | source)
XLA Modules:
  0.0 14.6 jit_solution(2222817614430156249)
XLA Ops:
  0.6 1.6 %pack.1 = (f32[160,128]{1,0:T(8,128)S(1)}, f32[32,128]{1,0:T(8,128)S(1)}, f32[64,512]{1,0:T(8,128)S(1)}, f32[64,512]{1,0:T(8,128)S(1)}, bf16[17,64,384]{2,1,0:T(...) custom-call(s32[1]{0:T(128)} %bitcast.dev, s32[96]{0:T(128)} %wet_hbm.1, f32[17,17]{1,0:T(8,128)} %kin_hbm.1, ...), custom_call_target="tpu_custom_call" | custom-call | flops 10000000 | tf_op jit(solution)/shard_map/pack/pallas_call | solution.py:633
  2.2 2.8 %own_tiles_early.1 = (f32[4,64,128]{2,1,0:T(8,128)S(1)}, f32[4,64,128]{2,1,0:T(8,128)S(1)}, f32[17,3,64,128]{3,2,1,0:T(8,128)S(1)}, bf16[288,144]{1,0:T(8,128)(2...) custom-call(s32[18]{0:T(128)S(4)} %get-tuple-element.35.facts, ...), custom_call_target="tpu_custom_call" | custom-call | flops 1000000000 | tf_op jit(solution)/shard_map/own_tiles_early/pallas_call | solution.py:633
  5.0 0.3 %collective-permute-start.1 = (f32[160,128]{1,0:T(8,128)S(1)}, f32[160,128]{1,0:T(8,128)S(1)}, u32[]{:S(2)}, u32[]{:S(2)}) collective-permute-start(f32[160,128]{1,0:T(8,128)S(1)} %get-tuple-element.53), channel_id=1, source_target_pairs={{0,1},{1,0},{2,3},{3,2},{4,5},{5,4},{6,7},{7,6},{8,9},{9,8},{10,11... | collective-permute-start | bytes 245768 | tf_op jit(solution)/shard_map/ppermute | solution.py:697
  5.3 3.6 %collective-permute-start = (f32[32,128]{1,0:T(8,128)S(1)}, f32[32,128]{1,0:T(8,128)S(1)}, u32[]{:S(2)}, u32[]{:S(2)}) collective-permute-start(f32[32,128]{1,0:T(8,128)S(1)} %get-tuple-element.52), channel_id=1, source_target_pairs={{0,31},{1,2},{2,1},{3,4},{4,3},{5,6},{6,5},{7,8},{8,7},{9,10},{10,... | collective-permute-start | bytes 49160 | tf_op jit(solution)/shard_map/ppermute | solution.py:707
  8.9 2.1 %own_tiles.1 = (f32[4,64,128]{2,1,0:T(8,128)S(1)}, f32[4,64,128]{2,1,0:T(8,128)S(1)}, f32[17,3,64,128]{3,2,1,0:T(8,128)S(1)}, bf16[288,144]{1,0:T(8,128)(2,1)S(1...) custom-call(s32[18]{0:T(128)S(4)} %get-tuple-element.35.facts, ...), custom_call_target="tpu_custom_call", output_to_operand_aliasing={{0}: (5, {}), {1}: (6, {}), {2}: (7, {}), {3}: (8, {}), {4}... | custom-call | tf_op jit(solution)/shard_map/own_tiles/pallas_call | solution.py:633
  11.0 0.0 collective-permute-done.1.inner
  11.0 0.4 %x_tile.1 = (f32[17,64,128]{2,1,0:T(8,128)S(1)}, f32[64,128]{1,0:T(8,128)S(1)}, f32[64,128]{1,0:T(8,128)S(1)}, f32[17,16,128]{2,1,0:T(8,128)S(1)}, f32[16,128]{1...) custom-call(s32[18]{0:T(128)S(4)} %get-tuple-element.35.facts, ...), custom_call_target="tpu_custom_call" | custom-call | tf_op jit(solution)/shard_map/x_tile/pallas_call | solution.py:633
  11.4 0.6 %collective-permute-done.outer = f32[32,128]{1,0:T(8,128)S(1)} collective-permute-done((f32[32,128]{1,0:T(8,128)S(1)}, f32[32,128]{1,0:T(8,128)S(1)}, u32[]{:S(2)}, u32[]{:S(2)}) %collective-permute-start) | collective-permute-done | bytes 16416 | tf_op jit(solution)/shard_map/ppermute | solution.py:707
  12.0 2.6 %boundaries.1 = (f32[64,512]{1,0:T(8,128)}, f32[64,512]{1,0:T(8,128)}, bf16[17,64,384]{2,1,0:T(8,128)(2,1)}) custom-call(s32[18]{0:T(128)S(4)} %get-tuple-element.35.facts, f32[17,17]{1,0:T(8,128)S(1)} %get-tuple-element.36.kin, bf16[288,144]{1,0:T(8,128)(2,1)S(1)} %get-tuple-element.51.kron, f32[32,128]{1,0:T(8,128)S(1)} %collective-permute-done.outer, ...), custom_call_target="tpu_custom_call" | custom-call | flops 1000000000 | tf_op jit(solution)/shard_map/boundaries/pallas_call | solution.py:633
  (1 shorter events, 0.0 us)
Async XLA Ops:
  5.0 6.0 %collective-permute-start.1 = (f32[160,128]{1,0:T(8,128)S(1)}, f32[160,128]{1,0:T(8,128)S(1)}, u32[]{:S(2)}, u32[]{:S(2)}) collective-permute-start(f32[160,128]{1,0:T(8,128)S(1)} %get-tuple-element.53), channel_id=1, source_target_pairs={{0,1},{1,0},{2,3},{3,2},{4,5},{5,4},{6,7},{7,6},{8,9},{9,8},{10,11... | collective-permute-start | bytes 245768 | tf_op jit(solution)/shard_map/ppermute | solution.py:697
  5.3 6.8 %collective-permute-start = (f32[32,128]{1,0:T(8,128)S(1)}, f32[32,128]{1,0:T(8,128)S(1)}, u32[]{:S(2)}, u32[]{:S(2)}) collective-permute-start(f32[32,128]{1,0:T(8,128)S(1)} %get-tuple-element.52), channel_id=1, source_target_pairs={{0,31},{1,2},{2,1},{3,4},{4,3},{5,6},{6,5},{7,8},{8,7},{9,10},{10,... | collective-permute-start | bytes 49160 | tf_op jit(solution)/shard_map/ppermute | solution.py:707

commit v6 on v5

--- a/solution.py
+++ b/solution.py
@@ -233,8 +233,12 @@
     return ref[:, pl.ds(pl.multiple_of(index * LANES, LANES), LANES)]
 
 
+def slot_as_stored(ref, j, index):
+    return ref[j, :, pl.ds(pl.multiple_of(index * LANES, LANES), LANES)]
+
+
 def slot_of(ref, j, index):
-    return ref[j, :, pl.ds(pl.multiple_of(index * LANES, LANES), LANES)].astype(F32)
+    return slot_as_stored(ref, j, index).astype(F32)
 
 
 U_AT, B_AT, T0_AT, COMBO_AT, WIDE = 40, 44, 48, 50, 3
@@ -369,7 +373,8 @@
         for p, field in ((p_u, u), (p_b, b)):
             p[...] = lay(field[f["outer_tile"]], field[f["beside_tile"]], field[f["x_tile"]])
         for j in range(n):
-            p_state[j] = lay(*[state[j, f[name]] for name in ("outer_slot", "beside_slot", "x_slot")])
+            slots = [slot_as_stored(tracers, j, f[name]) for name in ("outer_slot", "beside_slot", "x_slot")]
+            p_state[j] = lay(*slots).astype(F32)
 
     def one_step(count, first, tile, joined):
         light = []
@@ -593,7 +598,6 @@
     left, right = edge(rows, jnp.logical_not(odd)), edge(rows, odd)
     outer_fix = jnp.logical_and(left, f["outer_own_wet"] == 1)
     beside_fix = jnp.logical_and(right, f["beside_wet"] == 1)
-    third = jnp.where(gives, 1, f["x_slot"])
 
     def emit(r, values):
         if r is None:
@@ -612,17 +616,23 @@
                     whole[s, at(f["beside_tile"])] = jnp.where(right, seg1, own[f["beside_tile"], s, :])
                 send(whole, out)
             return
-        for g in range(GROUPS):
-            s = slice(rows * g, rows * (g + 1))
-            seg0, seg1, seg2 = (unfold(values, seg, g) for seg in range(3))
-            merged[:, 0, s, :] = jnp.where(outer_fix, seg0, own_t[:, f["outer_slot"], s, :]).astype(BF16)
-            merged[:, 1, s, :] = jnp.where(beside_fix, seg1, own_t[:, f["beside_slot"], s, :]).astype(BF16)
-            x = jnp.where(left, seg1, jnp.where(right, seg2, x_t[:, s, :]))
-            merged[:, 2, s, :] = jnp.where(gives, own_t[:, 1, s, :], x).astype(BF16)
+        rounded = values.astype(BF16)
+        parts = [slice(rows * g, rows * (g + 1)) for g in range(GROUPS)]
+        for g, s in enumerate(parts):
+            own = own_t[:, f["outer_slot"], s, :].astype(BF16)
+            merged[:, 0, s, :] = jnp.where(outer_fix, unfold(rounded, 0, g), own)
+        send(merged.at[:, 0], t_out.at[:, :, at(f["outer_slot"])])
+        for g, s in enumerate(parts):
+            own = own_t[:, f["beside_slot"], s, :].astype(BF16)
+            merged[:, 1, s, :] = jnp.where(beside_fix, unfold(rounded, 1, g), own)
+        send(merged.at[:, 1], t_out.at[:, :, at(f["beside_slot"])])
+        for g, s in enumerate(parts):
+            x = jnp.where(right, unfold(rounded, 2, g), x_t[:, s, :].astype(BF16))
+            x = jnp.where(left, unfold(rounded, 1, g), x)
+            merged[:, 2, s, :] = jnp.where(gives, own_t[:, 1, s, :].astype(BF16), x)
+        send(merged.at[:, 2], t_out.at[:, :, at(jnp.where(gives, 1, f["x_slot"]))])
 
     advance_alone(state, adv, u, b, heat, face_open, kron, n, rows, emit, True, GROUPS)
-    for i, slot in enumerate((f["outer_slot"], f["beside_slot"], third)):
-        send(merged.at[:, i], t_out.at[:, :, at(slot)])
     for c in copies:
         c.wait()
 
@@ -735,7 +745,7 @@
                 ocean,
                 ocean,
                 pltpu.VMEM((n, WET_DEV, *tile), BF16),
-                pltpu.SemaphoreType.DMA((2 + WET_DEV * (levels // 16),)),
+                pltpu.SemaphoreType.DMA((2 + WET_DEV,)),
             ],
             (facts, kinetic_v, kron, outer, p_state, p_combo, p_u, p_b, own_u, own_b, own_t, x_u, x_b, x_t),
             "s" + "v" * 13,

time: 14.8 us -> 14.6 us (0.986)
  starting transfers between devices: 3.93 us -> 4.8 us
  waiting for transfers between devices: 0.6 us -> 0.01 us
  Pallas kernels: 9.42 us -> 8.95 us
    ppermute x1, starting transfers between devices: 0.3 us -> 1.16 us  [on_device(): inner = lax.ppermute(inner, axes, in_pairs)]
    ppermute x1, waiting for transfers between devices: 0.6 us -> 0.01 us  [on_device(): outer = lax.ppermute(outer, axes, across)]
    pallas_call x6, Pallas kernels: 9.42 us -> 8.95 us  [call(): pl.pallas_call(kernel, out_shape=tuple((pltpu.SMEM(s, d) if c == 's' else...]
  transfers between devices with their start and end apart: 2 -> 2, of which waited for: 1 -> 0; matrix products, arithmetic and copies ran while one was open for 0% -> 0% of each run, Pallas kernels for 17% -> 22%
where the time goes in v6:
time: 14.6 us; the launch traced here: 14.4 us
  Pallas kernels  8.95 us (61%)
  starting transfers between devices  4.8 us (33%)
  between operations  0.69 us (5%)
    pallas_call x6, Pallas kernels, call(): pl.pallas_call(kernel, out_shape=tuple((pltpu.SMEM(s, d) if c == 's' else...  8.95 us
    ppermute x1, starting transfers between devices, on_device(): outer = lax.ppermute(outer, axes, across)  3.64 us
    ppermute x1, starting transfers between devices, on_device(): inner = lax.ppermute(inner, axes, in_pairs)  1.16 us
  transfers between devices with their start and end apart: 2, of which 0 were waited for; matrix products, arithmetic and copies ran while one was open for 0% of the time, Pallas kernels for 22%

profile of v6, /device:TPU:0, one launch (start us, length us, event | category | flops | bytes accessed | tf_op | source)
XLA Modules:
  0.0 14.4 jit_solution(14793866182477930275)
XLA Ops:
  0.6 1.6 %pack.1 = (f32[160,128]{1,0:T(8,128)S(1)}, f32[32,128]{1,0:T(8,128)S(1)}, f32[64,512]{1,0:T(8,128)S(1)}, f32[64,512]{1,0:T(8,128)S(1)}, bf16[17,64,384]{2,1,0:T(...) custom-call(s32[1]{0:T(128)} %bitcast.dev, s32[96]{0:T(128)} %wet_hbm.1, f32[17,17]{1,0:T(8,128)} %kin_hbm.1, ...), custom_call_target="tpu_custom_call" | custom-call | flops 10000000 | tf_op jit(solution)/shard_map/pack/pallas_call | solution.py:643
  2.2 1.9 %own_tiles_early.1 = (f32[4,64,128]{2,1,0:T(8,128)S(1)}, f32[4,64,128]{2,1,0:T(8,128)S(1)}, f32[17,3,64,128]{3,2,1,0:T(8,128)S(1)}, bf16[288,144]{1,0:T(8,128)(2...) custom-call(s32[18]{0:T(128)S(4)} %get-tuple-element.35.facts, ...), custom_call_target="tpu_custom_call" | custom-call | flops 1000000000 | tf_op jit(solution)/shard_map/own_tiles_early/pallas_call | solution.py:643
  4.1 1.2 %collective-permute-start.1 = (f32[160,128]{1,0:T(8,128)S(1)}, f32[160,128]{1,0:T(8,128)S(1)}, u32[]{:S(2)}, u32[]{:S(2)}) collective-permute-start(f32[160,128]{1,0:T(8,128)S(1)} %get-tuple-element.53), channel_id=1, source_target_pairs={{0,1},{1,0},{2,3},{3,2},{4,5},{5,4},{6,7},{7,6},{8,9},{9,8},{10,11... | collective-permute-start | bytes 245768 | tf_op jit(solution)/shard_map/ppermute | solution.py:707
  5.3 3.6 %collective-permute-start = (f32[32,128]{1,0:T(8,128)S(1)}, f32[32,128]{1,0:T(8,128)S(1)}, u32[]{:S(2)}, u32[]{:S(2)}) collective-permute-start(f32[32,128]{1,0:T(8,128)S(1)} %get-tuple-element.52), channel_id=1, source_target_pairs={{0,31},{1,2},{2,1},{3,4},{4,3},{5,6},{6,5},{7,8},{8,7},{9,10},{10,... | collective-permute-start | bytes 49160 | tf_op jit(solution)/shard_map/ppermute | solution.py:717
  8.9 1.5 %own_tiles.1 = (f32[4,64,128]{2,1,0:T(8,128)S(1)}, f32[4,64,128]{2,1,0:T(8,128)S(1)}, f32[17,3,64,128]{3,2,1,0:T(8,128)S(1)}, bf16[288,144]{1,0:T(8,128)(2,1)S(1...) custom-call(s32[18]{0:T(128)S(4)} %get-tuple-element.35.facts, ...), custom_call_target="tpu_custom_call", output_to_operand_aliasing={{0}: (5, {}), {1}: (6, {}), {2}: (7, {}), {3}: (8, {}), {4}... | custom-call | tf_op jit(solution)/shard_map/own_tiles/pallas_call | solution.py:643
  10.4 0.0 collective-permute-done.1.inner
  10.4 1.6 %x_tile.1 = (f32[17,64,128]{2,1,0:T(8,128)S(1)}, f32[64,128]{1,0:T(8,128)S(1)}, f32[64,128]{1,0:T(8,128)S(1)}, f32[17,16,128]{2,1,0:T(8,128)S(1)}, f32[16,128]{1...) custom-call(s32[18]{0:T(128)S(4)} %get-tuple-element.35.facts, ...), custom_call_target="tpu_custom_call" | custom-call | tf_op jit(solution)/shard_map/x_tile/pallas_call | solution.py:643
  12.0 0.0 collective-permute-done.outer
  12.1 2.4 %boundaries.1 = (f32[64,512]{1,0:T(8,128)}, f32[64,512]{1,0:T(8,128)}, bf16[17,64,384]{2,1,0:T(8,128)(2,1)}) custom-call(s32[18]{0:T(128)S(4)} %get-tuple-element.35.facts, f32[17,17]{1,0:T(8,128)S(1)} %get-tuple-element.36.kin, bf16[288,144]{1,0:T(8,128)(2,1)S(1)} %get-tuple-element.51.kron, f32[32,128]{1,0:T(8,128)S(1)} %collective-permute-done.outer, ...), custom_call_target="tpu_custom_call" | custom-call | flops 1000000000 | tf_op jit(solution)/shard_map/boundaries/pallas_call | solution.py:643
  (1 shorter events, 0.0 us)
Async XLA Ops:
  4.1 6.3 %collective-permute-start.1 = (f32[160,128]{1,0:T(8,128)S(1)}, f32[160,128]{1,0:T(8,128)S(1)}, u32[]{:S(2)}, u32[]{:S(2)}) collective-permute-start(f32[160,128]{1,0:T(8,128)S(1)} %get-tuple-element.53), channel_id=1, source_target_pairs={{0,1},{1,0},{2,3},{3,2},{4,5},{5,4},{6,7},{7,6},{8,9},{9,8},{10,11... | collective-permute-start | bytes 245768 | tf_op jit(solution)/shard_map/ppermute | solution.py:707
  5.3 6.8 %collective-permute-start = (f32[32,128]{1,0:T(8,128)S(1)}, f32[32,128]{1,0:T(8,128)S(1)}, u32[]{:S(2)}, u32[]{:S(2)}) collective-permute-start(f32[32,128]{1,0:T(8,128)S(1)} %get-tuple-element.52), channel_id=1, source_target_pairs={{0,31},{1,2},{2,1},{3,4},{4,3},{5,6},{6,5},{7,8},{8,7},{9,10},{10,... | collective-permute-start | bytes 49160 | tf_op jit(solution)/shard_map/ppermute | solution.py:717

commit v7 on v6

--- a/solution.py
+++ b/solution.py
@@ -148,10 +148,9 @@
         depth = depth + jnp.where(row >= step, pltpu.roll(depth, step, 0), 0.0)
         step *= 2
     if groups > 1:
-        total = jnp.broadcast_to(depth[rows - 1 :], depth.shape)
         lane = lane_of(rows)
-        for g in range(1, groups):
-            depth = depth + jnp.where(lane >= GROUP * g, lane_roll(total, GROUP * g), 0.0)
+        over = [jnp.where(lane >= GROUP * g, lane_roll(att, GROUP * g), 0.0) for g in range(1, groups)]
+        depth = depth + jnp.sum(sum(over[1:], over[0]), axis=0, keepdims=True)
     return SURFACE_LIGHT * (jnp.exp(att - depth) - jnp.exp(-depth))
 
 

time: 14.6 us -> 14.6 us (level)
  transfers between devices with their start and end apart: 2 -> 2, of which waited for: 0 -> 0; matrix products, arithmetic and copies ran while one was open for 0% -> 0% of each run, Pallas kernels for 22% -> 21%
where the time goes in v7:
time: 14.6 us; the launch traced here: 14.5 us
  Pallas kernels  8.96 us (61%)
  starting transfers between devices  4.8 us (33%)
  between operations  0.68 us (5%)
    pallas_call x6, Pallas kernels, call(): pl.pallas_call(kernel, out_shape=tuple((pltpu.SMEM(s, d) if c == 's' else...  8.96 us
    ppermute x1, starting transfers between devices, on_device(): outer = lax.ppermute(outer, axes, across)  3.63 us
    ppermute x1, starting transfers between devices, on_device(): inner = lax.ppermute(inner, axes, in_pairs)  1.16 us
  transfers between devices with their start and end apart: 2, of which 0 were waited for; matrix products, arithmetic and copies ran while one was open for 0% of the time, Pallas kernels for 21%

profile of v7, /device:TPU:0, one launch (start us, length us, event | category | flops | bytes accessed | tf_op | source)
XLA Modules:
  0.0 14.5 jit_solution(12214723810306399139)
XLA Ops:
  0.6 1.6 %pack.1 = (f32[160,128]{1,0:T(8,128)S(1)}, f32[32,128]{1,0:T(8,128)S(1)}, f32[64,512]{1,0:T(8,128)S(1)}, f32[64,512]{1,0:T(8,128)S(1)}, bf16[17,64,384]{2,1,0:T(...) custom-call(s32[1]{0:T(128)} %bitcast.dev, s32[96]{0:T(128)} %wet_hbm.1, f32[17,17]{1,0:T(8,128)} %kin_hbm.1, ...), custom_call_target="tpu_custom_call" | custom-call | flops 10000000 | tf_op jit(solution)/shard_map/pack/pallas_call | solution.py:642
  2.2 1.9 %own_tiles_early.1 = (f32[4,64,128]{2,1,0:T(8,128)S(1)}, f32[4,64,128]{2,1,0:T(8,128)S(1)}, f32[17,3,64,128]{3,2,1,0:T(8,128)S(1)}, bf16[288,144]{1,0:T(8,128)(2...) custom-call(s32[18]{0:T(128)S(4)} %get-tuple-element.35.facts, ...), custom_call_target="tpu_custom_call" | custom-call | flops 1000000000 | tf_op jit(solution)/shard_map/own_tiles_early/pallas_call | solution.py:642
  4.1 1.2 %collective-permute-start.1 = (f32[160,128]{1,0:T(8,128)S(1)}, f32[160,128]{1,0:T(8,128)S(1)}, u32[]{:S(2)}, u32[]{:S(2)}) collective-permute-start(f32[160,128]{1,0:T(8,128)S(1)} %get-tuple-element.53), channel_id=1, source_target_pairs={{0,1},{1,0},{2,3},{3,2},{4,5},{5,4},{6,7},{7,6},{8,9},{9,8},{10,11... | collective-permute-start | bytes 245768 | tf_op jit(solution)/shard_map/ppermute | solution.py:706
  5.3 3.6 %collective-permute-start = (f32[32,128]{1,0:T(8,128)S(1)}, f32[32,128]{1,0:T(8,128)S(1)}, u32[]{:S(2)}, u32[]{:S(2)}) collective-permute-start(f32[32,128]{1,0:T(8,128)S(1)} %get-tuple-element.52), channel_id=1, source_target_pairs={{0,31},{1,2},{2,1},{3,4},{4,3},{5,6},{6,5},{7,8},{8,7},{9,10},{10,... | collective-permute-start | bytes 49160 | tf_op jit(solution)/shard_map/ppermute | solution.py:716
  8.9 1.5 %own_tiles.1 = (f32[4,64,128]{2,1,0:T(8,128)S(1)}, f32[4,64,128]{2,1,0:T(8,128)S(1)}, f32[17,3,64,128]{3,2,1,0:T(8,128)S(1)}, bf16[288,144]{1,0:T(8,128)(2,1)S(1...) custom-call(s32[18]{0:T(128)S(4)} %get-tuple-element.35.facts, ...), custom_call_target="tpu_custom_call", output_to_operand_aliasing={{0}: (5, {}), {1}: (6, {}), {2}: (7, {}), {3}: (8, {}), {4}... | custom-call | tf_op jit(solution)/shard_map/own_tiles/pallas_call | solution.py:642
  10.4 0.0 collective-permute-done.1.inner
  10.4 1.7 %x_tile.1 = (f32[17,64,128]{2,1,0:T(8,128)S(1)}, f32[64,128]{1,0:T(8,128)S(1)}, f32[64,128]{1,0:T(8,128)S(1)}, f32[17,16,128]{2,1,0:T(8,128)S(1)}, f32[16,128]{1...) custom-call(s32[18]{0:T(128)S(4)} %get-tuple-element.35.facts, ...), custom_call_target="tpu_custom_call" | custom-call | tf_op jit(solution)/shard_map/x_tile/pallas_call | solution.py:642
  12.0 0.0 collective-permute-done.outer
  12.1 2.4 %boundaries.1 = (f32[64,512]{1,0:T(8,128)}, f32[64,512]{1,0:T(8,128)}, bf16[17,64,384]{2,1,0:T(8,128)(2,1)}) custom-call(s32[18]{0:T(128)S(4)} %get-tuple-element.35.facts, f32[17,17]{1,0:T(8,128)S(1)} %get-tuple-element.36.kin, bf16[288,144]{1,0:T(8,128)(2,1)S(1)} %get-tuple-element.51.kron, f32[32,128]{1,0:T(8,128)S(1)} %collective-permute-done.outer, ...), custom_call_target="tpu_custom_call" | custom-call | flops 1000000000 | tf_op jit(solution)/shard_map/boundaries/pallas_call | solution.py:642
  (1 shorter events, 0.0 us)
Async XLA Ops:
  4.1 6.3 %collective-permute-start.1 = (f32[160,128]{1,0:T(8,128)S(1)}, f32[160,128]{1,0:T(8,128)S(1)}, u32[]{:S(2)}, u32[]{:S(2)}) collective-permute-start(f32[160,128]{1,0:T(8,128)S(1)} %get-tuple-element.53), channel_id=1, source_target_pairs={{0,1},{1,0},{2,3},{3,2},{4,5},{5,4},{6,7},{7,6},{8,9},{9,8},{10,11... | collective-permute-start | bytes 245768 | tf_op jit(solution)/shard_map/ppermute | solution.py:706
  5.3 6.8 %collective-permute-start = (f32[32,128]{1,0:T(8,128)S(1)}, f32[32,128]{1,0:T(8,128)S(1)}, u32[]{:S(2)}, u32[]{:S(2)}) collective-permute-start(f32[32,128]{1,0:T(8,128)S(1)} %get-tuple-element.52), channel_id=1, source_target_pairs={{0,31},{1,2},{2,1},{3,4},{4,3},{5,6},{6,5},{7,8},{8,7},{9,10},{10,... | collective-permute-start | bytes 49160 | tf_op jit(solution)/shard_map/ppermute | solution.py:716
